TPU v7x, 32 devices: a whole 2x2x4 slice. The times are simulated.
32 devices in a mesh: groups: 2 (over x), row: 4 (over y, core), col: 4 (over z).
Axes of the slice: x: 2, y: 2, z: 4, core: 2. Of those that a mesh axis runs over, the one named last changes fastest.
Arguments:
- operand_panel: bfloat16 [4096, 8192], P(('groups', 'row'), 'col'), parts along dimension 0
- slot_blocks: bfloat16 [128, 4, 128, 128], P(('groups', 'col'), 'row'), parts along dimension 0
- slot_columns: int32 [128, 4], P(('groups', 'col')), parts along dimension 0, may hold values from 0 to 15, as said below
- live_counts: int32 [128], P(('groups', 'col')), parts along dimension 0, may hold values from 1 to 4, as said below
Outputs:
- mcl_columns: float32 [4096, 2048], P(('groups', 'row'), 'col'), parts along dimension 0
- column_load: int32 [32], P(('groups', 'col')), parts along dimension 0
There are 2 independent parts, one for each index of `groups`. A program takes and returns all parts, laid end to end along the dimension named above; each array names one. Nothing has to cross between parts.
Inputs may be any that keep to these rules, and one draw needn't show every extreme that they name: `slot_columns`: within each contraction block row the 4 slots name distinct block columns; values of slots that are not live are present but carry no block. A slot e of block row k is live exactly when ((e - k) mod 4) < live_counts[k].
All inputs are finite; a program needn't handle non-finite values.
Results may differ from a plain program's by a relative error of at most 0.0003.
Values may be sent and summed in bfloat16 or wider, within the bound.
No kernel may reach another device: no remote copies, remote signals or barrier semaphores. Data moves between devices by JAX's collectives and lax.ppermute only.
A program may use at most 128 MiB of HBM per device.

v0:
```python
import jax
import jax.numpy as jnp
from jax import lax
from jax.sharding import PartitionSpec as P

SLAB_DEV = 4


def densify(blocks, columns, counts, first_row, slab_width):
    rows_here, slots = columns.shape
    side = blocks.shape[2]
    places = jnp.arange(slots, dtype=jnp.int32)
    rows_index = first_row + jnp.arange(rows_here, dtype=jnp.int32)
    live = jnp.mod(places[None, :] - rows_index[:, None], slots) < counts[:, None]
    onehot = (columns[:, :, None] == jnp.arange(slab_width, dtype=jnp.int32)[None, None, :]) & live[
        :, :, None
    ]
    dense = jnp.einsum(
        "kej,kebc->kbjc", onehot.astype(jnp.bfloat16), blocks, preferred_element_type=jnp.float32
    )
    dense = dense.astype(jnp.bfloat16).reshape(rows_here * side, slab_width * side)
    return (dense, jnp.sum(onehot.astype(jnp.float32), axis=(0, 1)))


def body(operand_panel, slot_blocks, slot_columns, live_counts):
    gathered = lax.all_gather(slot_blocks, "row", axis=1, tiled=True)
    slab_width = SLAB_DEV * lax.axis_size("col")
    first_row = lax.axis_index("col") * slot_columns.shape[0]
    dense, load = densify(gathered, slot_columns, live_counts, first_row, slab_width)
    partial_terms = jnp.dot(operand_panel, dense, preferred_element_type=jnp.float32)
    expanded, load_mine = (
        lax.psum_scatter(partial_terms, "col", scatter_dimension=1, tiled=True),
        lax.psum_scatter(load, "col", scatter_dimension=0, tiled=True),
    )
    inflated = expanded * expanded
    totals = lax.psum(jnp.sum(inflated, axis=0), "row")
    all_rows = expanded.shape[0] * lax.axis_size("row")
    mcl_columns = inflated / (totals / all_rows + 1e-06)
    return (mcl_columns, load_mine.astype(jnp.int32))


def solution(mesh):
    placed = (
        P(("groups", "row"), "col"),
        P(("groups", "col"), "row", None, None),
        P(("groups", "col"), None),
        P(("groups", "col")),
    )
    return jax.shard_map(
        body,
        mesh=mesh,
        in_specs=placed,
        out_specs=(P(("groups", "row"), "col"), P(("groups", "col"))),
        check_vma=False,
    )
```

profile of v0, /device:TPU:0, one launch (start us, length us, event | category | flops | bytes accessed | tf_op | source)
XLA Modules:
  0.0 142.4 jit_solution(1521452157146558230)
XLA Ops:
  7.2 0.0 copy-start
  7.2 0.0 all-gather.2.cloned.1.call-start
  7.2 0.7 all-gather.2.cloned.1.call-update
  7.9 0.0 reduce-scatter.2.cloned.1.call-start
  8.0 0.8 copy.9
  8.7 0.7 fusion.13
  9.5 25.4 %all-gather.2.cloned.1.call-done = bf16[16,4,128,128]{3,2,0,1:T(8,128)(2,1)} async-done(((bf16[16,1,128,128]{3,2,0,1:T(8,128)(2,1)}), bf16[16,4,128,128]{3,2,0,1:T(8,128)(2,1)}) %all-gather.2.cloned.1.call-update) | async-done | bytes 2097168 | tf_op jit(solution)/shard_map/all_gather | solution.py:26
  34.9 5.6 %convolution_convert_fusion = bf16[16,16,128,128]{3,1,2,0:T(8,128)(2,1)S(1)} fusion(bf16[16,4,128,128]{3,2,0,1:T(8,128)(2,1)} %all-gather.2.cloned.1.call-done, s32[16,4]{1,0:T(8,128)S(1)} %copy.9, pred[16,4]{1,0:T(8,128)(4,1)S(1)} %fusion.13), kind=kOutput, calls=%fused_computation.3 | convolution fusion | flops 37750784 | bytes 10486080 | tf_op jit(solution)/shard_map/kej,kebc->kbjc/dot_general | solution.py:18
  40.5 0.0 copy-done
  40.5 7.2 %fusion.3 = f32[512,2048]{0,1:T(8,128)} fusion(bf16[512,2048]{1,0:T(8,128)(2,1)S(1)} %copy-done, bf16[256,8,16,128]{3,2,1,0:T(8,128)(2,1)S(1)} %bitcast.18), kind=kOutput, calls=%fused_computation.4 | convolution fusion | flops 4294967296 | bytes 14680064 | tf_op jit(solution)/shard_map/dot_general | solution.py:30
  47.7 0.0 copy-start.1
  47.7 0.0 reduce-scatter.2.cloned.1.call-update
  47.7 0.6 copy-done.1
  48.3 0.6 dynamic-slice
  49.6 0.1 convert_reduce_fusion
  49.7 11.9 %all-reduce = f32[16]{0:T(128)S(1)} all-reduce(f32[16]{0:T(128)S(1)} %convert_reduce_fusion), channel_id=3, replica_groups=mesh['groups'=2,'row'=4,'col'=4] {'col'}, use_global_device_ids=true, to_apply=%region_4.5.clone | all-reduce | flops 16 | bytes 128
  61.6 0.6 dynamic-slice_convert_fusion
  62.2 62.6 %reduce-scatter.2.cloned.1.call-done = f32[512,512]{0,1:T(8,128)} async-done(((f32[512,2048]{0,1:T(8,128)}), f32[512,512]{0,1:T(8,128)}) %reduce-scatter.2.cloned.1.call-update) | async-done | bytes 1048592 | tf_op jit(solution)/shard_map/reduce_scatter | solution.py:32
  124.7 1.4 multiply_reduce_fusion
  126.1 6.8 %psum.7 = f32[512]{0:T(512)S(1)} all-reduce(f32[512]{0:T(512)S(1)} %multiply_reduce_fusion), channel_id=1, replica_groups=mesh['groups'=2,'row'=4,'col'=4] {'row'}, use_global_device_ids=true, to_apply=%region_2.3 | all-reduce | flops 512 | bytes 4096 | tf_op jit(solution)/shard_map/psum | solution.py:36
  132.9 1.4 multiply_divide_fusion
  134.3 1.3 copy.12
  (2 shorter events, 0.0 us)
Async XLA Ops:
  7.2 33.3 %copy-start = (bf16[512,2048]{1,0:T(8,128)(2,1)S(1)}, bf16[512,2048]{1,0:T(8,128)(2,1)}, u32[]{:S(2)}) copy-start(bf16[512,2048]{1,0:T(8,128)(2,1)} %param.4) | copy-start | bytes 6291460
  7.2 27.7 %all-gather.2.cloned.1.call-start = ((), (), s32[]{:S(2)}) async-start(), calls=%async_computation.1 | async-start | bytes 2621440 | tf_op jit(solution)/shard_map/all_gather | solution.py:26
  7.9 116.8 %reduce-scatter.2.cloned.1.call-start = ((), (), s32[]{:S(2)}) async-start(), calls=%async_computation.2 | async-start | bytes 5242880 | tf_op jit(solution)/shard_map/reduce_scatter | solution.py:32
  47.7 0.7 copy-start.1
Sparse Core Ops, SparseCore 0:
  9.6 25.2 all-gather.1
  47.8 76.8 reduce-scatter.1
where the time goes:
time: 143 us; the launch traced here: 142 us
  waiting for transfers between devices  88.7 us (62%)
  blocking collectives  18.7 us (13%)
  between operations  14.7 us (10%)
  matrix products  12.7 us (9%)
  other arithmetic  4.19 us (3%)
  local copies, waits for them, and re-layouts  3.28 us (2%)
    reduce_scatter x1, waiting for transfers between devices, body(): lax.psum_scatter(partial_terms, 'col', scatter_dimension=1, tiled=True)  62.6 us
    all_gather x1, waiting for transfers between devices, body(): gathered = lax.all_gather(slot_blocks, 'row', axis=1, tiled=True)  25.4 us
    unnamed x1, blocking collectives  11.9 us
    dot_general x1, matrix products, body(): jnp.dot(operand_panel, dense, preferred_element_type=jnp.float32)  7.17 us
    psum x1, blocking collectives, body(): totals = lax.psum(jnp.sum(inflated, axis=0), 'row')  6.8 us
    dot_general x1, matrix products, densify(): jnp.einsum('kej,kebc->kbjc', onehot.astype(jnp.bfloat16), blocks, preferr...  5.58 us
    unnamed x7, local copies, waits for them, and re-layouts  3.28 us
  transfers between devices with their start and end apart: 2, of which 2 were waited for; matrix products, arithmetic and copies ran while one was open for 2% of the time, Pallas kernels for 0%

commit v1 on v0

--- a/solution.py
+++ b/solution.py
@@ -1,9 +1,296 @@
+import functools
+
 import jax
 import jax.numpy as jnp
 from jax import lax
+from jax.experimental import pallas as pl
+from jax.experimental.pallas import tpu as pltpu
 from jax.sharding import PartitionSpec as P
 
 SLAB_DEV = 4
+SIDE = 128
+HEAD = 16
+TILE = 256
+STEPS = 32752.0
+OCTAVE = 128.0
+
+VMEM = pl.BlockSpec(memory_space=pltpu.VMEM)
+SMEM = pl.BlockSpec(memory_space=pltpu.SMEM)
+
+
+def code_scale(values):
+    most = jnp.max(jnp.abs(values), axis=0, keepdims=True)
+    octaves = jnp.log2(jnp.maximum(most, 1e-30))
+    return jnp.ceil(octaves * OCTAVE)
+
+
+def encode(values, code):
+    scaled = jnp.round(values * (STEPS * jnp.exp2(code * (-1.0 / OCTAVE))))
+    return jnp.clip(scaled, -32767.0, 32767.0).astype(jnp.int32).astype(jnp.int16)
+
+
+def head_rows(code, counts):
+    shape = (HEAD, code.shape[1])
+    row = lax.broadcasted_iota(jnp.int32, shape, 0)
+    code = jnp.broadcast_to(code.astype(jnp.int32), shape)
+    counts = jnp.broadcast_to(counts, shape)
+    return jnp.where(row == 0, code, jnp.where(row == 1, counts, 0)).astype(jnp.int16)
+
+
+def put_coded(out, lanes, values, counts):
+    code = code_scale(values)
+    out[pl.ds(0, HEAD), lanes] = head_rows(code, counts)
+    out[pl.ds(HEAD, values.shape[0]), lanes] = encode(values, code)
+
+
+def decode(ref, lanes):
+    rows = ref.shape[0] - HEAD
+    head = ref[pl.ds(0, HEAD), lanes].astype(jnp.int32).astype(jnp.float32)
+    scale = jnp.exp2(head[0:1] * (1.0 / OCTAVE)) * (1.0 / STEPS)
+    return ref[pl.ds(HEAD, rows), lanes].astype(jnp.int32).astype(jnp.float32) * scale
+
+
+def head_counts(ref, lanes):
+    return ref[pl.ds(0, HEAD), lanes].astype(jnp.int32)[1:2]
+
+
+def slot_of(place, ny):
+    me = lax.axis_index("row")
+    y, core = lax.div(me, 2), lax.rem(me, 2)
+    return lax.rem(y + ny - place // 2, ny) * 2 + (core if place % 2 == 0 else 1 - core)
+
+
+def is_live(columns, counts, k, e):
+    rows, slots = columns.shape
+    row_index = lax.axis_index("col") * rows + k
+    all_rows = rows * lax.axis_size("col")
+    return lax.rem(e - row_index + all_rows * slots, slots) < counts[k]
+
+
+def fill(slab, shard, columns, counts, blocks):
+    rows, _ = columns.shape
+    slab[...] = jnp.zeros_like(slab)
+    for place, held in enumerate(blocks):
+        e = slot_of(place, len(blocks) // 2)
+
+        def one(k, carry, held=held, e=e):
+            column = columns[k, e] - shard * SLAB_DEV
+
+            @pl.when(is_live(columns, counts, k, e) & (column >= 0) & (column < SLAB_DEV))
+            def _():
+                at = (pl.ds(pl.multiple_of(k * SIDE, SIDE), SIDE), pl.ds(pl.multiple_of(column * SIDE, SIDE), SIDE))
+                slab[at] = held[k, 0]
+
+            return carry
+
+        lax.fori_loop(0, rows, one, 0, unroll=False)
+
+
+def count_live(load, columns, counts):
+    rows, slots = columns.shape
+
+    def clear(j, carry):
+        load[j] = 0
+        return carry
+
+    lax.fori_loop(0, load.shape[0], clear, 0)
+
+    def one(k, carry):
+        for e in range(slots):
+            j = columns[k, e]
+            load[j] = load[j] + is_live(columns, counts, k, e).astype(jnp.int32)
+        return carry
+
+    lax.fori_loop(0, rows, one, 0)
+
+
+def counts_of(load, shard, tile):
+    lane = lax.broadcasted_iota(jnp.int32, (1, TILE), 1)
+    counts = jnp.zeros((1, TILE), jnp.int32)
+    for j in range(TILE // SIDE):
+        block = shard * SLAB_DEV + tile * (TILE // SIDE) + j
+        counts = jnp.where((lane >= j * SIDE) & (lane < (j + 1) * SIDE), load[block], counts)
+    return counts
+
+
+def tiles(width, body):
+    def step(tile, carry):
+        body(tile, pl.ds(pl.multiple_of(tile * TILE, TILE), TILE))
+        return carry
+
+    lax.fori_loop(0, width // TILE, step, 0)
+
+
+def coded_product(which, nblocks, *refs):
+    columns, counts, operand, *blocks = refs[: 3 + nblocks]
+    out, slab, load = refs[3 + nblocks :]
+    shard = which(lax.axis_index("col"))
+    count_live(load, columns, counts)
+    fill(slab, shard, columns, counts, blocks)
+
+    def body(tile, lanes):
+        values = jnp.dot(operand[...], slab[:, lanes], preferred_element_type=jnp.float32)
+        put_coded(out, lanes, values, counts_of(load, shard, tile))
+
+    tiles(slab.shape[1], body)
+
+
+def plain_products(which, nblocks, *refs):
+    columns, counts, operand, *blocks = refs[: 3 + nblocks]
+    outs = refs[3 + nblocks : 3 + nblocks + len(which)]
+    loads = refs[3 + nblocks + len(which) : 3 + nblocks + 2 * len(which)]
+    slab, load = refs[3 + nblocks + 2 * len(which) :]
+    count_live(load, columns, counts)
+    for one, out, row in zip(which, outs, loads):
+        shard = one(lax.axis_index("col"))
+        fill(slab, shard, columns, counts, blocks)
+
+        def body(tile, lanes, out=out, row=row, shard=shard):
+            out[:, lanes] = jnp.dot(operand[...], slab[:, lanes], preferred_element_type=jnp.float32)
+            row[:, lanes] = jnp.broadcast_to(counts_of(load, shard, tile), (8, TILE))
+
+        tiles(slab.shape[1], body)
+
+
+def relay(own, own_load, came, out):
+    place = lax.axis_index("col")
+    inner = (place == 1) | (place == 2)
+
+    def body(tile, lanes):
+        @pl.when(inner)
+        def _():
+            put_coded(out, lanes, own[:, lanes] + decode(came, lanes), own_load[0:1, lanes] + head_counts(came, lanes))
+
+        @pl.when(jnp.logical_not(inner))
+        def _():
+            put_coded(out, lanes, own[:, lanes], own_load[0:1, lanes])
+
+    tiles(own.shape[1], body)
+
+
+def settle(own, own_load, came_a, came_b, came_f, out, out_load):
+    place = lax.axis_index("col")
+    inner = (place == 1) | (place == 2)
+
+    def body(tile, lanes):
+        @pl.when(inner)
+        def _():
+            out[:, lanes] = own[:, lanes] + decode(came_b, lanes) + decode(came_f, lanes)
+            load = own_load[0:1, lanes] + head_counts(came_b, lanes) + head_counts(came_f, lanes)
+            out_load[:, lanes] = jnp.broadcast_to(load, (8, TILE))
+
+        @pl.when(jnp.logical_not(inner))
+        def _():
+            out[:, lanes] = own[:, lanes] + decode(came_a, lanes)
+            out_load[:, lanes] = jnp.broadcast_to(own_load[0:1, lanes] + head_counts(came_a, lanes), (8, TILE))
+
+    tiles(own.shape[1], body)
+
+
+def inflate(own, own_load, came, out, totals, load):
+    def body(tile, lanes):
+        expanded = own[:, lanes] + decode(came, lanes)
+        inflated = expanded * expanded
+        out[:, lanes] = inflated
+        totals[:, lanes] = jnp.sum(inflated.reshape(-1, 8, TILE), axis=0)
+
+    tiles(own.shape[1], body)
+    for j in range(SLAB_DEV):
+        lanes = pl.ds(j * SIDE, SIDE)
+        load[j] = jnp.max(own_load[0:1, lanes] + head_counts(came, lanes))
+
+
+def scale(all_rows, inflated, *refs):
+    *totals, out = refs
+
+    def body(tile, lanes):
+        total = totals[0][:, lanes]
+        for other in totals[1:]:
+            total = total + other[:, lanes]
+        total = jnp.sum(total, axis=0, keepdims=True)
+        out[:, lanes] = inflated[:, lanes] * (1.0 / (total / all_rows + 1e-06))
+
+    tiles(inflated.shape[1], body)
+
+
+def call(kernel, ins, out_shape, out_specs, scratch=(), flops=0):
+    moved = sum(x.size * x.dtype.itemsize for x in list(ins) + list(out_shape))
+    return pl.pallas_call(
+        kernel,
+        in_specs=[SMEM if x.dtype == jnp.int32 and x.ndim < 3 and x.size <= 4096 and x.shape[-1] <= 32 else VMEM for x in ins],
+        out_shape=out_shape,
+        out_specs=out_specs,
+        scratch_shapes=list(scratch),
+        compiler_params=pltpu.CompilerParams(vmem_limit_bytes=40 << 20),
+        cost_estimate=pl.CostEstimate(flops=flops, bytes_accessed=moved, transcendentals=0),
+    )(*ins)
+
+
+def body_line(operand_panel, slot_blocks, slot_columns, live_counts):
+    ny = lax.axis_size("row") // 2
+    rows, depth = operand_panel.shape
+    width = SLAB_DEV * SIDE
+    slab_width = SLAB_DEV * lax.axis_size("col")
+    f32 = functools.partial(jax.ShapeDtypeStruct, dtype=jnp.float32)
+    i32 = functools.partial(jax.ShapeDtypeStruct, dtype=jnp.int32)
+    coded = jax.ShapeDtypeStruct((HEAD + rows, width), jnp.int16)
+
+    swap = [(a, a ^ 1) for a in range(2 * ny)]
+
+    def turn(by):
+        return [(a, ((a // 2 + by) % ny) * 2 + a % 2) for a in range(2 * ny)]
+
+    held = [slot_blocks] + [lax.ppermute(slot_blocks, "row", turn(by)) for by in range(1, ny)]
+    blocks = [x for mine in held for x in (mine, lax.ppermute(mine, "row", swap))]
+
+    ins = [slot_columns, live_counts, operand_panel, *blocks]
+    scratch = [pltpu.VMEM((depth, width), jnp.bfloat16), pltpu.SMEM((slab_width,), jnp.int32)]
+    flops = 2 * rows * depth * width
+
+    def first(z):
+        return jnp.where(lax.rem(z, 2) == 0, 3, 0)
+
+    def second(z):
+        return jnp.where(z < 2, 2, 1)
+
+    def third(z):
+        return jnp.where(z == 0, 1, jnp.where(z == 1, 3, jnp.where(z == 2, 0, 2)))
+
+    def product(which):
+        return call(functools.partial(coded_product, which, len(blocks)), ins, [coded], [VMEM], scratch, flops)[0]
+
+    send_a = product(first)
+    came_a = lax.ppermute(send_a, "col", [(0, 1), (1, 0), (2, 3), (3, 2)])
+    send_b = product(second)
+    came_b = lax.ppermute(send_b, "col", [(1, 2), (2, 1)])
+    came_f = lax.ppermute(send_b, "col", [(0, 2), (3, 1)])
+    passed, own, passed_load, own_load = call(
+        functools.partial(plain_products, (third, lambda z: z), len(blocks)),
+        ins,
+        [f32((rows, width)), f32((rows, width)), i32((8, width)), i32((8, width))],
+        [VMEM] * 4,
+        scratch,
+        2 * flops,
+    )
+    [send_t] = call(relay, [passed, passed_load, came_a], [coded], [VMEM])
+    came_t = lax.ppermute(send_t, "col", [(0, 1), (1, 3), (3, 2), (2, 0)])
+    own, own_load = call(
+        settle, [own, own_load, came_a, came_b, came_f], [f32((rows, width)), i32((8, width))], [VMEM] * 2
+    )
+    inflated, totals, load = call(
+        inflate, [own, own_load, came_t], [f32((rows, width)), f32((8, width)), i32((SLAB_DEV,))], [VMEM, VMEM, SMEM]
+    )
+    others = [totals]
+    for by in range(ny):
+        for flip in (0, 1):
+            if by or flip:
+                pairs = [(a, ((a // 2 + by) % ny) * 2 + (a % 2 ^ flip)) for a in range(2 * ny)]
+                others.append(lax.ppermute(totals, "row", pairs))
+    all_rows = rows * lax.axis_size("row")
+    [mcl_columns] = call(
+        functools.partial(scale, all_rows), [inflated, *others], [f32((rows, width))], [VMEM]
+    )
+    return mcl_columns, load
 
 
 def densify(blocks, columns, counts, first_row, slab_width):
@@ -12,9 +299,7 @@
     places = jnp.arange(slots, dtype=jnp.int32)
     rows_index = first_row + jnp.arange(rows_here, dtype=jnp.int32)
     live = jnp.mod(places[None, :] - rows_index[:, None], slots) < counts[:, None]
-    onehot = (columns[:, :, None] == jnp.arange(slab_width, dtype=jnp.int32)[None, None, :]) & live[
-        :, :, None
-    ]
+    onehot = (columns[:, :, None] == jnp.arange(slab_width, dtype=jnp.int32)[None, None, :]) & live[:, :, None]
     dense = jnp.einsum(
         "kej,kebc->kbjc", onehot.astype(jnp.bfloat16), blocks, preferred_element_type=jnp.float32
     )
@@ -22,7 +307,7 @@
     return (dense, jnp.sum(onehot.astype(jnp.float32), axis=(0, 1)))
 
 
-def body(operand_panel, slot_blocks, slot_columns, live_counts):
+def body_any(operand_panel, slot_blocks, slot_columns, live_counts):
     gathered = lax.all_gather(slot_blocks, "row", axis=1, tiled=True)
     slab_width = SLAB_DEV * lax.axis_size("col")
     first_row = lax.axis_index("col") * slot_columns.shape[0]
@@ -47,7 +332,7 @@
         P(("groups", "col")),
     )
     return jax.shard_map(
-        body,
+        body_line if mesh.shape["col"] == 4 else body_any,
         mesh=mesh,
         in_specs=placed,
         out_specs=(P(("groups", "row"), "col"), P(("groups", "col"))),

time: 143 us -> 79.1 us (0.55)
  waiting for transfers between devices: 88.7 us -> 43.1 us
  blocking collectives: 18.7 us -> 0 us
  Pallas kernels: 0 us -> 17.6 us
  between operations: 14.7 us -> 0.71 us
  starting transfers between devices: 0.08 us -> 13.3 us
  matrix products: 12.7 us -> 0 us
  other arithmetic: 4.19 us -> 0 us
    reduce_scatter x1 -> x0, waiting for transfers between devices: 62.6 us -> none  [body(): lax.psum_scatter(partial_terms, 'col', scatter_dimension=1, tiled=True)]
    ppermute x0 -> x10, waiting for transfers between devices: none -> 43.1 us  [the longest x1 21 us: body_line(): came_t = lax.ppermute(send_t, 'col', [(0, 1), (1, 3), (3, 2), (2, 0)])]
    all_gather x1 -> x0, waiting for transfers between devices: 25.4 us -> none  [body(): gathered = lax.all_gather(slot_blocks, 'row', axis=1, tiled=True)]
    pallas_call x0 -> x7, Pallas kernels: none -> 17.6 us  [call(): pl.pallas_call(kernel, in_specs=[SMEM if x.dtype == jnp.int32 and x.ndim...]
    ppermute x0 -> x10, starting transfers between devices: none -> 13.3 us  [the longest x1 4.54 us: body_line(): came_f = lax.ppermute(send_b, 'col', [(0, 2), (3, 1)])]
    dot_general x2 -> x0, matrix products: 12.7 us -> none  [the longest x1 7.17 us: body(): jnp.dot(operand_panel, dense, preferred_element_type=jnp.float32)]
    unnamed x1 -> x0, blocking collectives: 11.9 us -> none
    psum x1 -> x0, blocking collectives: 6.8 us -> none  [body(): totals = lax.psum(jnp.sum(inflated, axis=0), 'row')]
  transfers between devices with their start and end apart: 2 -> 10, of which waited for: 2 -> 6; matrix products, arithmetic and copies ran while one was open for 2% -> 1% of each run, Pallas kernels for 0% -> 14%
where the time goes in v1:
time: 79.1 us; the launch traced here: 78.8 us
  waiting for transfers between devices  43.1 us (54%)
  Pallas kernels  17.6 us (22%)
  starting transfers between devices  13.3 us (17%)
  local copies, waits for them, and re-layouts  4.05 us (5%)
    ppermute x1, waiting for transfers between devices, body_line(): came_t = lax.ppermute(send_t, 'col', [(0, 1), (1, 3), (3, 2), (2, 0)])  21 us
    pallas_call x7, Pallas kernels, call(): pl.pallas_call(kernel, in_specs=[SMEM if x.dtype == jnp.int32 and x.ndim...  17.6 us
    ppermute x1, waiting for transfers between devices, body_line(): lax.ppermute(slot_blocks, 'row', turn(by))  12.1 us
    ppermute x1, waiting for transfers between devices, body_line(): came_f = lax.ppermute(send_b, 'col', [(0, 2), (3, 1)])  6.52 us
    ppermute x1, starting transfers between devices, body_line(): came_f = lax.ppermute(send_b, 'col', [(0, 2), (3, 1)])  4.54 us
    unnamed x7, local copies, waits for them, and re-layouts  4.05 us
    ppermute x1, starting transfers between devices, body_line(): lax.ppermute(slot_blocks, 'row', turn(by))  3.03 us
    ppermute x3, waiting for transfers between devices, body_line(): others.append(lax.ppermute(totals, 'row', pairs))  2.31 us
  transfers between devices with their start and end apart: 10, of which 6 were waited for; matrix products, arithmetic and copies ran while one was open for 1% of the time, Pallas kernels for 14%

profile of v1, /device:TPU:0, one launch (start us, length us, event | category | flops | bytes accessed | tf_op | source)
XLA Modules:
  0.0 78.8 jit_solution(13461709943493555275)
XLA Ops:
  0.6 3.0 %collective-permute-start.1 = (bf16[16,1,128,128]{3,2,1,0:T(8,128)(2,1)}, bf16[16,1,128,128]{3,2,1,0:T(8,128)(2,1)S(1)}, u32[]{:S(2)}, u32[]{:S(2)}) collective-permute-start(bf16[16,1,128,128]{3,2,1,0:T(8,128)(2,1)} %refs_3_.5), channel_id=1, source_target_pairs={{0,8},{4,12},{8,0},{12,4},{1,9},{5,13},{9,1},{13,5},{2,10},{6,14},... | collective-permute-start | bytes 1572872 | tf_op jit(solution)/shard_map/ppermute | solution.py:243
  3.7 0.0 collective-permute-start
  3.7 12.1 %collective-permute-done.1.refs_5_ = bf16[16,1,128,128]{3,2,1,0:T(8,128)(2,1)S(1)} collective-permute-done((bf16[16,1,128,128]{3,2,1,0:T(8,128)(2,1)}, bf16[16,1,128,128]{3,2,1,0:T(8,128)(2,1)S(1)}, u32[]{:S(2)}, u32[]{:S(2)}) %collective-permute-start.1) | collective-permute-done | bytes 524320 | tf_op jit(solution)/shard_map/ppermute | solution.py:243
  15.8 0.0 collective-permute-start.2
  15.8 0.8 copy.6.refs_0_
  16.6 0.0 collective-permute-done.refs_4_
  16.6 1.1 %collective-permute-done.2.refs_6_ = bf16[16,1,128,128]{3,2,1,0:T(8,128)(2,1)S(1)} collective-permute-done((bf16[16,1,128,128]{3,2,1,0:T(8,128)(2,1)S(1)}, bf16[16,1,128,128]{3,2,1,0:T(8,128)(2,1)S(1)}, u32[]{:S(2)}, u32[]{:S(2)}) %collective-permute-start.2) | collective-permute-done | bytes 524320 | tf_op jit(solution)/shard_map/ppermute | solution.py:244
  17.7 0.0 copy-start
  17.7 1.6 %copy-done = bf16[512,2048]{1,0:T(8,128)(2,1)S(1)} copy-done((bf16[512,2048]{1,0:T(8,128)(2,1)S(1)}, bf16[512,2048]{1,0:T(8,128)(2,1)}, u32[]{:S(2)}) %copy-start) | copy-done | bytes 2097176
  19.3 0.0 copy-start.1
  19.3 1.0 %copy-done.1 = bf16[16,1,128,128]{3,2,1,0:T(8,128)(2,1)S(1)} copy-done((bf16[16,1,128,128]{3,2,1,0:T(8,128)(2,1)S(1)}, bf16[16,1,128,128]{3,2,1,0:T(8,128)(2,1)}, u32[]{:S(2)}) %copy-start.1) | copy-done | bytes 524312
  20.3 0.0 copy-start.2
  20.3 0.7 copy-done.2
  21.0 4.2 %shard_map.60 = s16[528,512]{1,0:T(8,128)(2,1)S(1)} custom-call(s32[16,4]{1,0:T(8,128)S(1)} %copy.6.refs_0_, s32[16]{0:T(128)S(1)} %copy-done.2, bf16[512,2048]{1,0:T(8,128)(2,1)S(1)} %copy-done, bf16[16,1,128,128]{3,2,1,0:T(8,128)(2,1)S(1)} %copy-done.1, bf16[16,1,128,128]{3,2,1,0:T(8,128)(2,1)S(1)} %collective-permute-done.refs_4_, ...), custom_call_target="tpu_custom_call" | custom-call | flops 1073741824 | bytes 4735296 | tf_op jit(solution)/shard_map/pallas_call | solution.py:218
  25.2 1.9 %collective-permute-start.3 = (s16[528,512]{1,0:T(8,128)(2,1)S(1)}, s16[528,512]{1,0:T(8,128)(2,1)S(1)}, u32[]{:S(2)}, u32[]{:S(2)}) collective-permute-start(s16[528,512]{1,0:T(8,128)(2,1)S(1)} %shard_map.60), channel_id=1, source_target_pairs={{0,1},{1,0},{2,3},{3,2},{4,5},{5,4},{6,7},{7,6},{8,9},{9,8},{10,11... | collective-permute-start | bytes 1622024 | tf_op jit(solution)/shard_map/ppermute | solution.py:263
  27.1 4.2 %shard_map.61 = s16[528,512]{1,0:T(8,128)(2,1)S(1)} custom-call(s32[16,4]{1,0:T(8,128)S(1)} %copy.6.refs_0_, s32[16]{0:T(128)S(1)} %copy-done.2, bf16[512,2048]{1,0:T(8,128)(2,1)S(1)} %copy-done, bf16[16,1,128,128]{3,2,1,0:T(8,128)(2,1)S(1)} %copy-done.1, bf16[16,1,128,128]{3,2,1,0:T(8,128)(2,1)S(1)} %collective-permute-done.refs_4_, ...), custom_call_target="tpu_custom_call" | custom-call | flops 1073741824 | bytes 4735296 | tf_op jit(solution)/shard_map/pallas_call | solution.py:218
  31.3 4.5 %collective-permute-start.5 = (s16[528,512]{1,0:T(8,128)(2,1)S(1)}, s16[528,512]{1,0:T(8,128)(2,1)S(1)}, u32[]{:S(2)}, u32[]{:S(2)}) collective-permute-start(s16[528,512]{1,0:T(8,128)(2,1)S(1)} %shard_map.61), channel_id=1, source_target_pairs={{0,2},{3,1},{4,6},{7,5},{8,10},{11,9},{12,14},{15,13},{16,18},{19,... | collective-permute-start | bytes 1622024 | tf_op jit(solution)/shard_map/ppermute | solution.py:266
  35.8 0.7 collective-permute-start.4
  36.5 6.7 %shard_map.59 = (f32[512,512]{1,0:T(8,128)S(1)}, f32[512,512]{1,0:T(8,128)S(1)}, s32[8,512]{1,0:T(8,128)S(1)}, s32[8,512]{1,0:T(8,128)S(1)}) custom-call(s32[16,4]{1,0:T(8,128)S(1)} %copy.6.refs_0_, s32[16]{0:T(128)S(1)} %copy-done.2, bf16[512,2048]{1,0:T(8,128)(2,1)S(1)} %copy-done, bf16[16,1,128,128]{3,2,1,0:T(8,128)(2,1)S(1)} %copy-done.1, ...), custom_call_target="tpu_custom_call" | custom-call | flops 2147483648 | bytes 6324544 | tf_op jit(solution)/shard_map/pallas_call | solution.py:218
  43.2 0.0 collective-permute-done.3.came_a.came
  43.2 0.3 shard_map.63
  43.6 1.3 %collective-permute-start.6 = (s16[528,512]{1,0:T(8,128)(2,1)S(1)}, s16[528,512]{1,0:T(8,128)(2,1)S(1)}, u32[]{:S(2)}, u32[]{:S(2)}) collective-permute-start(s16[528,512]{1,0:T(8,128)(2,1)S(1)} %shard_map.63), channel_id=1, source_target_pairs={{0,1},{1,3},{3,2},{2,0},{4,5},{5,7},{7,6},{6,4},{8,9},{9,11},{11,1... | collective-permute-start | bytes 1622024 | tf_op jit(solution)/shard_map/ppermute | solution.py:276
  44.8 6.5 %collective-permute-done.5.came_f = s16[528,512]{1,0:T(8,128)(2,1)S(1)} collective-permute-done((s16[528,512]{1,0:T(8,128)(2,1)S(1)}, s16[528,512]{1,0:T(8,128)(2,1)S(1)}, u32[]{:S(2)}, u32[]{:S(2)}) %collective-permute-start.5) | collective-permute-done | bytes 540704 | tf_op jit(solution)/shard_map/ppermute | solution.py:266
  51.4 0.0 collective-permute-done.4.came_b
  51.4 0.2 shard_map.62
  51.5 21.0 %collective-permute-done.6.came = s16[528,512]{1,0:T(8,128)(2,1)S(1)} collective-permute-done((s16[528,512]{1,0:T(8,128)(2,1)S(1)}, s16[528,512]{1,0:T(8,128)(2,1)S(1)}, u32[]{:S(2)}, u32[]{:S(2)}) %collective-permute-start.6) | collective-permute-done | bytes 540704 | tf_op jit(solution)/shard_map/ppermute | solution.py:276
  72.5 0.9 %shard_map.64 = (f32[512,512]{1,0:T(8,128)S(1)}, f32[8,512]{1,0:T(8,128)S(1)}, s32[4]{0:T(128)}) custom-call(f32[512,512]{1,0:T(8,128)S(1)} %get-tuple-element.13.own, s32[8,512]{1,0:T(8,128)S(1)} %get-tuple-element.14.own_load, s16[528,512]{1,0:T(8,128)(2,1)S(1)} %collective-permute-done.6.came), custom_call_target="tpu_custom_call" | custom-call | bytes 2670608 | tf_op jit(solution)/shard_map/pallas_call | solution.py:218
  73.5 0.5 collective-permute-start.9
  74.0 1.2 %collective-permute-start.8 = (f32[8,512]{1,0:T(8,128)S(1)}, f32[8,512]{1,0:T(8,128)S(1)}, u32[]{:S(2)}, u32[]{:S(2)}) collective-permute-start(f32[8,512]{1,0:T(8,128)S(1)} %get-tuple-element.18.refs_0_), channel_id=1, source_target_pairs={{0,8},{4,12},{8,0},{12,4},{1,9},{5,13},{9,1},{13,5},{2,10},{6,14},... | collective-permute-start | bytes 49160 | tf_op jit(solution)/shard_map/ppermute | solution.py:288
  75.2 0.3 collective-permute-start.7
  75.4 1.4 %collective-permute-done.9.refs_3_ = f32[8,512]{1,0:T(8,128)S(1)} collective-permute-done((f32[8,512]{1,0:T(8,128)S(1)}, f32[8,512]{1,0:T(8,128)S(1)}, u32[]{:S(2)}, u32[]{:S(2)}) %collective-permute-start.9) | collective-permute-done | bytes 16416 | tf_op jit(solution)/shard_map/ppermute | solution.py:288
  76.8 0.9 %collective-permute-done.8.refs_2_ = f32[8,512]{1,0:T(8,128)S(1)} collective-permute-done((f32[8,512]{1,0:T(8,128)S(1)}, f32[8,512]{1,0:T(8,128)S(1)}, u32[]{:S(2)}, u32[]{:S(2)}) %collective-permute-start.8) | collective-permute-done | bytes 16416 | tf_op jit(solution)/shard_map/ppermute | solution.py:288
  77.7 0.0 collective-permute-done.7.refs_1_
  77.7 1.1 %shard_map.65 = f32[512,512]{1,0:T(8,128)} custom-call(f32[512,512]{1,0:T(8,128)S(1)} %get-tuple-element.17.inflated, f32[8,512]{1,0:T(8,128)S(1)} %get-tuple-element.18.refs_0_, f32[8,512]{1,0:T(8,128)S(1)} %collective-permute-done.7.refs_1_, f32[8,512]{1,0:T(8,128)S(1)} %collective-permute-done.8.refs_2_, f32[8,512]{1,0:T(8,128)S(1)} %collective-permute-done.9.refs_3_), custom_call_target="tpu_custom_call" | custom-call | bytes 2162688 | tf_op jit(solution)/shard_map/pallas_call | solution.py:218
Async XLA Ops:
  0.6 15.2 %collective-permute-start.1 = (bf16[16,1,128,128]{3,2,1,0:T(8,128)(2,1)}, bf16[16,1,128,128]{3,2,1,0:T(8,128)(2,1)S(1)}, u32[]{:S(2)}, u32[]{:S(2)}) collective-permute-start(bf16[16,1,128,128]{3,2,1,0:T(8,128)(2,1)} %refs_3_.5), channel_id=1, source_target_pairs={{0,8},{4,12},{8,0},{12,4},{1,9},{5,13},{9,1},{13,5},{2,10},{6,14},... | collective-permute-start | bytes 1572872 | tf_op jit(solution)/shard_map/ppermute | solution.py:243
  3.7 12.9 %collective-permute-start = (bf16[16,1,128,128]{3,2,1,0:T(8,128)(2,1)}, bf16[16,1,128,128]{3,2,1,0:T(8,128)(2,1)S(1)}, u32[]{:S(2)}, u32[]{:S(2)}) collective-permute-start(bf16[16,1,128,128]{3,2,1,0:T(8,128)(2,1)} %refs_3_.5), channel_id=1, source_target_pairs={{0,4},{4,0},{8,12},{12,8},{1,5},{5,1},{9,13},{13,9},{2,6},{6,2},{1... | collective-permute-start | bytes 1572872 | tf_op jit(solution)/shard_map/ppermute | solution.py:244
  15.8 1.9 %collective-permute-start.2 = (bf16[16,1,128,128]{3,2,1,0:T(8,128)(2,1)S(1)}, bf16[16,1,128,128]{3,2,1,0:T(8,128)(2,1)S(1)}, u32[]{:S(2)}, u32[]{:S(2)}) collective-permute-start(bf16[16,1,128,128]{3,2,1,0:T(8,128)(2,1)S(1)} %collective-permute-done.1.refs_5_), channel_id=1, source_target_pairs={{0,4},{4,0},{8,12},{12,8},{1,5},{5,1},{9,13},{13,9},{2,6},{6,2},{1... | collective-permute-start | bytes 1572872 | tf_op jit(solution)/shard_map/ppermute | solution.py:244
  17.7 1.6 %copy-start = (bf16[512,2048]{1,0:T(8,128)(2,1)S(1)}, bf16[512,2048]{1,0:T(8,128)(2,1)}, u32[]{:S(2)}) copy-start(bf16[512,2048]{1,0:T(8,128)(2,1)} %refs_2_.5) | copy-start | bytes 6291460
  19.3 1.0 %copy-start.1 = (bf16[16,1,128,128]{3,2,1,0:T(8,128)(2,1)S(1)}, bf16[16,1,128,128]{3,2,1,0:T(8,128)(2,1)}, u32[]{:S(2)}) copy-start(bf16[16,1,128,128]{3,2,1,0:T(8,128)(2,1)} %refs_3_.5) | copy-start | bytes 1572868
  20.3 0.7 copy-start.2
  25.2 18.0 %collective-permute-start.3 = (s16[528,512]{1,0:T(8,128)(2,1)S(1)}, s16[528,512]{1,0:T(8,128)(2,1)S(1)}, u32[]{:S(2)}, u32[]{:S(2)}) collective-permute-start(s16[528,512]{1,0:T(8,128)(2,1)S(1)} %shard_map.60), channel_id=1, source_target_pairs={{0,1},{1,0},{2,3},{3,2},{4,5},{5,4},{6,7},{7,6},{8,9},{9,8},{10,11... | collective-permute-start | bytes 1622024 | tf_op jit(solution)/shard_map/ppermute | solution.py:263
  31.3 20.1 %collective-permute-start.5 = (s16[528,512]{1,0:T(8,128)(2,1)S(1)}, s16[528,512]{1,0:T(8,128)(2,1)S(1)}, u32[]{:S(2)}, u32[]{:S(2)}) collective-permute-start(s16[528,512]{1,0:T(8,128)(2,1)S(1)} %shard_map.61), channel_id=1, source_target_pairs={{0,2},{3,1},{4,6},{7,5},{8,10},{11,9},{12,14},{15,13},{16,18},{19,... | collective-permute-start | bytes 1622024 | tf_op jit(solution)/shard_map/ppermute | solution.py:266
  35.8 15.5 %collective-permute-start.4 = (s16[528,512]{1,0:T(8,128)(2,1)S(1)}, s16[528,512]{1,0:T(8,128)(2,1)S(1)}, u32[]{:S(2)}, u32[]{:S(2)}) collective-permute-start(s16[528,512]{1,0:T(8,128)(2,1)S(1)} %shard_map.61), channel_id=1, source_target_pairs={{1,2},{2,1},{5,6},{6,5},{9,10},{10,9},{13,14},{14,13},{17,18},{18,... | collective-permute-start | bytes 1622024 | tf_op jit(solution)/shard_map/ppermute | solution.py:265
  43.6 29.0 %collective-permute-start.6 = (s16[528,512]{1,0:T(8,128)(2,1)S(1)}, s16[528,512]{1,0:T(8,128)(2,1)S(1)}, u32[]{:S(2)}, u32[]{:S(2)}) collective-permute-start(s16[528,512]{1,0:T(8,128)(2,1)S(1)} %shard_map.63), channel_id=1, source_target_pairs={{0,1},{1,3},{3,2},{2,0},{4,5},{5,7},{7,6},{6,4},{8,9},{9,11},{11,1... | collective-permute-start | bytes 1622024 | tf_op jit(solution)/shard_map/ppermute | solution.py:276
  73.5 3.3 %collective-permute-start.9 = (f32[8,512]{1,0:T(8,128)S(1)}, f32[8,512]{1,0:T(8,128)S(1)}, u32[]{:S(2)}, u32[]{:S(2)}) collective-permute-start(f32[8,512]{1,0:T(8,128)S(1)} %get-tuple-element.18.refs_0_), channel_id=1, source_target_pairs={{0,12},{4,8},{8,4},{12,0},{1,13},{5,9},{9,5},{13,1},{2,14},{6,10},... | collective-permute-start | bytes 49160 | tf_op jit(solution)/shard_map/ppermute | solution.py:288
  74.0 3.7 %collective-permute-start.8 = (f32[8,512]{1,0:T(8,128)S(1)}, f32[8,512]{1,0:T(8,128)S(1)}, u32[]{:S(2)}, u32[]{:S(2)}) collective-permute-start(f32[8,512]{1,0:T(8,128)S(1)} %get-tuple-element.18.refs_0_), channel_id=1, source_target_pairs={{0,8},{4,12},{8,0},{12,4},{1,9},{5,13},{9,1},{13,5},{2,10},{6,14},... | collective-permute-start | bytes 49160 | tf_op jit(solution)/shard_map/ppermute | solution.py:288
  75.2 2.6 %collective-permute-start.7 = (f32[8,512]{1,0:T(8,128)S(1)}, f32[8,512]{1,0:T(8,128)S(1)}, u32[]{:S(2)}, u32[]{:S(2)}) collective-permute-start(f32[8,512]{1,0:T(8,128)S(1)} %get-tuple-element.18.refs_0_), channel_id=1, source_target_pairs={{0,4},{4,0},{8,12},{12,8},{1,5},{5,1},{9,13},{13,9},{2,6},{6,2},{1... | collective-permute-start | bytes 49160 | tf_op jit(solution)/shard_map/ppermute | solution.py:288

commit v2 on v1

--- a/solution.py
+++ b/solution.py
@@ -61,47 +61,67 @@
 
 
 def is_live(columns, counts, k, e):
-    rows, slots = columns.shape
+    slots, rows = columns.shape
     row_index = lax.axis_index("col") * rows + k
     all_rows = rows * lax.axis_size("col")
     return lax.rem(e - row_index + all_rows * slots, slots) < counts[k]
 
 
-def fill(slab, shard, columns, counts, blocks):
-    rows, _ = columns.shape
+def sort_live(ny, columns, counts, operand, own, lists, lens, load, operand_near, own_near, sems):
+    copies = [
+        pltpu.make_async_copy(far, near, sems.at[j])
+        for j, (far, near) in enumerate(((operand, operand_near), (own, own_near)))
+    ]
+    for copy in copies:
+        copy.start()
+    slots, rows = columns.shape
+    shards = load.shape[0] // SLAB_DEV
+
+    def clear(ref):
+        def step(j, carry):
+            ref[j] = 0
+            return carry
+
+        lax.fori_loop(0, ref.shape[0], step, 0)
+
+    clear(lens)
+    clear(load)
+    for place in range(slots):
+        e = slot_of(place, ny)
+
+        def one(k, carry, place=place, e=e):
+            @pl.when(is_live(columns, counts, k, e))
+            def _():
+                column = columns[e, k]
+                load[column] = load[column] + 1
+                shard = lax.div(column, SLAB_DEV)
+                at = place * shards + shard
+                length = lens[at]
+                lists[at * rows + length] = k * SLAB_DEV + column - shard * SLAB_DEV
+                lens[at] = length + 1
+
+            return carry
+
+        lax.fori_loop(0, rows, one, 0)
+    for copy in copies:
+        copy.wait()
+
+
+def fill(slab, shard, lists, lens, blocks):
+    rows = blocks[0].shape[0]
+    shards = lens.shape[0] // len(blocks)
     slab[...] = jnp.zeros_like(slab)
     for place, held in enumerate(blocks):
-        e = slot_of(place, len(blocks) // 2)
-
-        def one(k, carry, held=held, e=e):
-            column = columns[k, e] - shard * SLAB_DEV
-
-            @pl.when(is_live(columns, counts, k, e) & (column >= 0) & (column < SLAB_DEV))
-            def _():
-                at = (pl.ds(pl.multiple_of(k * SIDE, SIDE), SIDE), pl.ds(pl.multiple_of(column * SIDE, SIDE), SIDE))
-                slab[at] = held[k, 0]
-
+        at = place * shards + shard
+
+        def one(j, carry, held=held, at=at):
+            entry = lists[at * rows + j]
+            k, column = lax.div(entry, SLAB_DEV), lax.rem(entry, SLAB_DEV)
+            where = (pl.ds(pl.multiple_of(k * SIDE, SIDE), SIDE), pl.ds(pl.multiple_of(column * SIDE, SIDE), SIDE))
+            slab[where] = held[k, 0]
             return carry
 
-        lax.fori_loop(0, rows, one, 0, unroll=False)
-
-
-def count_live(load, columns, counts):
-    rows, slots = columns.shape
-
-    def clear(j, carry):
-        load[j] = 0
-        return carry
-
-    lax.fori_loop(0, load.shape[0], clear, 0)
-
-    def one(k, carry):
-        for e in range(slots):
-            j = columns[k, e]
-            load[j] = load[j] + is_live(columns, counts, k, e).astype(jnp.int32)
-        return carry
-
-    lax.fori_loop(0, rows, one, 0)
+        lax.fori_loop(0, lens[at], one, 0)
 
 
 def counts_of(load, shard, tile):
@@ -121,29 +141,29 @@
     lax.fori_loop(0, width // TILE, step, 0)
 
 
-def coded_product(which, nblocks, *refs):
-    columns, counts, operand, *blocks = refs[: 3 + nblocks]
-    out, slab, load = refs[3 + nblocks :]
-    shard = which(lax.axis_index("col"))
-    count_live(load, columns, counts)
-    fill(slab, shard, columns, counts, blocks)
-
-    def body(tile, lanes):
-        values = jnp.dot(operand[...], slab[:, lanes], preferred_element_type=jnp.float32)
-        put_coded(out, lanes, values, counts_of(load, shard, tile))
-
-    tiles(slab.shape[1], body)
+def coded_products(which, nblocks, *refs):
+    lists, lens, load, operand, *blocks = refs[: 4 + nblocks]
+    outs = refs[4 + nblocks : 4 + nblocks + len(which)]
+    slab = refs[-1]
+    for one, out in zip(which, outs):
+        shard = one(lax.axis_index("col"))
+        fill(slab, shard, lists, lens, blocks)
+
+        def body(tile, lanes, out=out, shard=shard):
+            values = jnp.dot(operand[...], slab[:, lanes], preferred_element_type=jnp.float32)
+            put_coded(out, lanes, values, counts_of(load, shard, tile))
+
+        tiles(slab.shape[1], body)
 
 
 def plain_products(which, nblocks, *refs):
-    columns, counts, operand, *blocks = refs[: 3 + nblocks]
-    outs = refs[3 + nblocks : 3 + nblocks + len(which)]
-    loads = refs[3 + nblocks + len(which) : 3 + nblocks + 2 * len(which)]
-    slab, load = refs[3 + nblocks + 2 * len(which) :]
-    count_live(load, columns, counts)
-    for one, out, row in zip(which, outs, loads):
+    lists, lens, load, operand, *blocks = refs[: 4 + nblocks]
+    outs = refs[4 + nblocks : 4 + nblocks + len(which)]
+    rows_out = refs[4 + nblocks + len(which) : 4 + nblocks + 2 * len(which)]
+    slab = refs[-1]
+    for one, out, row in zip(which, outs, rows_out):
         shard = one(lax.axis_index("col"))
-        fill(slab, shard, columns, counts, blocks)
+        fill(slab, shard, lists, lens, blocks)
 
         def body(tile, lanes, out=out, row=row, shard=shard):
             out[:, lanes] = jnp.dot(operand[...], slab[:, lanes], preferred_element_type=jnp.float32)
@@ -213,15 +233,15 @@
     tiles(inflated.shape[1], body)
 
 
-def call(kernel, ins, out_shape, out_specs, scratch=(), flops=0):
+def call(kernel, ins, out_shape, out_specs, scratch=(), flops=0, few=0, space=VMEM):
     moved = sum(x.size * x.dtype.itemsize for x in list(ins) + list(out_shape))
     return pl.pallas_call(
         kernel,
-        in_specs=[SMEM if x.dtype == jnp.int32 and x.ndim < 3 and x.size <= 4096 and x.shape[-1] <= 32 else VMEM for x in ins],
+        in_specs=[SMEM] * few + [space] * (len(ins) - few),
         out_shape=out_shape,
         out_specs=out_specs,
         scratch_shapes=list(scratch),
-        compiler_params=pltpu.CompilerParams(vmem_limit_bytes=40 << 20),
+        compiler_params=pltpu.CompilerParams(vmem_limit_bytes=24 << 20),
         cost_estimate=pl.CostEstimate(flops=flops, bytes_accessed=moved, transcendentals=0),
     )(*ins)
 
@@ -229,8 +249,9 @@
 def body_line(operand_panel, slot_blocks, slot_columns, live_counts):
     ny = lax.axis_size("row") // 2
     rows, depth = operand_panel.shape
+    here, slots = slot_columns.shape
     width = SLAB_DEV * SIDE
-    slab_width = SLAB_DEV * lax.axis_size("col")
+    shards = lax.axis_size("col")
     f32 = functools.partial(jax.ShapeDtypeStruct, dtype=jnp.float32)
     i32 = functools.partial(jax.ShapeDtypeStruct, dtype=jnp.int32)
     coded = jax.ShapeDtypeStruct((HEAD + rows, width), jnp.int16)
@@ -240,12 +261,28 @@
     def turn(by):
         return [(a, ((a // 2 + by) % ny) * 2 + a % 2) for a in range(2 * ny)]
 
-    held = [slot_blocks] + [lax.ppermute(slot_blocks, "row", turn(by)) for by in range(1, ny)]
-    blocks = [x for mine in held for x in (mine, lax.ppermute(mine, "row", swap))]
-
-    ins = [slot_columns, live_counts, operand_panel, *blocks]
-    scratch = [pltpu.VMEM((depth, width), jnp.bfloat16), pltpu.SMEM((slab_width,), jnp.int32)]
-    flops = 2 * rows * depth * width
+    lists, lens, load, operand_near, own_near = call(
+        functools.partial(sort_live, ny),
+        [slot_columns.T, live_counts, operand_panel, slot_blocks],
+        [
+            i32((slots * shards * here,)),
+            i32((slots * shards,)),
+            i32((SLAB_DEV * shards,)),
+            jax.ShapeDtypeStruct(operand_panel.shape, operand_panel.dtype),
+            jax.ShapeDtypeStruct(slot_blocks.shape, slot_blocks.dtype),
+        ],
+        [SMEM] * 3 + [VMEM] * 2,
+        [pltpu.SemaphoreType.DMA((2,))],
+        few=2,
+        space=pl.BlockSpec(memory_space=pltpu.HBM),
+    )
+    turned = [lax.ppermute(slot_blocks, "row", turn(by)) for by in range(1, ny)]
+    turned, lists = lax.optimization_barrier((turned, lists))
+    blocks = [own_near, lax.ppermute(slot_blocks, "row", swap)]
+    blocks += [x for came in turned for x in (came, lax.ppermute(came, "row", swap))]
+    ins = [lists, lens, load, operand_near, *blocks]
+    scratch = [pltpu.VMEM((depth, width), jnp.bfloat16)]
+    flops = 4 * rows * depth * width
 
     def first(z):
         return jnp.where(lax.rem(z, 2) == 0, 3, 0)
@@ -256,22 +293,22 @@
     def third(z):
         return jnp.where(z == 0, 1, jnp.where(z == 1, 3, jnp.where(z == 2, 0, 2)))
 
-    def product(which):
-        return call(functools.partial(coded_product, which, len(blocks)), ins, [coded], [VMEM], scratch, flops)[0]
-
-    send_a = product(first)
+    send_a, send_b = call(
+        functools.partial(coded_products, (first, second), len(blocks)), ins, [coded] * 2, [VMEM] * 2, scratch, flops, 3
+    )
+    came_b = lax.ppermute(send_b, "col", [(1, 2), (2, 1)])
     came_a = lax.ppermute(send_a, "col", [(0, 1), (1, 0), (2, 3), (3, 2)])
-    send_b = product(second)
-    came_b = lax.ppermute(send_b, "col", [(1, 2), (2, 1)])
-    came_f = lax.ppermute(send_b, "col", [(0, 2), (3, 1)])
     passed, own, passed_load, own_load = call(
         functools.partial(plain_products, (third, lambda z: z), len(blocks)),
         ins,
         [f32((rows, width)), f32((rows, width)), i32((8, width)), i32((8, width))],
         [VMEM] * 4,
         scratch,
-        2 * flops,
-    )
+        flops,
+        3,
+    )
+    send_f, passed = lax.optimization_barrier((send_b, passed))
+    came_f = lax.ppermute(send_f, "col", [(0, 2), (3, 1)])
     [send_t] = call(relay, [passed, passed_load, came_a], [coded], [VMEM])
     came_t = lax.ppermute(send_t, "col", [(0, 1), (1, 3), (3, 2), (2, 0)])
     own, own_load = call(
@@ -287,9 +324,7 @@
                 pairs = [(a, ((a // 2 + by) % ny) * 2 + (a % 2 ^ flip)) for a in range(2 * ny)]
                 others.append(lax.ppermute(totals, "row", pairs))
     all_rows = rows * lax.axis_size("row")
-    [mcl_columns] = call(
-        functools.partial(scale, all_rows), [inflated, *others], [f32((rows, width))], [VMEM]
-    )
+    [mcl_columns] = call(functools.partial(scale, all_rows), [inflated, *others], [f32((rows, width))], [VMEM])
     return mcl_columns, load
 
 

time: 79.1 us -> 70.5 us (0.89)
  waiting for transfers between devices: 43.1 us -> 36 us
  Pallas kernels: 17.6 us -> 13.8 us
  starting transfers between devices: 13.3 us -> 15.7 us
    ppermute x1, waiting for transfers between devices: 21 us -> 15.5 us  [body_line(): came_t = lax.ppermute(send_t, 'col', [(0, 1), (1, 3), (3, 2), (2, 0)])]
    ppermute x4, waiting for transfers between devices: 19.8 us -> 15.9 us  [the longest x1 8.71 us: body_line(): came_f = lax.ppermute(send_f, 'col', [(0, 2), (3, 1)])]
    pallas_call x7, Pallas kernels: 17.6 us -> 13.8 us  [call(): pl.pallas_call(kernel, in_specs=[SMEM] * few + [space] * (len(ins) - few)...]
    ppermute x1, waiting for transfers between devices: 0.01 us -> 2.32 us  [body_line(): came_a = lax.ppermute(send_a, 'col', [(0, 1), (1, 0), (2, 3), (3, 2)])]
    ppermute x1, starting transfers between devices: 1.28 us -> 2.63 us  [body_line(): came_t = lax.ppermute(send_t, 'col', [(0, 1), (1, 3), (3, 2), (2, 0)])]
    ppermute x4, starting transfers between devices: 7.57 us -> 8.71 us  [the longest x1 5.68 us: body_line(): came_f = lax.ppermute(send_f, 'col', [(0, 2), (3, 1)])]
    unnamed x7 -> x8, local copies, waits for them, and re-layouts: 4.05 us -> 3.97 us
  transfers between devices with their start and end apart: 10 -> 10, of which waited for: 6 -> 7; matrix products, arithmetic and copies ran while one was open for 1% -> 0% of each run, Pallas kernels for 14% -> 10%
where the time goes in v2:
time: 70.5 us; the launch traced here: 70.2 us
  waiting for transfers between devices  36 us (51%)
  starting transfers between devices  15.7 us (22%)
  Pallas kernels  13.8 us (20%)
  local copies, waits for them, and re-layouts  3.97 us (6%)
  between operations  0.71 us (1%)
    ppermute x1, waiting for transfers between devices, body_line(): came_t = lax.ppermute(send_t, 'col', [(0, 1), (1, 3), (3, 2), (2, 0)])  15.5 us
    pallas_call x7, Pallas kernels, call(): pl.pallas_call(kernel, in_specs=[SMEM] * few + [space] * (len(ins) - few)...  13.8 us
    ppermute x1, waiting for transfers between devices, body_line(): came_f = lax.ppermute(send_f, 'col', [(0, 2), (3, 1)])  8.71 us
    ppermute x1, starting transfers between devices, body_line(): came_f = lax.ppermute(send_f, 'col', [(0, 2), (3, 1)])  5.68 us
    ppermute x1, waiting for transfers between devices, body_line(): turned = [lax.ppermute(slot_blocks, 'row', turn(by)) for by in range(1, ny)]  5.33 us
    unnamed x8, local copies, waits for them, and re-layouts  3.97 us
    ppermute x1, starting transfers between devices, body_line(): turned = [lax.ppermute(slot_blocks, 'row', turn(by)) for by in range(1, ny)]  3.03 us
    ppermute x1, starting transfers between devices, body_line(): came_t = lax.ppermute(send_t, 'col', [(0, 1), (1, 3), (3, 2), (2, 0)])  2.63 us
  transfers between devices with their start and end apart: 10, of which 7 were waited for; matrix products, arithmetic and copies ran while one was open for 0% of the time, Pallas kernels for 10%

profile of v2, /device:TPU:0, one launch (start us, length us, event | category | flops | bytes accessed | tf_op | source)
XLA Modules:
  0.0 70.2 jit_solution(16601109920770085201)
XLA Ops:
  0.6 3.0 %collective-permute-start = (bf16[16,1,128,128]{3,2,1,0:T(8,128)(2,1)}, bf16[16,1,128,128]{3,2,1,0:T(8,128)(2,1)S(1)}, u32[]{:S(2)}, u32[]{:S(2)}) collective-permute-start(bf16[16,1,128,128]{3,2,1,0:T(8,128)(2,1)} %own.1), channel_id=1, source_target_pairs={{0,8},{4,12},{8,0},{12,4},{1,9},{5,13},{9,1},{13,5},{2,10},{6,14},... | collective-permute-start | bytes 1572872 | tf_op jit(solution)/shard_map/ppermute | solution.py:279
  3.7 0.0 collective-permute-start.1
  3.7 0.0 copy-start
  3.7 1.6 %copy-done = bf16[512,2048]{1,0:T(8,128)(2,1)S(1)} copy-done((bf16[512,2048]{1,0:T(8,128)(2,1)S(1)}, bf16[512,2048]{1,0:T(8,128)(2,1)}, u32[]{:S(2)}) %copy-start) | copy-done | bytes 2097176
  5.3 0.0 copy-start.1
  5.3 1.0 %copy-done.1 = bf16[16,1,128,128]{3,2,1,0:T(8,128)(2,1)S(1)} copy-done((bf16[16,1,128,128]{3,2,1,0:T(8,128)(2,1)S(1)}, bf16[16,1,128,128]{3,2,1,0:T(8,128)(2,1)}, u32[]{:S(2)}) %copy-start.1) | copy-done | bytes 524312
  6.3 0.0 copy-start.2
  6.3 0.7 copy-done.2
  7.0 0.0 copy-start.3
  7.0 0.7 copy-done.3
  7.6 2.8 %shard_map.59 = (s32[256]{0:T(256)S(1)}, s32[16]{0:T(128)S(1)}, s32[16]{0:T(128)S(1)}, bf16[512,2048]{1,0:T(8,128)(2,1)S(1)}, bf16[16,1,128,128]{3,2,1,0:T(8,128)(2,1)S(1)}) custom-call(s32[4,16]{1,0:T(4,128)S(1)} %bitcast.1, s32[16]{0:T(128)S(1)} %copy-done.3, bf16[512,2048]{1,0:T(8,128)(2,1)S(1)} %copy-done, bf16[16,1,128,128]{3,2,1,0:T(8,128)(2,1)S(1)} %copy-done.1), custom_call_target="tpu_custom_call" | custom-call | bytes 5244352 | tf_op jit(solution)/shard_map/pallas_call | solution.py:238
  10.5 5.3 %collective-permute-done.refs_6_ = bf16[16,1,128,128]{3,2,1,0:T(8,128)(2,1)S(1)} collective-permute-done((bf16[16,1,128,128]{3,2,1,0:T(8,128)(2,1)}, bf16[16,1,128,128]{3,2,1,0:T(8,128)(2,1)S(1)}, u32[]{:S(2)}, u32[]{:S(2)}) %collective-permute-start) | collective-permute-done | bytes 524320 | tf_op jit(solution)/shard_map/ppermute | solution.py:279
  15.8 0.0 collective-permute-start.2
  15.8 0.0 collective-permute-done.1.refs_5_
  15.8 1.9 %collective-permute-done.2.refs_7_ = bf16[16,1,128,128]{3,2,1,0:T(8,128)(2,1)S(1)} collective-permute-done((bf16[16,1,128,128]{3,2,1,0:T(8,128)(2,1)S(1)}, bf16[16,1,128,128]{3,2,1,0:T(8,128)(2,1)S(1)}, u32[]{:S(2)}, u32[]{:S(2)}) %collective-permute-start.2) | collective-permute-done | bytes 524320 | tf_op jit(solution)/shard_map/ppermute | solution.py:282
  17.7 4.5 %shard_map.61 = (s16[528,512]{1,0:T(8,128)(2,1)S(1)}, s16[528,512]{1,0:T(8,128)(2,1)S(1)}) custom-call(s32[256]{0:T(256)S(1)} %get-tuple-element.23.refs_0_, s32[16]{0:T(128)S(1)} %get-tuple-element.24.refs_1_, s32[16]{0:T(128)S(1)} %get-tuple-element.25.refs_2_, bf16[512,2048]{1,0:T(8,128)(2,1)S(1)} %get-tuple-element.26.refs_3_, ...), custom_call_target="tpu_custom_call" | custom-call | flops 2147483648 | bytes 5276800 | tf_op jit(solution)/shard_map/pallas_call | solution.py:238
  22.3 1.8 %collective-permute-start.3 = (s16[528,512]{1,0:T(8,128)(2,1)S(1)}, s16[528,512]{1,0:T(8,128)(2,1)S(1)}, u32[]{:S(2)}, u32[]{:S(2)}) collective-permute-start(s16[528,512]{1,0:T(8,128)(2,1)S(1)} %get-tuple-element.31), channel_id=1, source_target_pairs={{0,1},{1,0},{2,3},{3,2},{4,5},{5,4},{6,7},{7,6},{8,9},{9,8},{10,11... | collective-permute-start | bytes 1622024 | tf_op jit(solution)/shard_map/ppermute | solution.py:300
  24.1 0.7 collective-permute-start.4
  24.7 3.9 %shard_map.60 = (f32[512,512]{1,0:T(8,128)S(1)}, f32[512,512]{1,0:T(8,128)S(1)}, s32[8,512]{1,0:T(8,128)S(1)}, s32[8,512]{1,0:T(8,128)S(1)}) custom-call(s32[256]{0:T(256)S(1)} %get-tuple-element.23.refs_0_, s32[16]{0:T(128)S(1)} %get-tuple-element.24.refs_1_, s32[16]{0:T(128)S(1)} %get-tuple-element.25.refs_2_, ...), custom_call_target="tpu_custom_call" | custom-call | flops 2147483648 | bytes 6325376 | tf_op jit(solution)/shard_map/pallas_call | solution.py:238
  28.7 5.7 %collective-permute-start.5 = (s16[528,512]{1,0:T(8,128)(2,1)S(1)}, s16[528,512]{1,0:T(8,128)(2,1)S(1)}, u32[]{:S(2)}, u32[]{:S(2)}) collective-permute-start(s16[528,512]{1,0:T(8,128)(2,1)S(1)} %get-tuple-element.34), channel_id=1, source_target_pairs={{0,2},{3,1},{4,6},{7,5},{8,10},{11,9},{12,14},{15,13},{16,18},{19,... | collective-permute-start | bytes 1622024 | tf_op jit(solution)/shard_map/ppermute | solution.py:311
  34.4 2.3 %collective-permute-done.3.came_a.came = s16[528,512]{1,0:T(8,128)(2,1)S(1)} collective-permute-done((s16[528,512]{1,0:T(8,128)(2,1)S(1)}, s16[528,512]{1,0:T(8,128)(2,1)S(1)}, u32[]{:S(2)}, u32[]{:S(2)}) %collective-permute-start.3) | collective-permute-done | bytes 540704 | tf_op jit(solution)/shard_map/ppermute | solution.py:300
  36.7 0.3 shard_map.63
  37.0 2.6 %collective-permute-start.6 = (s16[528,512]{1,0:T(8,128)(2,1)S(1)}, s16[528,512]{1,0:T(8,128)(2,1)S(1)}, u32[]{:S(2)}, u32[]{:S(2)}) collective-permute-start(s16[528,512]{1,0:T(8,128)(2,1)S(1)} %shard_map.63), channel_id=1, source_target_pairs={{0,1},{1,3},{3,2},{2,0},{4,5},{5,7},{7,6},{6,4},{8,9},{9,11},{11,1... | collective-permute-start | bytes 1622024 | tf_op jit(solution)/shard_map/ppermute | solution.py:313
  39.6 8.7 %collective-permute-done.5.came_f = s16[528,512]{1,0:T(8,128)(2,1)S(1)} collective-permute-done((s16[528,512]{1,0:T(8,128)(2,1)S(1)}, s16[528,512]{1,0:T(8,128)(2,1)S(1)}, u32[]{:S(2)}, u32[]{:S(2)}) %collective-permute-start.5) | collective-permute-done | bytes 540704 | tf_op jit(solution)/shard_map/ppermute | solution.py:311
  48.3 0.0 collective-permute-done.4.came_b
  48.3 0.2 shard_map.62
  48.5 15.5 %collective-permute-done.6.came = s16[528,512]{1,0:T(8,128)(2,1)S(1)} collective-permute-done((s16[528,512]{1,0:T(8,128)(2,1)S(1)}, s16[528,512]{1,0:T(8,128)(2,1)S(1)}, u32[]{:S(2)}, u32[]{:S(2)}) %collective-permute-start.6) | collective-permute-done | bytes 540704 | tf_op jit(solution)/shard_map/ppermute | solution.py:313
  64.0 0.9 %shard_map.64 = (f32[512,512]{1,0:T(8,128)S(1)}, f32[8,512]{1,0:T(8,128)S(1)}, s32[4]{0:T(128)}) custom-call(f32[512,512]{1,0:T(8,128)S(1)} %get-tuple-element.35.own, s32[8,512]{1,0:T(8,128)S(1)} %get-tuple-element.36.own_load, s16[528,512]{1,0:T(8,128)(2,1)S(1)} %collective-permute-done.6.came), custom_call_target="tpu_custom_call" | custom-call | bytes 2670608 | tf_op jit(solution)/shard_map/pallas_call | solution.py:238
  64.9 0.5 collective-permute-start.9
  65.4 1.2 %collective-permute-start.8 = (f32[8,512]{1,0:T(8,128)S(1)}, f32[8,512]{1,0:T(8,128)S(1)}, u32[]{:S(2)}, u32[]{:S(2)}) collective-permute-start(f32[8,512]{1,0:T(8,128)S(1)} %get-tuple-element.40.refs_0_), channel_id=1, source_target_pairs={{0,8},{4,12},{8,0},{12,4},{1,9},{5,13},{9,1},{13,5},{2,10},{6,14},... | collective-permute-start | bytes 49160 | tf_op jit(solution)/shard_map/ppermute | solution.py:325
  66.6 0.3 collective-permute-start.7
  66.8 1.4 %collective-permute-done.9.refs_3_ = f32[8,512]{1,0:T(8,128)S(1)} collective-permute-done((f32[8,512]{1,0:T(8,128)S(1)}, f32[8,512]{1,0:T(8,128)S(1)}, u32[]{:S(2)}, u32[]{:S(2)}) %collective-permute-start.9) | collective-permute-done | bytes 16416 | tf_op jit(solution)/shard_map/ppermute | solution.py:325
  68.2 0.9 %collective-permute-done.8.refs_2_ = f32[8,512]{1,0:T(8,128)S(1)} collective-permute-done((f32[8,512]{1,0:T(8,128)S(1)}, f32[8,512]{1,0:T(8,128)S(1)}, u32[]{:S(2)}, u32[]{:S(2)}) %collective-permute-start.8) | collective-permute-done | bytes 16416 | tf_op jit(solution)/shard_map/ppermute | solution.py:325
  69.1 0.0 collective-permute-done.7.refs_1_
  69.1 1.1 %shard_map.65 = f32[512,512]{1,0:T(8,128)} custom-call(f32[512,512]{1,0:T(8,128)S(1)} %get-tuple-element.39.inflated, f32[8,512]{1,0:T(8,128)S(1)} %get-tuple-element.40.refs_0_, f32[8,512]{1,0:T(8,128)S(1)} %collective-permute-done.7.refs_1_, f32[8,512]{1,0:T(8,128)S(1)} %collective-permute-done.8.refs_2_, f32[8,512]{1,0:T(8,128)S(1)} %collective-permute-done.9.refs_3_), custom_call_target="tpu_custom_call" | custom-call | bytes 2162688 | tf_op jit(solution)/shard_map/pallas_call | solution.py:238
Async XLA Ops:
  0.6 15.2 %collective-permute-start = (bf16[16,1,128,128]{3,2,1,0:T(8,128)(2,1)}, bf16[16,1,128,128]{3,2,1,0:T(8,128)(2,1)S(1)}, u32[]{:S(2)}, u32[]{:S(2)}) collective-permute-start(bf16[16,1,128,128]{3,2,1,0:T(8,128)(2,1)} %own.1), channel_id=1, source_target_pairs={{0,8},{4,12},{8,0},{12,4},{1,9},{5,13},{9,1},{13,5},{2,10},{6,14},... | collective-permute-start | bytes 1572872 | tf_op jit(solution)/shard_map/ppermute | solution.py:279
  3.7 12.1 %collective-permute-start.1 = (bf16[16,1,128,128]{3,2,1,0:T(8,128)(2,1)}, bf16[16,1,128,128]{3,2,1,0:T(8,128)(2,1)S(1)}, u32[]{:S(2)}, u32[]{:S(2)}) collective-permute-start(bf16[16,1,128,128]{3,2,1,0:T(8,128)(2,1)} %own.1), channel_id=1, source_target_pairs={{0,4},{4,0},{8,12},{12,8},{1,5},{5,1},{9,13},{13,9},{2,6},{6,2},{1... | collective-permute-start | bytes 1572872 | tf_op jit(solution)/shard_map/ppermute | solution.py:281
  3.7 1.6 %copy-start = (bf16[512,2048]{1,0:T(8,128)(2,1)S(1)}, bf16[512,2048]{1,0:T(8,128)(2,1)}, u32[]{:S(2)}) copy-start(bf16[512,2048]{1,0:T(8,128)(2,1)} %operand.1) | copy-start | bytes 6291460
  5.3 1.0 %copy-start.1 = (bf16[16,1,128,128]{3,2,1,0:T(8,128)(2,1)S(1)}, bf16[16,1,128,128]{3,2,1,0:T(8,128)(2,1)}, u32[]{:S(2)}) copy-start(bf16[16,1,128,128]{3,2,1,0:T(8,128)(2,1)} %own.1) | copy-start | bytes 1572868
  6.3 0.7 copy-start.2
  7.0 0.7 copy-start.3
  15.8 1.9 %collective-permute-start.2 = (bf16[16,1,128,128]{3,2,1,0:T(8,128)(2,1)S(1)}, bf16[16,1,128,128]{3,2,1,0:T(8,128)(2,1)S(1)}, u32[]{:S(2)}, u32[]{:S(2)}) collective-permute-start(bf16[16,1,128,128]{3,2,1,0:T(8,128)(2,1)S(1)} %collective-permute-done.refs_6_), channel_id=1, source_target_pairs={{0,4},{4,0},{8,12},{12,8},{1,5},{5,1},{9,13},{13,9},{2,6},{6,2},{1... | collective-permute-start | bytes 1572872 | tf_op jit(solution)/shard_map/ppermute | solution.py:282
  22.3 14.4 %collective-permute-start.3 = (s16[528,512]{1,0:T(8,128)(2,1)S(1)}, s16[528,512]{1,0:T(8,128)(2,1)S(1)}, u32[]{:S(2)}, u32[]{:S(2)}) collective-permute-start(s16[528,512]{1,0:T(8,128)(2,1)S(1)} %get-tuple-element.31), channel_id=1, source_target_pairs={{0,1},{1,0},{2,3},{3,2},{4,5},{5,4},{6,7},{7,6},{8,9},{9,8},{10,11... | collective-permute-start | bytes 1622024 | tf_op jit(solution)/shard_map/ppermute | solution.py:300
  24.1 24.3 %collective-permute-start.4 = (s16[528,512]{1,0:T(8,128)(2,1)S(1)}, s16[528,512]{1,0:T(8,128)(2,1)S(1)}, u32[]{:S(2)}, u32[]{:S(2)}) collective-permute-start(s16[528,512]{1,0:T(8,128)(2,1)S(1)} %get-tuple-element.34), channel_id=1, source_target_pairs={{1,2},{2,1},{5,6},{6,5},{9,10},{10,9},{13,14},{14,13},{17,18},{18,... | collective-permute-start | bytes 1622024 | tf_op jit(solution)/shard_map/ppermute | solution.py:299
  28.7 19.6 %collective-permute-start.5 = (s16[528,512]{1,0:T(8,128)(2,1)S(1)}, s16[528,512]{1,0:T(8,128)(2,1)S(1)}, u32[]{:S(2)}, u32[]{:S(2)}) collective-permute-start(s16[528,512]{1,0:T(8,128)(2,1)S(1)} %get-tuple-element.34), channel_id=1, source_target_pairs={{0,2},{3,1},{4,6},{7,5},{8,10},{11,9},{12,14},{15,13},{16,18},{19,... | collective-permute-start | bytes 1622024 | tf_op jit(solution)/shard_map/ppermute | solution.py:311
  37.0 27.0 %collective-permute-start.6 = (s16[528,512]{1,0:T(8,128)(2,1)S(1)}, s16[528,512]{1,0:T(8,128)(2,1)S(1)}, u32[]{:S(2)}, u32[]{:S(2)}) collective-permute-start(s16[528,512]{1,0:T(8,128)(2,1)S(1)} %shard_map.63), channel_id=1, source_target_pairs={{0,1},{1,3},{3,2},{2,0},{4,5},{5,7},{7,6},{6,4},{8,9},{9,11},{11,1... | collective-permute-start | bytes 1622024 | tf_op jit(solution)/shard_map/ppermute | solution.py:313
  64.9 3.3 %collective-permute-start.9 = (f32[8,512]{1,0:T(8,128)S(1)}, f32[8,512]{1,0:T(8,128)S(1)}, u32[]{:S(2)}, u32[]{:S(2)}) collective-permute-start(f32[8,512]{1,0:T(8,128)S(1)} %get-tuple-element.40.refs_0_), channel_id=1, source_target_pairs={{0,12},{4,8},{8,4},{12,0},{1,13},{5,9},{9,5},{13,1},{2,14},{6,10},... | collective-permute-start | bytes 49160 | tf_op jit(solution)/shard_map/ppermute | solution.py:325
  65.4 3.7 %collective-permute-start.8 = (f32[8,512]{1,0:T(8,128)S(1)}, f32[8,512]{1,0:T(8,128)S(1)}, u32[]{:S(2)}, u32[]{:S(2)}) collective-permute-start(f32[8,512]{1,0:T(8,128)S(1)} %get-tuple-element.40.refs_0_), channel_id=1, source_target_pairs={{0,8},{4,12},{8,0},{12,4},{1,9},{5,13},{9,1},{13,5},{2,10},{6,14},... | collective-permute-start | bytes 49160 | tf_op jit(solution)/shard_map/ppermute | solution.py:325
  66.6 2.6 %collective-permute-start.7 = (f32[8,512]{1,0:T(8,128)S(1)}, f32[8,512]{1,0:T(8,128)S(1)}, u32[]{:S(2)}, u32[]{:S(2)}) collective-permute-start(f32[8,512]{1,0:T(8,128)S(1)} %get-tuple-element.40.refs_0_), channel_id=1, source_target_pairs={{0,4},{4,0},{8,12},{12,8},{1,5},{5,1},{9,13},{13,9},{2,6},{6,2},{1... | collective-permute-start | bytes 49160 | tf_op jit(solution)/shard_map/ppermute | solution.py:325

commit v3 on v2

--- a/solution.py
+++ b/solution.py
@@ -11,7 +11,8 @@
 SIDE = 128
 HEAD = 16
 TILE = 256
-STEPS = 32752.0
+STEPS = 32700.0
+NEAREST = 12582912.0
 OCTAVE = 128.0
 
 VMEM = pl.BlockSpec(memory_space=pltpu.VMEM)
@@ -25,8 +26,8 @@
 
 
 def encode(values, code):
-    scaled = jnp.round(values * (STEPS * jnp.exp2(code * (-1.0 / OCTAVE))))
-    return jnp.clip(scaled, -32767.0, 32767.0).astype(jnp.int32).astype(jnp.int16)
+    scaled = values * (STEPS * jnp.exp2(code * (-1.0 / OCTAVE)))
+    return ((scaled + NEAREST) - NEAREST).astype(jnp.int32).astype(jnp.int16)
 
 
 def head_rows(code, counts):
@@ -67,7 +68,29 @@
     return lax.rem(e - row_index + all_rows * slots, slots) < counts[k]
 
 
-def sort_live(ny, columns, counts, operand, own, lists, lens, load, operand_near, own_near, sems):
+class Plan:
+    def __init__(self, ref, rows, slots, shards):
+        self.ref, self.rows, self.slots, self.shards = ref, rows, slots, shards
+        self.lens = rows * slots * shards
+        self.loads = self.lens + slots * shards
+        self.size = self.loads + SLAB_DEV * shards
+
+    def entry(self, place, shard, j):
+        return (place * self.shards + shard) * self.rows + j
+
+    def length(self, place, shard):
+        return self.lens + place * self.shards + shard
+
+    def load(self, column):
+        return self.loads + column
+
+
+def plan_of(ref, operand):
+    rows = operand.shape[1] // SIDE
+    return Plan(ref, rows, lax.axis_size("row"), lax.axis_size("col"))
+
+
+def begin(ny, which, columns, counts, operand, own, twin, plan_ref, operand_near, own_near, total, sems):
     copies = [
         pltpu.make_async_copy(far, near, sems.at[j])
         for j, (far, near) in enumerate(((operand, operand_near), (own, own_near)))
@@ -75,17 +98,13 @@
     for copy in copies:
         copy.start()
     slots, rows = columns.shape
-    shards = load.shape[0] // SLAB_DEV
-
-    def clear(ref):
-        def step(j, carry):
-            ref[j] = 0
-            return carry
-
-        lax.fori_loop(0, ref.shape[0], step, 0)
-
-    clear(lens)
-    clear(load)
+    plan = plan_of(plan_ref, operand)
+
+    def clear(j, carry):
+        plan_ref[plan.lens + j] = 0
+        return carry
+
+    lax.fori_loop(0, plan.size - plan.lens, clear, 0)
     for place in range(slots):
         e = slot_of(place, ny)
 
@@ -93,43 +112,78 @@
             @pl.when(is_live(columns, counts, k, e))
             def _():
                 column = columns[e, k]
-                load[column] = load[column] + 1
+                plan_ref[plan.load(column)] = plan_ref[plan.load(column)] + 1
                 shard = lax.div(column, SLAB_DEV)
-                at = place * shards + shard
-                length = lens[at]
-                lists[at * rows + length] = k * SLAB_DEV + column - shard * SLAB_DEV
-                lens[at] = length + 1
+                at = plan.length(place, shard)
+                length = plan_ref[at]
+                plan_ref[plan.entry(place, shard, length)] = k * SLAB_DEV + column - shard * SLAB_DEV
+                plan_ref[at] = length + 1
 
             return carry
 
         lax.fori_loop(0, rows, one, 0)
     for copy in copies:
         copy.wait()
-
-
-def fill(slab, shard, lists, lens, blocks):
-    rows = blocks[0].shape[0]
-    shards = lens.shape[0] // len(blocks)
+    total[...] = jnp.zeros_like(total)
+    for place, held in enumerate((own_near, twin)):
+        add_terms(plan, which(lax.axis_index("col")), place, held, total, operand_near)
+
+
+def add_terms(plan, shard, place, held, total, operand):
+    length = plan.ref[plan.length(place, shard)]
+
+    def term(j):
+        entry = jnp.where(j < length, plan.ref[plan.entry(place, shard, jnp.minimum(j, plan.rows - 1))], 0)
+        k, column = lax.div(entry, SLAB_DEV), lax.rem(entry, SLAB_DEV)
+        block = held[k, 0]
+        block = jnp.where(j < length, block, jnp.zeros_like(block))
+        left = operand[:, pl.ds(pl.multiple_of(k * SIDE, SIDE), SIDE)]
+        lanes = pl.ds(pl.multiple_of(column * SIDE, SIDE), SIDE)
+        return lanes, jnp.dot(left, block, preferred_element_type=jnp.float32)
+
+    def step(pair, carry):
+        for lanes, value in [term(2 * pair), term(2 * pair + 1)]:
+            total[:, lanes] = total[:, lanes] + value
+        return carry
+
+    lax.fori_loop(0, lax.div(length + 1, 2), step, 0)
+
+
+def go_on(which, place, plan_ref, operand, held, _, total):
+    add_terms(plan_of(plan_ref, operand), which(lax.axis_index("col")), place, held, total, operand)
+
+
+def code_sum(which, place, plan_ref, operand, held, total, out):
+    plan = plan_of(plan_ref, operand)
+    shard = which(lax.axis_index("col"))
+    add_terms(plan, shard, place, held, total, operand)
+
+    def body(tile, lanes):
+        put_coded(out, lanes, total[:, lanes], counts_of(plan, shard, tile))
+
+    tiles(total.shape[1], body)
+
+
+def fill(slab, plan, shard, blocks):
     slab[...] = jnp.zeros_like(slab)
     for place, held in enumerate(blocks):
-        at = place * shards + shard
-
-        def one(j, carry, held=held, at=at):
-            entry = lists[at * rows + j]
+
+        def one(j, carry, place=place, held=held):
+            entry = plan.ref[plan.entry(place, shard, j)]
             k, column = lax.div(entry, SLAB_DEV), lax.rem(entry, SLAB_DEV)
             where = (pl.ds(pl.multiple_of(k * SIDE, SIDE), SIDE), pl.ds(pl.multiple_of(column * SIDE, SIDE), SIDE))
             slab[where] = held[k, 0]
             return carry
 
-        lax.fori_loop(0, lens[at], one, 0)
-
-
-def counts_of(load, shard, tile):
+        lax.fori_loop(0, plan.ref[plan.length(place, shard)], one, 0)
+
+
+def counts_of(plan, shard, tile):
     lane = lax.broadcasted_iota(jnp.int32, (1, TILE), 1)
     counts = jnp.zeros((1, TILE), jnp.int32)
     for j in range(TILE // SIDE):
         block = shard * SLAB_DEV + tile * (TILE // SIDE) + j
-        counts = jnp.where((lane >= j * SIDE) & (lane < (j + 1) * SIDE), load[block], counts)
+        counts = jnp.where((lane >= j * SIDE) & (lane < (j + 1) * SIDE), plan.ref[plan.load(block)], counts)
     return counts
 
 
@@ -141,35 +195,30 @@
     lax.fori_loop(0, width // TILE, step, 0)
 
 
-def coded_products(which, nblocks, *refs):
-    lists, lens, load, operand, *blocks = refs[: 4 + nblocks]
-    outs = refs[4 + nblocks : 4 + nblocks + len(which)]
-    slab = refs[-1]
-    for one, out in zip(which, outs):
-        shard = one(lax.axis_index("col"))
-        fill(slab, shard, lists, lens, blocks)
-
-        def body(tile, lanes, out=out, shard=shard):
+def products(coded, plain, nblocks, *refs):
+    plan_ref, operand, *blocks = refs[: 2 + nblocks]
+    out_coded, *outs, slab = refs[2 + nblocks :]
+    plan = plan_of(plan_ref, operand)
+    outs, loads = outs[: len(plain)], outs[len(plain) :]
+
+    def one_shard(which, put):
+        shard = which(lax.axis_index("col"))
+        fill(slab, plan, shard, blocks)
+
+        def body(tile, lanes):
             values = jnp.dot(operand[...], slab[:, lanes], preferred_element_type=jnp.float32)
-            put_coded(out, lanes, values, counts_of(load, shard, tile))
+            put(lanes, values, counts_of(plan, shard, tile))
 
         tiles(slab.shape[1], body)
 
-
-def plain_products(which, nblocks, *refs):
-    lists, lens, load, operand, *blocks = refs[: 4 + nblocks]
-    outs = refs[4 + nblocks : 4 + nblocks + len(which)]
-    rows_out = refs[4 + nblocks + len(which) : 4 + nblocks + 2 * len(which)]
-    slab = refs[-1]
-    for one, out, row in zip(which, outs, rows_out):
-        shard = one(lax.axis_index("col"))
-        fill(slab, shard, lists, lens, blocks)
-
-        def body(tile, lanes, out=out, row=row, shard=shard):
-            out[:, lanes] = jnp.dot(operand[...], slab[:, lanes], preferred_element_type=jnp.float32)
-            row[:, lanes] = jnp.broadcast_to(counts_of(load, shard, tile), (8, TILE))
-
-        tiles(slab.shape[1], body)
+    one_shard(coded, functools.partial(put_coded, out_coded))
+    for which, out, row in zip(plain, outs, loads):
+
+        def put(lanes, values, counts, out=out, row=row):
+            out[:, lanes] = values
+            row[:, lanes] = jnp.broadcast_to(counts, (8, TILE))
+
+        one_shard(which, put)
 
 
 def relay(own, own_load, came, out):
@@ -188,21 +237,18 @@
     tiles(own.shape[1], body)
 
 
-def settle(own, own_load, came_a, came_b, came_f, out, out_load):
+def settle(own, own_load, came_b, came_f, out, out_load):
     place = lax.axis_index("col")
     inner = (place == 1) | (place == 2)
 
     def body(tile, lanes):
+        out[:, lanes] = own[:, lanes] + decode(came_f, lanes)
+        out_load[:, lanes] = own_load[:, lanes] + head_counts(came_f, lanes)
+
         @pl.when(inner)
         def _():
-            out[:, lanes] = own[:, lanes] + decode(came_b, lanes) + decode(came_f, lanes)
-            load = own_load[0:1, lanes] + head_counts(came_b, lanes) + head_counts(came_f, lanes)
-            out_load[:, lanes] = jnp.broadcast_to(load, (8, TILE))
-
-        @pl.when(jnp.logical_not(inner))
-        def _():
-            out[:, lanes] = own[:, lanes] + decode(came_a, lanes)
-            out_load[:, lanes] = jnp.broadcast_to(own_load[0:1, lanes] + head_counts(came_a, lanes), (8, TILE))
+            out[:, lanes] = out[:, lanes] + decode(came_b, lanes)
+            out_load[:, lanes] = out_load[:, lanes] + head_counts(came_b, lanes)
 
     tiles(own.shape[1], body)
 
@@ -233,14 +279,15 @@
     tiles(inflated.shape[1], body)
 
 
-def call(kernel, ins, out_shape, out_specs, scratch=(), flops=0, few=0, space=VMEM):
+def call(kernel, ins, out_shape, out_specs, scratch=(), flops=0, few=0, far=0, onto=None):
     moved = sum(x.size * x.dtype.itemsize for x in list(ins) + list(out_shape))
     return pl.pallas_call(
         kernel,
-        in_specs=[SMEM] * few + [space] * (len(ins) - few),
+        in_specs=[SMEM] * few + [pl.BlockSpec(memory_space=pltpu.HBM)] * far + [VMEM] * (len(ins) - few - far),
         out_shape=out_shape,
         out_specs=out_specs,
         scratch_shapes=list(scratch),
+        input_output_aliases=onto or {},
         compiler_params=pltpu.CompilerParams(vmem_limit_bytes=24 << 20),
         cost_estimate=pl.CostEstimate(flops=flops, bytes_accessed=moved, transcendentals=0),
     )(*ins)
@@ -261,58 +308,76 @@
     def turn(by):
         return [(a, ((a // 2 + by) % ny) * 2 + a % 2) for a in range(2 * ny)]
 
-    lists, lens, load, operand_near, own_near = call(
-        functools.partial(sort_live, ny),
-        [slot_columns.T, live_counts, operand_panel, slot_blocks],
+    def first(z):
+        return 3 - z
+
+    def second(z):
+        return jnp.where(z == 0, 2, jnp.where(z == 1, 0, jnp.where(z == 2, 3, 1)))
+
+    def third(z):
+        return 3 - second(z)
+
+    flops = 2 * rows * depth * width
+    turned = [lax.ppermute(slot_blocks, "row", turn(by)) for by in range(1, ny)]
+    twin = lax.ppermute(slot_blocks, "row", swap)
+    plan, operand_near, own_near, total = call(
+        functools.partial(begin, ny, first),
+        [slot_columns.T, live_counts, operand_panel, slot_blocks, twin],
         [
-            i32((slots * shards * here,)),
-            i32((slots * shards,)),
-            i32((SLAB_DEV * shards,)),
+            i32((Plan(None, here, slots, shards).size,)),
             jax.ShapeDtypeStruct(operand_panel.shape, operand_panel.dtype),
             jax.ShapeDtypeStruct(slot_blocks.shape, slot_blocks.dtype),
+            f32((rows, width)),
         ],
-        [SMEM] * 3 + [VMEM] * 2,
+        [SMEM] + [VMEM] * 3,
         [pltpu.SemaphoreType.DMA((2,))],
+        flops // 4,
         few=2,
-        space=pl.BlockSpec(memory_space=pltpu.HBM),
-    )
-    turned = [lax.ppermute(slot_blocks, "row", turn(by)) for by in range(1, ny)]
-    turned, lists = lax.optimization_barrier((turned, lists))
-    blocks = [own_near, lax.ppermute(slot_blocks, "row", swap)]
+        far=2,
+    )
+    turned, plan = lax.optimization_barrier((turned, plan))
+    blocks = [own_near, twin]
     blocks += [x for came in turned for x in (came, lax.ppermute(came, "row", swap))]
-    ins = [lists, lens, load, operand_near, *blocks]
-    scratch = [pltpu.VMEM((depth, width), jnp.bfloat16)]
-    flops = 4 * rows * depth * width
-
-    def first(z):
-        return jnp.where(lax.rem(z, 2) == 0, 3, 0)
-
-    def second(z):
-        return jnp.where(z < 2, 2, 1)
-
-    def third(z):
-        return jnp.where(z == 0, 1, jnp.where(z == 1, 3, jnp.where(z == 2, 0, 2)))
-
-    send_a, send_b = call(
-        functools.partial(coded_products, (first, second), len(blocks)), ins, [coded] * 2, [VMEM] * 2, scratch, flops, 3
-    )
-    came_b = lax.ppermute(send_b, "col", [(1, 2), (2, 1)])
+    for place in range(2, slots - 1):
+        [total] = call(
+            functools.partial(go_on, first, place),
+            [plan, operand_near, blocks[place], total],
+            [f32((rows, width))],
+            [VMEM],
+            (),
+            flops // 8,
+            1,
+            onto={3: 0},
+        )
+    [send_a] = call(
+        functools.partial(code_sum, first, slots - 1),
+        [plan, operand_near, blocks[-1], total],
+        [coded],
+        [VMEM],
+        (),
+        flops // 8,
+        1,
+    )
     came_a = lax.ppermute(send_a, "col", [(0, 1), (1, 0), (2, 3), (3, 2)])
-    passed, own, passed_load, own_load = call(
-        functools.partial(plain_products, (third, lambda z: z), len(blocks)),
-        ins,
-        [f32((rows, width)), f32((rows, width)), i32((8, width)), i32((8, width))],
-        [VMEM] * 4,
-        scratch,
-        flops,
-        3,
-    )
-    send_f, passed = lax.optimization_barrier((send_b, passed))
-    came_f = lax.ppermute(send_f, "col", [(0, 2), (3, 1)])
+    came_b = lax.ppermute(
+        send_a,
+        ("row", "col"),
+        [(4 * r + c, 4 * r + 3 - c if c in (1, 2) else 4 * (r ^ 1) + c) for r in range(2 * ny) for c in range(4)],
+    )
+    send_f, passed, own, passed_load, own_load = call(
+        functools.partial(products, second, (third, lambda z: z), len(blocks)),
+        [plan, operand_near, *blocks],
+        [coded, f32((rows, width)), f32((rows, width)), i32((8, width)), i32((8, width))],
+        [VMEM] * 5,
+        [pltpu.VMEM((depth, width), jnp.bfloat16)],
+        3 * flops,
+        1,
+    )
+    came_f = lax.ppermute(send_f, "col", [(0, 2), (1, 0), (2, 3), (3, 1)])
     [send_t] = call(relay, [passed, passed_load, came_a], [coded], [VMEM])
     came_t = lax.ppermute(send_t, "col", [(0, 1), (1, 3), (3, 2), (2, 0)])
     own, own_load = call(
-        settle, [own, own_load, came_a, came_b, came_f], [f32((rows, width)), i32((8, width))], [VMEM] * 2
+        settle, [own, own_load, came_b, came_f], [f32((rows, width)), i32((8, width))], [VMEM] * 2
     )
     inflated, totals, load = call(
         inflate, [own, own_load, came_t], [f32((rows, width)), f32((8, width)), i32((SLAB_DEV,))], [VMEM, VMEM, SMEM]

time: 70.5 us -> 67 us (0.950)
  starting transfers between devices: 15.7 us -> 11.2 us
  Pallas kernels: 13.8 us -> 15.5 us
    ppermute x3, starting transfers between devices: 6.36 us -> 3.46 us  [the longest x1 2.78 us: body_line(): came_f = lax.ppermute(send_f, 'col', [(0, 2), (1, 0), (2, 3), (3, 1)])]
    ppermute x1, waiting for transfers between devices: 2.32 us -> 4.57 us  [body_line(): came_a = lax.ppermute(send_a, 'col', [(0, 1), (1, 0), (2, 3), (3, 2)])]
    ppermute x1, waiting for transfers between devices: 15.5 us -> 13.4 us  [body_line(): came_t = lax.ppermute(send_t, 'col', [(0, 1), (1, 3), (3, 2), (2, 0)])]
    pallas_call x7 -> x8, Pallas kernels: 13.8 us -> 15.5 us  [call(): pl.pallas_call(kernel, in_specs=[SMEM] * few + [pl.BlockSpec(memory_space...]
    ppermute x1, waiting for transfers between devices: 5.33 us -> 4.28 us  [body_line(): turned = [lax.ppermute(slot_blocks, 'row', turn(by)) for by in range(1, ny)]]
    ppermute x1, starting transfers between devices: 2.63 us -> 1.64 us  [body_line(): came_t = lax.ppermute(send_t, 'col', [(0, 1), (1, 3), (3, 2), (2, 0)])]
    ppermute x3, waiting for transfers between devices: 2.29 us -> 3.22 us  [body_line(): others.append(lax.ppermute(totals, 'row', pairs))]
    ppermute x1, waiting for transfers between devices: 1.9 us -> 1.04 us  [body_line(): lax.ppermute(came, 'row', swap)]
  transfers between devices with their start and end apart: 10 -> 10, of which waited for: 7 -> 7; matrix products, arithmetic and copies ran while one was open for 0% -> 0% of each run, Pallas kernels for 10% -> 18%
where the time goes in v3:
time: 67 us; the launch traced here: 66.7 us
  waiting for transfers between devices  35.3 us (53%)
  Pallas kernels  15.5 us (23%)
  starting transfers between devices  11.2 us (17%)
  local copies, waits for them, and re-layouts  3.97 us (6%)
  between operations  0.7 us (1%)
    pallas_call x8, Pallas kernels, call(): pl.pallas_call(kernel, in_specs=[SMEM] * few + [pl.BlockSpec(memory_space...  15.5 us
    ppermute x1, waiting for transfers between devices, body_line(): came_t = lax.ppermute(send_t, 'col', [(0, 1), (1, 3), (3, 2), (2, 0)])  13.4 us
    ppermute x1, waiting for transfers between devices, body_line(): came_f = lax.ppermute(send_f, 'col', [(0, 2), (1, 0), (2, 3), (3, 1)])  8.86 us
    ppermute x1, waiting for transfers between devices, body_line(): came_a = lax.ppermute(send_a, 'col', [(0, 1), (1, 0), (2, 3), (3, 2)])  4.57 us
    ppermute x1, waiting for transfers between devices, body_line(): turned = [lax.ppermute(slot_blocks, 'row', turn(by)) for by in range(1, ny)]  4.28 us
    unnamed x8, local copies, waits for them, and re-layouts  3.97 us
    ppermute x3, waiting for transfers between devices, body_line(): others.append(lax.ppermute(totals, 'row', pairs))  3.22 us
    ppermute x1, starting transfers between devices, body_line(): came_f = lax.ppermute(send_f, 'col', [(0, 2), (1, 0), (2, 3), (3, 1)])  2.78 us
  transfers between devices with their start and end apart: 10, of which 7 were waited for; matrix products, arithmetic and copies ran while one was open for 0% of the time, Pallas kernels for 18%

profile of v3, /device:TPU:0, one launch (start us, length us, event | category | flops | bytes accessed | tf_op | source)
XLA Modules:
  0.0 66.7 jit_solution(14402015961994370244)
XLA Ops:
  0.6 0.5 collective-permute-start.1
  1.1 2.6 %collective-permute-start = (bf16[16,1,128,128]{3,2,1,0:T(8,128)(2,1)}, bf16[16,1,128,128]{3,2,1,0:T(8,128)(2,1)S(1)}, u32[]{:S(2)}, u32[]{:S(2)}) collective-permute-start(bf16[16,1,128,128]{3,2,1,0:T(8,128)(2,1)} %own.1), channel_id=1, source_target_pairs={{0,8},{4,12},{8,0},{12,4},{1,9},{5,13},{9,1},{13,5},{2,10},{6,14},... | collective-permute-start | bytes 1572872 | tf_op jit(solution)/shard_map/ppermute | solution.py:321
  3.7 0.0 collective-permute-done.1.twin.refs_3_
  3.7 0.0 copy-start
  3.7 1.6 %copy-done = bf16[512,2048]{1,0:T(8,128)(2,1)S(1)} copy-done((bf16[512,2048]{1,0:T(8,128)(2,1)S(1)}, bf16[512,2048]{1,0:T(8,128)(2,1)}, u32[]{:S(2)}) %copy-start) | copy-done | bytes 2097176
  5.3 0.0 copy-start.1
  5.3 1.0 %copy-done.1 = bf16[16,1,128,128]{3,2,1,0:T(8,128)(2,1)S(1)} copy-done((bf16[16,1,128,128]{3,2,1,0:T(8,128)(2,1)S(1)}, bf16[16,1,128,128]{3,2,1,0:T(8,128)(2,1)}, u32[]{:S(2)}) %copy-start.1) | copy-done | bytes 524312
  6.4 0.0 copy-start.2
  6.4 0.7 %copy-done.2 = s32[16,4]{0,1:T(4,128)S(1)} copy-done((s32[16,4]{0,1:T(4,128)S(1)}, s32[16,4]{0,1:T(4,128)}, u32[]{:S(2)}) %copy-start.2) | copy-done | bytes 280
  7.1 0.0 copy-start.3
  7.1 0.7 copy-done.3
  7.7 4.5 %shard_map.59 = (s32[288]{0:T(512)S(1)}, bf16[512,2048]{1,0:T(8,128)(2,1)S(1)}, bf16[16,1,128,128]{3,2,1,0:T(8,128)(2,1)S(1)}, f32[512,512]{1,0:T(8,128)S(1)}) custom-call(s32[4,16]{1,0:T(4,128)S(1)} %bitcast.1, s32[16]{0:T(128)S(1)} %copy-done.3, bf16[512,2048]{1,0:T(8,128)(2,1)S(1)} %copy-done, bf16[16,1,128,128]{3,2,1,0:T(8,128)(2,1)S(1)} %copy-done.1, ...), custom_call_target="tpu_custom_call" | custom-call | flops 268435456 | bytes 6817216 | tf_op jit(solution)/shard_map/pallas_call | solution.py:284
  12.2 4.3 %collective-permute-done.refs_4_.held = bf16[16,1,128,128]{3,2,1,0:T(8,128)(2,1)S(1)} collective-permute-done((bf16[16,1,128,128]{3,2,1,0:T(8,128)(2,1)}, bf16[16,1,128,128]{3,2,1,0:T(8,128)(2,1)S(1)}, u32[]{:S(2)}, u32[]{:S(2)}) %collective-permute-start) | collective-permute-done | bytes 524320 | tf_op jit(solution)/shard_map/ppermute | solution.py:321
  16.5 0.0 collective-permute-start.2
  16.5 0.9 %shard_map.61.total = f32[512,512]{1,0:T(8,128)S(1)} custom-call(s32[288]{0:T(512)S(1)} %get-tuple-element.19.refs_0_.plan_ref, bf16[512,2048]{1,0:T(8,128)(2,1)S(1)} %get-tuple-element.20.refs_1_.operand, bf16[16,1,128,128]{3,2,1,0:T(8,128)(2,1)S(1)} %collective-permute-done.refs_4_.held, ...), custom_call_target="tpu_custom_call", output_to_operand_aliasing={{}: (3, {})} | custom-call | flops 134217728 | bytes 4719744 | tf_op jit(solution)/shard_map/pallas_call | solution.py:284
  17.3 1.0 %collective-permute-done.2.refs_5_.held = bf16[16,1,128,128]{3,2,1,0:T(8,128)(2,1)S(1)} collective-permute-done((bf16[16,1,128,128]{3,2,1,0:T(8,128)(2,1)S(1)}, bf16[16,1,128,128]{3,2,1,0:T(8,128)(2,1)S(1)}, u32[]{:S(2)}, u32[]{:S(2)}) %collective-permute-start.2) | collective-permute-done | bytes 524320 | tf_op jit(solution)/shard_map/ppermute | solution.py:340
  18.4 1.5 %shard_map.62 = s16[528,512]{1,0:T(8,128)(2,1)S(1)} custom-call(s32[288]{0:T(512)S(1)} %get-tuple-element.19.refs_0_.plan_ref, bf16[512,2048]{1,0:T(8,128)(2,1)S(1)} %get-tuple-element.20.refs_1_.operand, bf16[16,1,128,128]{3,2,1,0:T(8,128)(2,1)S(1)} %collective-permute-done.2.refs_5_.held, f32[512,512]{1,0:T(8,128)S(1)} %shard_map.61.total), custom_call_target="tpu_custom_call" | custom-call | flops 134217728 | bytes 4211840 | tf_op jit(solution)/shard_map/pallas_call | solution.py:284
  19.9 1.6 %collective-permute-start.5 = (s16[528,512]{1,0:T(8,128)(2,1)S(1)}, s16[528,512]{1,0:T(8,128)(2,1)S(1)}, u32[]{:S(2)}, u32[]{:S(2)}) collective-permute-start(s16[528,512]{1,0:T(8,128)(2,1)S(1)} %shard_map.62), channel_id=1, source_target_pairs={{0,1},{1,0},{2,3},{3,2},{4,5},{5,4},{6,7},{7,6},{8,9},{9,8},{10,11... | collective-permute-start | bytes 1622024 | tf_op jit(solution)/shard_map/ppermute | solution.py:361
  21.5 0.2 collective-permute-start.3
  21.7 6.1 %shard_map.60 = (s16[528,512]{1,0:T(8,128)(2,1)S(1)}, f32[512,512]{1,0:T(8,128)S(1)}, f32[512,512]{1,0:T(8,128)S(1)}, s32[8,512]{1,0:T(8,128)S(1)}, s32[8,512]{1,0:T(8,128)S(1)}) custom-call(s32[288]{0:T(512)S(1)} %get-tuple-element.19.refs_0_.plan_ref, bf16[512,2048]{1,0:T(8,128)(2,1)S(1)} %get-tuple-element.20.refs_1_.operand, ...), custom_call_target="tpu_custom_call" | custom-call | flops 3221225472 | bytes 6866048 | tf_op jit(solution)/shard_map/pallas_call | solution.py:284
  27.7 2.8 %collective-permute-start.4 = (s16[528,512]{1,0:T(8,128)(2,1)S(1)}, s16[528,512]{1,0:T(8,128)(2,1)S(1)}, u32[]{:S(2)}, u32[]{:S(2)}) collective-permute-start(s16[528,512]{1,0:T(8,128)(2,1)S(1)} %get-tuple-element.26), channel_id=1, source_target_pairs={{0,2},{1,0},{2,3},{3,1},{4,6},{5,4},{6,7},{7,5},{8,10},{9,8},{10,1... | collective-permute-start | bytes 1622024 | tf_op jit(solution)/shard_map/ppermute | solution.py:376
  30.5 4.6 %collective-permute-done.5.came = s16[528,512]{1,0:T(8,128)(2,1)S(1)} collective-permute-done((s16[528,512]{1,0:T(8,128)(2,1)S(1)}, s16[528,512]{1,0:T(8,128)(2,1)S(1)}, u32[]{:S(2)}, u32[]{:S(2)}) %collective-permute-start.5) | collective-permute-done | bytes 540704 | tf_op jit(solution)/shard_map/ppermute | solution.py:361
  35.1 0.4 shard_map.64
  35.5 1.6 %collective-permute-start.6 = (s16[528,512]{1,0:T(8,128)(2,1)S(1)}, s16[528,512]{1,0:T(8,128)(2,1)S(1)}, u32[]{:S(2)}, u32[]{:S(2)}) collective-permute-start(s16[528,512]{1,0:T(8,128)(2,1)S(1)} %shard_map.64), channel_id=1, source_target_pairs={{0,1},{1,3},{3,2},{2,0},{4,5},{5,7},{7,6},{6,4},{8,9},{9,11},{11,1... | collective-permute-start | bytes 1622024 | tf_op jit(solution)/shard_map/ppermute | solution.py:378
  37.1 8.9 %collective-permute-done.4.came_f = s16[528,512]{1,0:T(8,128)(2,1)S(1)} collective-permute-done((s16[528,512]{1,0:T(8,128)(2,1)S(1)}, s16[528,512]{1,0:T(8,128)(2,1)S(1)}, u32[]{:S(2)}, u32[]{:S(2)}) %collective-permute-start.4) | collective-permute-done | bytes 540704 | tf_op jit(solution)/shard_map/ppermute | solution.py:376
  46.0 0.0 collective-permute-done.3.came_b
  46.0 0.2 shard_map.63
  46.1 13.4 %collective-permute-done.6.came = s16[528,512]{1,0:T(8,128)(2,1)S(1)} collective-permute-done((s16[528,512]{1,0:T(8,128)(2,1)S(1)}, s16[528,512]{1,0:T(8,128)(2,1)S(1)}, u32[]{:S(2)}, u32[]{:S(2)}) %collective-permute-start.6) | collective-permute-done | bytes 540704 | tf_op jit(solution)/shard_map/ppermute | solution.py:378
  59.5 0.9 %shard_map.65 = (f32[512,512]{1,0:T(8,128)S(1)}, f32[8,512]{1,0:T(8,128)S(1)}, s32[4]{0:T(128)}) custom-call(f32[512,512]{1,0:T(8,128)S(1)} %get-tuple-element.27.own, s32[8,512]{1,0:T(8,128)S(1)} %get-tuple-element.28.own_load, s16[528,512]{1,0:T(8,128)(2,1)S(1)} %collective-permute-done.6.came), custom_call_target="tpu_custom_call" | custom-call | bytes 2670608 | tf_op jit(solution)/shard_map/pallas_call | solution.py:284
  60.4 1.4 %collective-permute-start.9 = (f32[8,512]{1,0:T(8,128)S(1)}, f32[8,512]{1,0:T(8,128)S(1)}, u32[]{:S(2)}, u32[]{:S(2)}) collective-permute-start(f32[8,512]{1,0:T(8,128)S(1)} %get-tuple-element.32.refs_0_), channel_id=1, source_target_pairs={{0,12},{4,8},{8,4},{12,0},{1,13},{5,9},{9,5},{13,1},{2,14},{6,10},... | collective-permute-start | bytes 49160 | tf_op jit(solution)/shard_map/ppermute | solution.py:390
  61.9 0.5 collective-permute-start.8
  62.3 0.1 collective-permute-start.7
  62.4 1.3 %collective-permute-done.9.refs_3_ = f32[8,512]{1,0:T(8,128)S(1)} collective-permute-done((f32[8,512]{1,0:T(8,128)S(1)}, f32[8,512]{1,0:T(8,128)S(1)}, u32[]{:S(2)}, u32[]{:S(2)}) %collective-permute-start.9) | collective-permute-done | bytes 16416 | tf_op jit(solution)/shard_map/ppermute | solution.py:390
  63.7 2.0 %collective-permute-done.8.refs_2_ = f32[8,512]{1,0:T(8,128)S(1)} collective-permute-done((f32[8,512]{1,0:T(8,128)S(1)}, f32[8,512]{1,0:T(8,128)S(1)}, u32[]{:S(2)}, u32[]{:S(2)}) %collective-permute-start.8) | collective-permute-done | bytes 16416 | tf_op jit(solution)/shard_map/ppermute | solution.py:390
  65.6 0.0 collective-permute-done.7.refs_1_
  65.6 1.1 %shard_map.66 = f32[512,512]{1,0:T(8,128)} custom-call(f32[512,512]{1,0:T(8,128)S(1)} %get-tuple-element.31.inflated, f32[8,512]{1,0:T(8,128)S(1)} %get-tuple-element.32.refs_0_, f32[8,512]{1,0:T(8,128)S(1)} %collective-permute-done.7.refs_1_, f32[8,512]{1,0:T(8,128)S(1)} %collective-permute-done.8.refs_2_, f32[8,512]{1,0:T(8,128)S(1)} %collective-permute-done.9.refs_3_), custom_call_target="tpu_custom_call" | custom-call | bytes 2162688 | tf_op jit(solution)/shard_map/pallas_call | solution.py:284
Async XLA Ops:
  0.6 3.1 %collective-permute-start.1 = (bf16[16,1,128,128]{3,2,1,0:T(8,128)(2,1)}, bf16[16,1,128,128]{3,2,1,0:T(8,128)(2,1)S(1)}, u32[]{:S(2)}, u32[]{:S(2)}) collective-permute-start(bf16[16,1,128,128]{3,2,1,0:T(8,128)(2,1)} %own.1), channel_id=1, source_target_pairs={{0,4},{4,0},{8,12},{12,8},{1,5},{5,1},{9,13},{13,9},{2,6},{6,2},{1... | collective-permute-start | bytes 1572872 | tf_op jit(solution)/shard_map/ppermute | solution.py:322
  1.1 15.3 %collective-permute-start = (bf16[16,1,128,128]{3,2,1,0:T(8,128)(2,1)}, bf16[16,1,128,128]{3,2,1,0:T(8,128)(2,1)S(1)}, u32[]{:S(2)}, u32[]{:S(2)}) collective-permute-start(bf16[16,1,128,128]{3,2,1,0:T(8,128)(2,1)} %own.1), channel_id=1, source_target_pairs={{0,8},{4,12},{8,0},{12,4},{1,9},{5,13},{9,1},{13,5},{2,10},{6,14},... | collective-permute-start | bytes 1572872 | tf_op jit(solution)/shard_map/ppermute | solution.py:321
  3.7 1.6 %copy-start = (bf16[512,2048]{1,0:T(8,128)(2,1)S(1)}, bf16[512,2048]{1,0:T(8,128)(2,1)}, u32[]{:S(2)}) copy-start(bf16[512,2048]{1,0:T(8,128)(2,1)} %operand.1) | copy-start | bytes 6291460
  5.3 1.0 %copy-start.1 = (bf16[16,1,128,128]{3,2,1,0:T(8,128)(2,1)S(1)}, bf16[16,1,128,128]{3,2,1,0:T(8,128)(2,1)}, u32[]{:S(2)}) copy-start(bf16[16,1,128,128]{3,2,1,0:T(8,128)(2,1)} %own.1) | copy-start | bytes 1572868
  6.4 0.7 %copy-start.2 = (s32[16,4]{0,1:T(4,128)S(1)}, s32[16,4]{0,1:T(4,128)}, u32[]{:S(2)}) copy-start(s32[16,4]{0,1:T(4,128)} %param.6) | copy-start | bytes 772
  7.1 0.7 copy-start.3
  16.5 1.9 %collective-permute-start.2 = (bf16[16,1,128,128]{3,2,1,0:T(8,128)(2,1)S(1)}, bf16[16,1,128,128]{3,2,1,0:T(8,128)(2,1)S(1)}, u32[]{:S(2)}, u32[]{:S(2)}) collective-permute-start(bf16[16,1,128,128]{3,2,1,0:T(8,128)(2,1)S(1)} %collective-permute-done.refs_4_.held), channel_id=1, source_target_pairs={{0,4},{4,0},{8,12},{12,8},{1,5},{5,1},{9,13},{13,9},{2,6},{6,2},{1... | collective-permute-start | bytes 1572872 | tf_op jit(solution)/shard_map/ppermute | solution.py:340
  19.9 15.2 %collective-permute-start.5 = (s16[528,512]{1,0:T(8,128)(2,1)S(1)}, s16[528,512]{1,0:T(8,128)(2,1)S(1)}, u32[]{:S(2)}, u32[]{:S(2)}) collective-permute-start(s16[528,512]{1,0:T(8,128)(2,1)S(1)} %shard_map.62), channel_id=1, source_target_pairs={{0,1},{1,0},{2,3},{3,2},{4,5},{5,4},{6,7},{7,6},{8,9},{9,8},{10,11... | collective-permute-start | bytes 1622024 | tf_op jit(solution)/shard_map/ppermute | solution.py:361
  21.5 24.5 %collective-permute-start.3 = (s16[528,512]{1,0:T(8,128)(2,1)S(1)}, s16[528,512]{1,0:T(8,128)(2,1)S(1)}, u32[]{:S(2)}, u32[]{:S(2)}) collective-permute-start(s16[528,512]{1,0:T(8,128)(2,1)S(1)} %shard_map.62), channel_id=1, source_target_pairs={{0,4},{1,2},{2,1},{3,7},{4,0},{5,6},{6,5},{7,3},{8,12},{9,10},{10,... | collective-permute-start | bytes 1622024 | tf_op jit(solution)/shard_map/ppermute | solution.py:362
  27.7 18.2 %collective-permute-start.4 = (s16[528,512]{1,0:T(8,128)(2,1)S(1)}, s16[528,512]{1,0:T(8,128)(2,1)S(1)}, u32[]{:S(2)}, u32[]{:S(2)}) collective-permute-start(s16[528,512]{1,0:T(8,128)(2,1)S(1)} %get-tuple-element.26), channel_id=1, source_target_pairs={{0,2},{1,0},{2,3},{3,1},{4,6},{5,4},{6,7},{7,5},{8,10},{9,8},{10,1... | collective-permute-start | bytes 1622024 | tf_op jit(solution)/shard_map/ppermute | solution.py:376
  35.5 24.0 %collective-permute-start.6 = (s16[528,512]{1,0:T(8,128)(2,1)S(1)}, s16[528,512]{1,0:T(8,128)(2,1)S(1)}, u32[]{:S(2)}, u32[]{:S(2)}) collective-permute-start(s16[528,512]{1,0:T(8,128)(2,1)S(1)} %shard_map.64), channel_id=1, source_target_pairs={{0,1},{1,3},{3,2},{2,0},{4,5},{5,7},{7,6},{6,4},{8,9},{9,11},{11,1... | collective-permute-start | bytes 1622024 | tf_op jit(solution)/shard_map/ppermute | solution.py:378
  60.4 3.2 %collective-permute-start.9 = (f32[8,512]{1,0:T(8,128)S(1)}, f32[8,512]{1,0:T(8,128)S(1)}, u32[]{:S(2)}, u32[]{:S(2)}) collective-permute-start(f32[8,512]{1,0:T(8,128)S(1)} %get-tuple-element.32.refs_0_), channel_id=1, source_target_pairs={{0,12},{4,8},{8,4},{12,0},{1,13},{5,9},{9,5},{13,1},{2,14},{6,10},... | collective-permute-start | bytes 49160 | tf_op jit(solution)/shard_map/ppermute | solution.py:390
  61.9 3.7 %collective-permute-start.8 = (f32[8,512]{1,0:T(8,128)S(1)}, f32[8,512]{1,0:T(8,128)S(1)}, u32[]{:S(2)}, u32[]{:S(2)}) collective-permute-start(f32[8,512]{1,0:T(8,128)S(1)} %get-tuple-element.32.refs_0_), channel_id=1, source_target_pairs={{0,8},{4,12},{8,0},{12,4},{1,9},{5,13},{9,1},{13,5},{2,10},{6,14},... | collective-permute-start | bytes 49160 | tf_op jit(solution)/shard_map/ppermute | solution.py:390
  62.3 3.3 %collective-permute-start.7 = (f32[8,512]{1,0:T(8,128)S(1)}, f32[8,512]{1,0:T(8,128)S(1)}, u32[]{:S(2)}, u32[]{:S(2)}) collective-permute-start(f32[8,512]{1,0:T(8,128)S(1)} %get-tuple-element.32.refs_0_), channel_id=1, source_target_pairs={{0,4},{4,0},{8,12},{12,8},{1,5},{5,1},{9,13},{13,9},{2,6},{6,2},{1... | collective-permute-start | bytes 49160 | tf_op jit(solution)/shard_map/ppermute | solution.py:390

commit v4 on v3

--- a/solution.py
+++ b/solution.py
@@ -11,6 +11,9 @@
 SIDE = 128
 HEAD = 16
 TILE = 256
+ABREAST = 4
+PARTS = 2
+COST = 1
 STEPS = 32700.0
 NEAREST = 12582912.0
 OCTAVE = 128.0
@@ -30,17 +33,18 @@
     return ((scaled + NEAREST) - NEAREST).astype(jnp.int32).astype(jnp.int16)
 
 
-def head_rows(code, counts):
+def head_rows(code, *counts):
     shape = (HEAD, code.shape[1])
     row = lax.broadcasted_iota(jnp.int32, shape, 0)
-    code = jnp.broadcast_to(code.astype(jnp.int32), shape)
-    counts = jnp.broadcast_to(counts, shape)
-    return jnp.where(row == 0, code, jnp.where(row == 1, counts, 0)).astype(jnp.int16)
-
-
-def put_coded(out, lanes, values, counts):
+    head = jnp.broadcast_to(code.astype(jnp.int32), shape)
+    for j, one in enumerate(counts):
+        head = jnp.where(row > j, jnp.broadcast_to(one, shape), head)
+    return head.astype(jnp.int16)
+
+
+def put_coded(out, lanes, values, *counts):
     code = code_scale(values)
-    out[pl.ds(0, HEAD), lanes] = head_rows(code, counts)
+    out[pl.ds(0, HEAD), lanes] = head_rows(code, *counts)
     out[pl.ds(HEAD, values.shape[0]), lanes] = encode(values, code)
 
 
@@ -51,8 +55,8 @@
     return ref[pl.ds(HEAD, rows), lanes].astype(jnp.int32).astype(jnp.float32) * scale
 
 
-def head_counts(ref, lanes):
-    return ref[pl.ds(0, HEAD), lanes].astype(jnp.int32)[1:2]
+def head_counts(ref, lanes, part=0):
+    return ref[pl.ds(0, HEAD), lanes].astype(jnp.int32)[1 + part : 2 + part]
 
 
 def slot_of(place, ny):
@@ -141,12 +145,12 @@
         lanes = pl.ds(pl.multiple_of(column * SIDE, SIDE), SIDE)
         return lanes, jnp.dot(left, block, preferred_element_type=jnp.float32)
 
-    def step(pair, carry):
-        for lanes, value in [term(2 * pair), term(2 * pair + 1)]:
+    def step(some, carry):
+        for lanes, value in [term(ABREAST * some + j) for j in range(ABREAST)]:
             total[:, lanes] = total[:, lanes] + value
         return carry
 
-    lax.fori_loop(0, lax.div(length + 1, 2), step, 0)
+    lax.fori_loop(0, lax.div(length + ABREAST - 1, ABREAST), step, 0)
 
 
 def go_on(which, place, plan_ref, operand, held, _, total):
@@ -221,20 +225,26 @@
         one_shard(which, put)
 
 
-def relay(own, own_load, came, out):
+def relay(own, own_load, came, *outs):
     place = lax.axis_index("col")
     inner = (place == 1) | (place == 2)
-
-    def body(tile, lanes):
-        @pl.when(inner)
-        def _():
-            put_coded(out, lanes, own[:, lanes] + decode(came, lanes), own_load[0:1, lanes] + head_counts(came, lanes))
-
-        @pl.when(jnp.logical_not(inner))
-        def _():
-            put_coded(out, lanes, own[:, lanes], own_load[0:1, lanes])
-
-    tiles(own.shape[1], body)
+    width = outs[0].shape[1]
+    for part, out in enumerate(outs):
+
+        def body(tile, lanes, part=part, out=out):
+            ats = [pl.ds(pl.multiple_of(j * width + tile * TILE, TILE), TILE) for j in range(len(outs))]
+            at = ats[part]
+
+            @pl.when(inner)
+            def _():
+                counts = [own_load[0:1, one] + head_counts(came, one) for one in ats]
+                put_coded(out, lanes, own[:, at] + decode(came, at), *counts)
+
+            @pl.when(jnp.logical_not(inner))
+            def _():
+                put_coded(out, lanes, own[:, at], *[own_load[0:1, one] for one in ats])
+
+        tiles(width, body)
 
 
 def settle(own, own_load, came_b, came_f, out, out_load):
@@ -253,43 +263,57 @@
     tiles(own.shape[1], body)
 
 
-def inflate(own, own_load, came, out, totals, load):
+def inflate(part, own, came, out, totals):
+    width = out.shape[1]
+
     def body(tile, lanes):
-        expanded = own[:, lanes] + decode(came, lanes)
+        at = pl.ds(pl.multiple_of(part * width + tile * TILE, TILE), TILE)
+        expanded = own[:, at] + decode(came, lanes)
         inflated = expanded * expanded
         out[:, lanes] = inflated
         totals[:, lanes] = jnp.sum(inflated.reshape(-1, 8, TILE), axis=0)
 
-    tiles(own.shape[1], body)
+    tiles(width, body)
+
+
+def count(own_load, came, load):
+    width = came.shape[1]
     for j in range(SLAB_DEV):
-        lanes = pl.ds(j * SIDE, SIDE)
-        load[j] = jnp.max(own_load[0:1, lanes] + head_counts(came, lanes))
-
-
-def scale(all_rows, inflated, *refs):
-    *totals, out = refs
-
-    def body(tile, lanes):
-        total = totals[0][:, lanes]
-        for other in totals[1:]:
-            total = total + other[:, lanes]
-        total = jnp.sum(total, axis=0, keepdims=True)
-        out[:, lanes] = inflated[:, lanes] * (1.0 / (total / all_rows + 1e-06))
-
-    tiles(inflated.shape[1], body)
-
-
-def call(kernel, ins, out_shape, out_specs, scratch=(), flops=0, few=0, far=0, onto=None):
+        lanes, at = pl.ds(j * SIDE % width, SIDE), pl.ds(j * SIDE, SIDE)
+        load[j] = jnp.max(own_load[0:1, at] + head_counts(came, lanes, j * SIDE // width))
+
+
+def scale(all_rows, part, inflated, *refs):
+    *totals, out, scaled, sems = refs[:-4] + refs[-3:] if part else refs
+    rows, width = inflated.shape
+    total = totals[0][...]
+    for other in totals[1:]:
+        total = total + other[...]
+    total = jnp.sum(total, axis=0, keepdims=True)
+    factor = 1.0 / (total / all_rows + 1e-06)
+    few = rows // sems.shape[0]
+    copies = []
+    for j in range(sems.shape[0]):
+        these = pl.ds(j * few, few)
+        scaled[these, :] = inflated[these, :] * factor
+        copy = pltpu.make_async_copy(scaled.at[these, :], out.at[these, pl.ds(part * width, width)], sems.at[j])
+        copy.start()
+        copies.append(copy)
+    for copy in copies:
+        copy.wait()
+
+
+def call(kernel, ins, out_shape, out_specs, scratch=(), flops=0, few=0, far=0, onto=None, last=False):
     moved = sum(x.size * x.dtype.itemsize for x in list(ins) + list(out_shape))
     return pl.pallas_call(
         kernel,
-        in_specs=[SMEM] * few + [pl.BlockSpec(memory_space=pltpu.HBM)] * far + [VMEM] * (len(ins) - few - far),
+        in_specs=[SMEM] * few + [pl.BlockSpec(memory_space=pltpu.HBM)] * far + [VMEM] * (len(ins) - few - far - last) + [pl.BlockSpec(memory_space=pl.ANY)] * last,
         out_shape=out_shape,
         out_specs=out_specs,
         scratch_shapes=list(scratch),
         input_output_aliases=onto or {},
         compiler_params=pltpu.CompilerParams(vmem_limit_bytes=24 << 20),
-        cost_estimate=pl.CostEstimate(flops=flops, bytes_accessed=moved, transcendentals=0),
+        cost_estimate=pl.CostEstimate(flops=flops // COST, bytes_accessed=moved // COST, transcendentals=0),
     )(*ins)
 
 
@@ -374,23 +398,40 @@
         1,
     )
     came_f = lax.ppermute(send_f, "col", [(0, 2), (1, 0), (2, 3), (3, 1)])
-    [send_t] = call(relay, [passed, passed_load, came_a], [coded], [VMEM])
-    came_t = lax.ppermute(send_t, "col", [(0, 1), (1, 3), (3, 2), (2, 0)])
+    came_a, came_b = lax.optimization_barrier((came_a, came_b))
+    sent = jax.ShapeDtypeStruct((HEAD + rows, width // PARTS), jnp.int16)
+    send_t = call(relay, [passed, passed_load, came_a], [sent] * PARTS, [VMEM] * PARTS)
+    came_t = [lax.ppermute(one, "col", [(0, 1), (1, 3), (3, 2), (2, 0)]) for one in send_t]
     own, own_load = call(
         settle, [own, own_load, came_b, came_f], [f32((rows, width)), i32((8, width))], [VMEM] * 2
     )
-    inflated, totals, load = call(
-        inflate, [own, own_load, came_t], [f32((rows, width)), f32((8, width)), i32((SLAB_DEV,))], [VMEM, VMEM, SMEM]
-    )
-    others = [totals]
-    for by in range(ny):
-        for flip in (0, 1):
-            if by or flip:
-                pairs = [(a, ((a // 2 + by) % ny) * 2 + (a % 2 ^ flip)) for a in range(2 * ny)]
-                others.append(lax.ppermute(totals, "row", pairs))
     all_rows = rows * lax.axis_size("row")
-    [mcl_columns] = call(functools.partial(scale, all_rows), [inflated, *others], [f32((rows, width))], [VMEM])
-    return mcl_columns, load
+    hbm = pl.BlockSpec(memory_space=pl.ANY)
+    result = []
+    [load] = call(count, [own_load, came_t[0]], [i32((SLAB_DEV,))], [SMEM])
+    for part in range(PARTS):
+        inflated, totals = call(
+            functools.partial(inflate, part),
+            [own, came_t[part]],
+            [f32((rows, width // PARTS)), f32((8, width // PARTS))],
+            [VMEM] * 2,
+        )
+        others = [totals]
+        for by in range(ny):
+            for flip in (0, 1):
+                if by or flip:
+                    pairs = [(a, ((a // 2 + by) % ny) * 2 + (a % 2 ^ flip)) for a in range(2 * ny)]
+                    others.append(lax.ppermute(totals, "row", pairs))
+        result = call(
+            functools.partial(scale, all_rows, part),
+            [inflated, *others, *result],
+            [f32((rows, width))],
+            [hbm],
+            [pltpu.VMEM((rows, width // PARTS), jnp.float32), pltpu.SemaphoreType.DMA((4,))],
+            onto={1 + len(others): 0} if part else None,
+            last=bool(part),
+        )
+    return result[0], load
 
 
 def densify(blocks, columns, counts, first_row, slab_width):

time: 67 us -> 66.1 us (0.987)
  waiting for transfers between devices: 35.3 us -> 30.9 us
  starting transfers between devices: 11.2 us -> 14.9 us
    ppermute x1 -> x2, waiting for transfers between devices: 13.4 us -> 9.33 us  [body_line(): lax.ppermute(one, 'col', [(0, 1), (1, 3), (3, 2), (2, 0)])]
    ppermute x3 -> x6, starting transfers between devices: 1.96 us -> 4.28 us  [body_line(): others.append(lax.ppermute(totals, 'row', pairs))]
    ppermute x1, starting transfers between devices: 1.59 us -> 3.69 us  [body_line(): came_a = lax.ppermute(send_a, 'col', [(0, 1), (1, 0), (2, 3), (3, 2)])]
    ppermute x1, starting transfers between devices: 2.78 us -> 0.95 us  [body_line(): came_f = lax.ppermute(send_f, 'col', [(0, 2), (1, 0), (2, 3), (3, 1)])]
    ppermute x3 -> x6, waiting for transfers between devices: 3.22 us -> 1.55 us  [body_line(): others.append(lax.ppermute(totals, 'row', pairs))]
    ppermute x1, waiting for transfers between devices: 4.57 us -> 6.19 us  [body_line(): came_a = lax.ppermute(send_a, 'col', [(0, 1), (1, 0), (2, 3), (3, 2)])]
    ppermute x1 -> x2, starting transfers between devices: 1.64 us -> 2.71 us  [body_line(): lax.ppermute(one, 'col', [(0, 1), (1, 3), (3, 2), (2, 0)])]
    ppermute x1, waiting for transfers between devices: 8.86 us -> 8.13 us  [body_line(): came_f = lax.ppermute(send_f, 'col', [(0, 2), (1, 0), (2, 3), (3, 1)])]
  transfers between devices with their start and end apart: 10 -> 14, of which waited for: 7 -> 7; matrix products, arithmetic and copies ran while one was open for 0% -> 0% of each run, Pallas kernels for 18% -> 20%
where the time goes in v4:
time: 66.1 us; the launch traced here: 66 us
  waiting for transfers between devices  30.9 us (47%)
  Pallas kernels  15.5 us (23%)
  starting transfers between devices  14.9 us (23%)
  local copies, waits for them, and re-layouts  3.97 us (6%)
  between operations  0.74 us (1%)
    pallas_call x11, Pallas kernels, call(): pl.pallas_call(kernel, in_specs=[SMEM] * few + [pl.BlockSpec(memory_space...  15.5 us
    ppermute x2, waiting for transfers between devices, body_line(): lax.ppermute(one, 'col', [(0, 1), (1, 3), (3, 2), (2, 0)])  9.33 us
    ppermute x1, waiting for transfers between devices, body_line(): came_f = lax.ppermute(send_f, 'col', [(0, 2), (1, 0), (2, 3), (3, 1)])  8.13 us
    ppermute x1, waiting for transfers between devices, body_line(): came_a = lax.ppermute(send_a, 'col', [(0, 1), (1, 0), (2, 3), (3, 2)])  6.19 us
    ppermute x1, waiting for transfers between devices, body_line(): turned = [lax.ppermute(slot_blocks, 'row', turn(by)) for by in range(1, ny)]  4.86 us
    ppermute x6, starting transfers between devices, body_line(): others.append(lax.ppermute(totals, 'row', pairs))  4.28 us
    unnamed x8, local copies, waits for them, and re-layouts  3.97 us
    ppermute x1, starting transfers between devices, body_line(): came_a = lax.ppermute(send_a, 'col', [(0, 1), (1, 0), (2, 3), (3, 2)])  3.69 us
  transfers between devices with their start and end apart: 14, of which 7 were waited for; matrix products, arithmetic and copies ran while one was open for 0% of the time, Pallas kernels for 20%

profile of v4, /device:TPU:0, one launch (start us, length us, event | category | flops | bytes accessed | tf_op | source)
XLA Modules:
  0.0 66.0 jit_solution(6417079223828599807)
XLA Ops:
  0.6 0.5 collective-permute-start.1
  1.1 2.6 %collective-permute-start = (bf16[16,1,128,128]{3,2,1,0:T(8,128)(2,1)}, bf16[16,1,128,128]{3,2,1,0:T(8,128)(2,1)S(1)}, u32[]{:S(2)}, u32[]{:S(2)}) collective-permute-start(bf16[16,1,128,128]{3,2,1,0:T(8,128)(2,1)} %own.1), channel_id=1, source_target_pairs={{0,8},{4,12},{8,0},{12,4},{1,9},{5,13},{9,1},{13,5},{2,10},{6,14},... | collective-permute-start | bytes 1572872 | tf_op jit(solution)/shard_map/ppermute | solution.py:345
  3.7 0.0 collective-permute-done.1.twin.refs_3_
  3.7 0.0 copy-start
  3.7 1.6 %copy-done = bf16[512,2048]{1,0:T(8,128)(2,1)S(1)} copy-done((bf16[512,2048]{1,0:T(8,128)(2,1)S(1)}, bf16[512,2048]{1,0:T(8,128)(2,1)}, u32[]{:S(2)}) %copy-start) | copy-done | bytes 2097176
  5.3 0.0 copy-start.1
  5.3 1.0 %copy-done.1 = bf16[16,1,128,128]{3,2,1,0:T(8,128)(2,1)S(1)} copy-done((bf16[16,1,128,128]{3,2,1,0:T(8,128)(2,1)S(1)}, bf16[16,1,128,128]{3,2,1,0:T(8,128)(2,1)}, u32[]{:S(2)}) %copy-start.1) | copy-done | bytes 524312
  6.4 0.0 copy-start.2
  6.4 0.7 %copy-done.2 = s32[16,4]{0,1:T(4,128)S(1)} copy-done((s32[16,4]{0,1:T(4,128)S(1)}, s32[16,4]{0,1:T(4,128)}, u32[]{:S(2)}) %copy-start.2) | copy-done | bytes 280
  7.1 0.0 copy-start.3
  7.1 0.7 copy-done.3
  7.7 3.9 %shard_map.59 = (s32[288]{0:T(512)S(1)}, bf16[512,2048]{1,0:T(8,128)(2,1)S(1)}, bf16[16,1,128,128]{3,2,1,0:T(8,128)(2,1)S(1)}, f32[512,512]{1,0:T(8,128)S(1)}) custom-call(s32[4,16]{1,0:T(4,128)S(1)} %bitcast.1, s32[16]{0:T(128)S(1)} %copy-done.3, bf16[512,2048]{1,0:T(8,128)(2,1)S(1)} %copy-done, bf16[16,1,128,128]{3,2,1,0:T(8,128)(2,1)S(1)} %copy-done.1, ...), custom_call_target="tpu_custom_call" | custom-call | flops 268435456 | bytes 6817216 | tf_op jit(solution)/shard_map/pallas_call | solution.py:308
  11.6 4.9 %collective-permute-done.refs_4_.held = bf16[16,1,128,128]{3,2,1,0:T(8,128)(2,1)S(1)} collective-permute-done((bf16[16,1,128,128]{3,2,1,0:T(8,128)(2,1)}, bf16[16,1,128,128]{3,2,1,0:T(8,128)(2,1)S(1)}, u32[]{:S(2)}, u32[]{:S(2)}) %collective-permute-start) | collective-permute-done | bytes 524320 | tf_op jit(solution)/shard_map/ppermute | solution.py:345
  16.5 0.0 collective-permute-start.2
  16.5 1.0 %shard_map.61.total = f32[512,512]{1,0:T(8,128)S(1)} custom-call(s32[288]{0:T(512)S(1)} %get-tuple-element.24.refs_0_.plan_ref, bf16[512,2048]{1,0:T(8,128)(2,1)S(1)} %get-tuple-element.25.refs_1_.operand, bf16[16,1,128,128]{3,2,1,0:T(8,128)(2,1)S(1)} %collective-permute-done.refs_4_.held, ...), custom_call_target="tpu_custom_call", output_to_operand_aliasing={{}: (3, {})} | custom-call | flops 134217728 | bytes 4719744 | tf_op jit(solution)/shard_map/pallas_call | solution.py:308
  17.5 0.9 %collective-permute-done.2.refs_5_.held = bf16[16,1,128,128]{3,2,1,0:T(8,128)(2,1)S(1)} collective-permute-done((bf16[16,1,128,128]{3,2,1,0:T(8,128)(2,1)S(1)}, bf16[16,1,128,128]{3,2,1,0:T(8,128)(2,1)S(1)}, u32[]{:S(2)}, u32[]{:S(2)}) %collective-permute-start.2) | collective-permute-done | bytes 524320 | tf_op jit(solution)/shard_map/ppermute | solution.py:364
  18.4 1.4 %shard_map.62 = s16[528,512]{1,0:T(8,128)(2,1)S(1)} custom-call(s32[288]{0:T(512)S(1)} %get-tuple-element.24.refs_0_.plan_ref, bf16[512,2048]{1,0:T(8,128)(2,1)S(1)} %get-tuple-element.25.refs_1_.operand, bf16[16,1,128,128]{3,2,1,0:T(8,128)(2,1)S(1)} %collective-permute-done.2.refs_5_.held, f32[512,512]{1,0:T(8,128)S(1)} %shard_map.61.total), custom_call_target="tpu_custom_call" | custom-call | flops 134217728 | bytes 4211840 | tf_op jit(solution)/shard_map/pallas_call | solution.py:308
  19.8 0.2 collective-permute-start.4
  20.0 3.7 %collective-permute-start.3 = (s16[528,512]{1,0:T(8,128)(2,1)S(1)}, s16[528,512]{1,0:T(8,128)(2,1)S(1)}, u32[]{:S(2)}, u32[]{:S(2)}) collective-permute-start(s16[528,512]{1,0:T(8,128)(2,1)S(1)} %shard_map.62), channel_id=1, source_target_pairs={{0,1},{1,0},{2,3},{3,2},{4,5},{5,4},{6,7},{7,6},{8,9},{9,8},{10,11... | collective-permute-start | bytes 1622024 | tf_op jit(solution)/shard_map/ppermute | solution.py:385
  23.7 6.0 %shard_map.60 = (s16[528,512]{1,0:T(8,128)(2,1)S(1)}, f32[512,512]{1,0:T(8,128)S(1)}, f32[512,512]{1,0:T(8,128)S(1)}, s32[8,512]{1,0:T(8,128)S(1)}, s32[8,512]{1,0:T(8,128)S(1)}) custom-call(s32[288]{0:T(512)S(1)} %get-tuple-element.24.refs_0_.plan_ref, bf16[512,2048]{1,0:T(8,128)(2,1)S(1)} %get-tuple-element.25.refs_1_.operand, ...), custom_call_target="tpu_custom_call" | custom-call | flops 3221225472 | bytes 6866048 | tf_op jit(solution)/shard_map/pallas_call | solution.py:308
  29.7 0.9 %collective-permute-start.5 = (s16[528,512]{1,0:T(8,128)(2,1)S(1)}, s16[528,512]{1,0:T(8,128)(2,1)S(1)}, u32[]{:S(2)}, u32[]{:S(2)}) collective-permute-start(s16[528,512]{1,0:T(8,128)(2,1)S(1)} %get-tuple-element.32), channel_id=1, source_target_pairs={{0,2},{1,0},{2,3},{3,1},{4,6},{5,4},{6,7},{7,5},{8,10},{9,8},{10,1... | collective-permute-start | bytes 1622024 | tf_op jit(solution)/shard_map/ppermute | solution.py:400
  30.6 0.0 collective-permute-done.4.came_b
  30.6 6.2 %collective-permute-done.3.came = s16[528,512]{1,0:T(8,128)(2,1)S(1)} collective-permute-done((s16[528,512]{1,0:T(8,128)(2,1)S(1)}, s16[528,512]{1,0:T(8,128)(2,1)S(1)}, u32[]{:S(2)}, u32[]{:S(2)}) %collective-permute-start.3) | collective-permute-done | bytes 540704 | tf_op jit(solution)/shard_map/ppermute | solution.py:385
  36.8 0.4 shard_map.64
  37.2 2.2 %collective-permute-start.10 = (s16[528,256]{1,0:T(8,128)(2,1)S(1)}, s16[528,256]{1,0:T(8,128)(2,1)S(1)}, u32[]{:S(2)}, u32[]{:S(2)}) collective-permute-start(s16[528,256]{1,0:T(8,128)(2,1)S(1)} %get-tuple-element.40), channel_id=1, source_target_pairs={{0,1},{1,3},{3,2},{2,0},{4,5},{5,7},{7,6},{6,4},{8,9},{9,11},{11,1... | collective-permute-start | bytes 811016 | tf_op jit(solution)/shard_map/ppermute | solution.py:404
  39.4 0.5 collective-permute-start.6
  39.9 8.1 %collective-permute-done.5.came_f = s16[528,512]{1,0:T(8,128)(2,1)S(1)} collective-permute-done((s16[528,512]{1,0:T(8,128)(2,1)S(1)}, s16[528,512]{1,0:T(8,128)(2,1)S(1)}, u32[]{:S(2)}, u32[]{:S(2)}) %collective-permute-start.5) | collective-permute-done | bytes 540704 | tf_op jit(solution)/shard_map/ppermute | solution.py:400
  48.0 0.2 shard_map.63
  48.2 5.9 %collective-permute-done.10.came = s16[528,256]{1,0:T(8,128)(2,1)S(1)} collective-permute-done((s16[528,256]{1,0:T(8,128)(2,1)S(1)}, s16[528,256]{1,0:T(8,128)(2,1)S(1)}, u32[]{:S(2)}, u32[]{:S(2)}) %collective-permute-start.10) | collective-permute-done | bytes 270368 | tf_op jit(solution)/shard_map/ppermute | solution.py:404
  54.1 0.1 shard_map.66
  54.2 1.5 %collective-permute-start.13 = (f32[8,256]{1,0:T(8,128)S(1)}, f32[8,256]{1,0:T(8,128)S(1)}, u32[]{:S(2)}, u32[]{:S(2)}) collective-permute-start(f32[8,256]{1,0:T(8,128)S(1)} %get-tuple-element.42.refs_0_), channel_id=1, source_target_pairs={{0,12},{4,8},{8,4},{12,0},{1,13},{5,9},{9,5},{13,1},{2,14},{6,10},... | collective-permute-start | bytes 24584 | tf_op jit(solution)/shard_map/ppermute | solution.py:424
  55.8 0.6 collective-permute-start.12
  56.3 0.0 collective-permute-start.11
  56.3 3.4 %collective-permute-done.6.came = s16[528,256]{1,0:T(8,128)(2,1)S(1)} collective-permute-done((s16[528,256]{1,0:T(8,128)(2,1)S(1)}, s16[528,256]{1,0:T(8,128)(2,1)S(1)}, u32[]{:S(2)}, u32[]{:S(2)}) %collective-permute-start.6) | collective-permute-done | bytes 270368 | tf_op jit(solution)/shard_map/ppermute | solution.py:404
  59.8 0.1 shard_map.65
  59.9 1.6 %collective-permute-start.9 = (f32[8,256]{1,0:T(8,128)S(1)}, f32[8,256]{1,0:T(8,128)S(1)}, u32[]{:S(2)}, u32[]{:S(2)}) collective-permute-start(f32[8,256]{1,0:T(8,128)S(1)} %get-tuple-element.39.refs_0_), channel_id=1, source_target_pairs={{0,12},{4,8},{8,4},{12,0},{1,13},{5,9},{9,5},{13,1},{2,14},{6,10},... | collective-permute-start | bytes 24584 | tf_op jit(solution)/shard_map/ppermute | solution.py:424
  61.5 0.5 collective-permute-start.8
  62.0 0.0 collective-permute-done.13.refs_3_
  62.0 0.0 collective-permute-start.7
  62.0 0.7 %shard_map.69 = s32[4]{0:T(128)} custom-call(s32[8,512]{1,0:T(8,128)S(1)} %get-tuple-element.43.own_load, s16[528,256]{1,0:T(8,128)(2,1)S(1)} %collective-permute-done.10.came), custom_call_target="tpu_custom_call" | custom-call | bytes 286736 | tf_op jit(solution)/shard_map/pallas_call | solution.py:308
  62.8 0.0 collective-permute-done.12.refs_2_
  62.8 0.0 collective-permute-done.11.refs_1_
  62.8 0.8 %shard_map.67.refs_4_ = f32[512,512]{1,0:T(8,128)} custom-call(f32[512,256]{1,0:T(8,128)S(1)} %get-tuple-element.41.inflated, f32[8,256]{1,0:T(8,128)S(1)} %get-tuple-element.42.refs_0_, f32[8,256]{1,0:T(8,128)S(1)} %collective-permute-done.11.refs_1_, f32[8,256]{1,0:T(8,128)S(1)} %collective-permute-done.12.refs_2_, ...), custom_call_target="tpu_custom_call" | custom-call | bytes 1605632 | tf_op jit(solution)/shard_map/pallas_call | solution.py:308
  63.7 0.0 collective-permute-done.9.refs_3_
  63.7 1.5 %collective-permute-done.8.refs_2_ = f32[8,256]{1,0:T(8,128)S(1)} collective-permute-done((f32[8,256]{1,0:T(8,128)S(1)}, f32[8,256]{1,0:T(8,128)S(1)}, u32[]{:S(2)}, u32[]{:S(2)}) %collective-permute-start.8) | collective-permute-done | bytes 8224 | tf_op jit(solution)/shard_map/ppermute | solution.py:424
  65.2 0.0 collective-permute-done.7.refs_1_
  65.2 0.8 %shard_map.68 = f32[512,512]{1,0:T(8,128)} custom-call(f32[512,256]{1,0:T(8,128)S(1)} %get-tuple-element.38.inflated, f32[8,256]{1,0:T(8,128)S(1)} %get-tuple-element.39.refs_0_, f32[8,256]{1,0:T(8,128)S(1)} %collective-permute-done.7.refs_1_, f32[8,256]{1,0:T(8,128)S(1)} %collective-permute-done.8.refs_2_, ...), custom_call_target="tpu_custom_call", output_to_operand_aliasing={{}: (5, {})} | custom-call | bytes 2654208 | tf_op jit(solution)/shard_map/pallas_call | solution.py:308
Async XLA Ops:
  0.6 3.1 %collective-permute-start.1 = (bf16[16,1,128,128]{3,2,1,0:T(8,128)(2,1)}, bf16[16,1,128,128]{3,2,1,0:T(8,128)(2,1)S(1)}, u32[]{:S(2)}, u32[]{:S(2)}) collective-permute-start(bf16[16,1,128,128]{3,2,1,0:T(8,128)(2,1)} %own.1), channel_id=1, source_target_pairs={{0,4},{4,0},{8,12},{12,8},{1,5},{5,1},{9,13},{13,9},{2,6},{6,2},{1... | collective-permute-start | bytes 1572872 | tf_op jit(solution)/shard_map/ppermute | solution.py:346
  1.1 15.3 %collective-permute-start = (bf16[16,1,128,128]{3,2,1,0:T(8,128)(2,1)}, bf16[16,1,128,128]{3,2,1,0:T(8,128)(2,1)S(1)}, u32[]{:S(2)}, u32[]{:S(2)}) collective-permute-start(bf16[16,1,128,128]{3,2,1,0:T(8,128)(2,1)} %own.1), channel_id=1, source_target_pairs={{0,8},{4,12},{8,0},{12,4},{1,9},{5,13},{9,1},{13,5},{2,10},{6,14},... | collective-permute-start | bytes 1572872 | tf_op jit(solution)/shard_map/ppermute | solution.py:345
  3.7 1.6 %copy-start = (bf16[512,2048]{1,0:T(8,128)(2,1)S(1)}, bf16[512,2048]{1,0:T(8,128)(2,1)}, u32[]{:S(2)}) copy-start(bf16[512,2048]{1,0:T(8,128)(2,1)} %operand.1) | copy-start | bytes 6291460
  5.3 1.0 %copy-start.1 = (bf16[16,1,128,128]{3,2,1,0:T(8,128)(2,1)S(1)}, bf16[16,1,128,128]{3,2,1,0:T(8,128)(2,1)}, u32[]{:S(2)}) copy-start(bf16[16,1,128,128]{3,2,1,0:T(8,128)(2,1)} %own.1) | copy-start | bytes 1572868
  6.4 0.7 %copy-start.2 = (s32[16,4]{0,1:T(4,128)S(1)}, s32[16,4]{0,1:T(4,128)}, u32[]{:S(2)}) copy-start(s32[16,4]{0,1:T(4,128)} %param.6) | copy-start | bytes 772
  7.1 0.7 copy-start.3
  16.5 1.9 %collective-permute-start.2 = (bf16[16,1,128,128]{3,2,1,0:T(8,128)(2,1)S(1)}, bf16[16,1,128,128]{3,2,1,0:T(8,128)(2,1)S(1)}, u32[]{:S(2)}, u32[]{:S(2)}) collective-permute-start(bf16[16,1,128,128]{3,2,1,0:T(8,128)(2,1)S(1)} %collective-permute-done.refs_4_.held), channel_id=1, source_target_pairs={{0,4},{4,0},{8,12},{12,8},{1,5},{5,1},{9,13},{13,9},{2,6},{6,2},{1... | collective-permute-start | bytes 1572872 | tf_op jit(solution)/shard_map/ppermute | solution.py:364
  19.8 10.9 %collective-permute-start.4 = (s16[528,512]{1,0:T(8,128)(2,1)S(1)}, s16[528,512]{1,0:T(8,128)(2,1)S(1)}, u32[]{:S(2)}, u32[]{:S(2)}) collective-permute-start(s16[528,512]{1,0:T(8,128)(2,1)S(1)} %shard_map.62), channel_id=1, source_target_pairs={{0,4},{1,2},{2,1},{3,7},{4,0},{5,6},{6,5},{7,3},{8,12},{9,10},{10,... | collective-permute-start | bytes 1622024 | tf_op jit(solution)/shard_map/ppermute | solution.py:386
  20.0 16.9 %collective-permute-start.3 = (s16[528,512]{1,0:T(8,128)(2,1)S(1)}, s16[528,512]{1,0:T(8,128)(2,1)S(1)}, u32[]{:S(2)}, u32[]{:S(2)}) collective-permute-start(s16[528,512]{1,0:T(8,128)(2,1)S(1)} %shard_map.62), channel_id=1, source_target_pairs={{0,1},{1,0},{2,3},{3,2},{4,5},{5,4},{6,7},{7,6},{8,9},{9,8},{10,11... | collective-permute-start | bytes 1622024 | tf_op jit(solution)/shard_map/ppermute | solution.py:385
  29.7 18.3 %collective-permute-start.5 = (s16[528,512]{1,0:T(8,128)(2,1)S(1)}, s16[528,512]{1,0:T(8,128)(2,1)S(1)}, u32[]{:S(2)}, u32[]{:S(2)}) collective-permute-start(s16[528,512]{1,0:T(8,128)(2,1)S(1)} %get-tuple-element.32), channel_id=1, source_target_pairs={{0,2},{1,0},{2,3},{3,1},{4,6},{5,4},{6,7},{7,5},{8,10},{9,8},{10,1... | collective-permute-start | bytes 1622024 | tf_op jit(solution)/shard_map/ppermute | solution.py:400
  37.2 16.9 %collective-permute-start.10 = (s16[528,256]{1,0:T(8,128)(2,1)S(1)}, s16[528,256]{1,0:T(8,128)(2,1)S(1)}, u32[]{:S(2)}, u32[]{:S(2)}) collective-permute-start(s16[528,256]{1,0:T(8,128)(2,1)S(1)} %get-tuple-element.40), channel_id=1, source_target_pairs={{0,1},{1,3},{3,2},{2,0},{4,5},{5,7},{7,6},{6,4},{8,9},{9,11},{11,1... | collective-permute-start | bytes 811016 | tf_op jit(solution)/shard_map/ppermute | solution.py:404
  39.4 20.4 %collective-permute-start.6 = (s16[528,256]{1,0:T(8,128)(2,1)S(1)}, s16[528,256]{1,0:T(8,128)(2,1)S(1)}, u32[]{:S(2)}, u32[]{:S(2)}) collective-permute-start(s16[528,256]{1,0:T(8,128)(2,1)S(1)} %get-tuple-element.37), channel_id=1, source_target_pairs={{0,1},{1,3},{3,2},{2,0},{4,5},{5,7},{7,6},{6,4},{8,9},{9,11},{11,1... | collective-permute-start | bytes 811016 | tf_op jit(solution)/shard_map/ppermute | solution.py:404
  54.2 7.8 %collective-permute-start.13 = (f32[8,256]{1,0:T(8,128)S(1)}, f32[8,256]{1,0:T(8,128)S(1)}, u32[]{:S(2)}, u32[]{:S(2)}) collective-permute-start(f32[8,256]{1,0:T(8,128)S(1)} %get-tuple-element.42.refs_0_), channel_id=1, source_target_pairs={{0,12},{4,8},{8,4},{12,0},{1,13},{5,9},{9,5},{13,1},{2,14},{6,10},... | collective-permute-start | bytes 24584 | tf_op jit(solution)/shard_map/ppermute | solution.py:424
  55.8 7.0 %collective-permute-start.12 = (f32[8,256]{1,0:T(8,128)S(1)}, f32[8,256]{1,0:T(8,128)S(1)}, u32[]{:S(2)}, u32[]{:S(2)}) collective-permute-start(f32[8,256]{1,0:T(8,128)S(1)} %get-tuple-element.42.refs_0_), channel_id=1, source_target_pairs={{0,8},{4,12},{8,0},{12,4},{1,9},{5,13},{9,1},{13,5},{2,10},{6,14},... | collective-permute-start | bytes 24584 | tf_op jit(solution)/shard_map/ppermute | solution.py:424
  56.3 6.5 %collective-permute-start.11 = (f32[8,256]{1,0:T(8,128)S(1)}, f32[8,256]{1,0:T(8,128)S(1)}, u32[]{:S(2)}, u32[]{:S(2)}) collective-permute-start(f32[8,256]{1,0:T(8,128)S(1)} %get-tuple-element.42.refs_0_), channel_id=1, source_target_pairs={{0,4},{4,0},{8,12},{12,8},{1,5},{5,1},{9,13},{13,9},{2,6},{6,2},{1... | collective-permute-start | bytes 24584 | tf_op jit(solution)/shard_map/ppermute | solution.py:424
  59.9 3.8 %collective-permute-start.9 = (f32[8,256]{1,0:T(8,128)S(1)}, f32[8,256]{1,0:T(8,128)S(1)}, u32[]{:S(2)}, u32[]{:S(2)}) collective-permute-start(f32[8,256]{1,0:T(8,128)S(1)} %get-tuple-element.39.refs_0_), channel_id=1, source_target_pairs={{0,12},{4,8},{8,4},{12,0},{1,13},{5,9},{9,5},{13,1},{2,14},{6,10},... | collective-permute-start | bytes 24584 | tf_op jit(solution)/shard_map/ppermute | solution.py:424
  61.5 3.7 %collective-permute-start.8 = (f32[8,256]{1,0:T(8,128)S(1)}, f32[8,256]{1,0:T(8,128)S(1)}, u32[]{:S(2)}, u32[]{:S(2)}) collective-permute-start(f32[8,256]{1,0:T(8,128)S(1)} %get-tuple-element.39.refs_0_), channel_id=1, source_target_pairs={{0,8},{4,12},{8,0},{12,4},{1,9},{5,13},{9,1},{13,5},{2,10},{6,14},... | collective-permute-start | bytes 24584 | tf_op jit(solution)/shard_map/ppermute | solution.py:424
  62.0 3.2 %collective-permute-start.7 = (f32[8,256]{1,0:T(8,128)S(1)}, f32[8,256]{1,0:T(8,128)S(1)}, u32[]{:S(2)}, u32[]{:S(2)}) collective-permute-start(f32[8,256]{1,0:T(8,128)S(1)} %get-tuple-element.39.refs_0_), channel_id=1, source_target_pairs={{0,4},{4,0},{8,12},{12,8},{1,5},{5,1},{9,13},{13,9},{2,6},{6,2},{1... | collective-permute-start | bytes 24584 | tf_op jit(solution)/shard_map/ppermute | solution.py:424

commit v5 on v4

--- a/solution.py
+++ b/solution.py
@@ -18,8 +18,14 @@
 NEAREST = 12582912.0
 OCTAVE = 128.0
 
+ALL = list(range(SLAB_DEV))
+
 VMEM = pl.BlockSpec(memory_space=pltpu.VMEM)
 SMEM = pl.BlockSpec(memory_space=pltpu.SMEM)
+
+
+def blocks_of(part):
+    return ALL[part * SLAB_DEV // PARTS : (part + 1) * SLAB_DEV // PARTS]
 
 
 def code_scale(values):
@@ -33,30 +39,34 @@
     return ((scaled + NEAREST) - NEAREST).astype(jnp.int32).astype(jnp.int16)
 
 
-def head_rows(code, *counts):
-    shape = (HEAD, code.shape[1])
-    row = lax.broadcasted_iota(jnp.int32, shape, 0)
-    head = jnp.broadcast_to(code.astype(jnp.int32), shape)
-    for j, one in enumerate(counts):
-        head = jnp.where(row > j, jnp.broadcast_to(one, shape), head)
-    return head.astype(jnp.int16)
-
-
-def put_coded(out, lanes, values, *counts):
-    code = code_scale(values)
-    out[pl.ds(0, HEAD), lanes] = head_rows(code, *counts)
-    out[pl.ds(HEAD, values.shape[0]), lanes] = encode(values, code)
-
-
-def decode(ref, lanes):
-    rows = ref.shape[0] - HEAD
-    head = ref[pl.ds(0, HEAD), lanes].astype(jnp.int32).astype(jnp.float32)
-    scale = jnp.exp2(head[0:1] * (1.0 / OCTAVE)) * (1.0 / STEPS)
-    return ref[pl.ds(HEAD, rows), lanes].astype(jnp.int32).astype(jnp.float32) * scale
-
-
-def head_counts(ref, lanes, part=0):
-    return ref[pl.ds(0, HEAD), lanes].astype(jnp.int32)[1 + part : 2 + part]
+def put_coded(outs, values, counts):
+    row = lax.broadcasted_iota(jnp.int32, counts.shape, 0)
+    heads = [jnp.where(row < SLAB_DEV, 0, counts) for _ in outs]
+    for block, get in values:
+        value = get()
+        rows = value.shape[0]
+        code = code_scale(value)
+        coded = encode(value, code)
+        for j, (out, held) in enumerate(outs):
+            if block in held:
+                at = held.index(block)
+                out[pl.ds(at * rows, rows), :] = coded
+                heads[j] = jnp.where(row == at, jnp.broadcast_to(code.astype(jnp.int32), counts.shape), heads[j])
+    for (out, _), head in zip(outs, heads):
+        out[pl.ds(out.shape[0] - HEAD, HEAD), :] = head.astype(jnp.int16)
+
+
+def head_of(ref):
+    return ref[pl.ds(ref.shape[0] - HEAD, HEAD), :].astype(jnp.int32)
+
+
+def decode(ref, head, at, rows):
+    scale = jnp.exp2(head[at : at + 1].astype(jnp.float32) * (1.0 / OCTAVE)) * (1.0 / STEPS)
+    return ref[pl.ds(at * rows, rows), :].astype(jnp.int32).astype(jnp.float32) * scale
+
+
+def lanes_of(block):
+    return pl.ds(block * SIDE, SIDE)
 
 
 def slot_of(place, ny):
@@ -161,11 +171,8 @@
     plan = plan_of(plan_ref, operand)
     shard = which(lax.axis_index("col"))
     add_terms(plan, shard, place, held, total, operand)
-
-    def body(tile, lanes):
-        put_coded(out, lanes, total[:, lanes], counts_of(plan, shard, tile))
-
-    tiles(total.shape[1], body)
+    values = [(b, lambda b=b: total[:, lanes_of(b)]) for b in range(SLAB_DEV)]
+    put_coded([(out, ALL)], values, counts_of(plan, shard))
 
 
 def fill(slab, plan, shard, blocks):
@@ -182,13 +189,12 @@
         lax.fori_loop(0, plan.ref[plan.length(place, shard)], one, 0)
 
 
-def counts_of(plan, shard, tile):
-    lane = lax.broadcasted_iota(jnp.int32, (1, TILE), 1)
-    counts = jnp.zeros((1, TILE), jnp.int32)
-    for j in range(TILE // SIDE):
-        block = shard * SLAB_DEV + tile * (TILE // SIDE) + j
-        counts = jnp.where((lane >= j * SIDE) & (lane < (j + 1) * SIDE), plan.ref[plan.load(block)], counts)
-    return counts
+def counts_of(plan, shard):
+    row = lax.broadcasted_iota(jnp.int32, (HEAD, SIDE), 0)
+    head = jnp.zeros((HEAD, SIDE), jnp.int32)
+    for b in range(SLAB_DEV):
+        head = jnp.where(row == SLAB_DEV + b, plan.ref[plan.load(shard * SLAB_DEV + b)], head)
+    return head
 
 
 def tiles(width, body):
@@ -199,88 +205,86 @@
     lax.fori_loop(0, width // TILE, step, 0)
 
 
-def products(coded, plain, nblocks, *refs):
-    plan_ref, operand, *blocks = refs[: 2 + nblocks]
-    out_coded, *outs, slab = refs[2 + nblocks :]
+def coded_product(which, nblocks, plan_ref, operand, *refs):
+    blocks, (whole, *parts, slab) = refs[:nblocks], refs[nblocks:]
     plan = plan_of(plan_ref, operand)
+    shard = which(lax.axis_index("col"))
+    fill(slab, plan, shard, blocks)
+    done = {}
+
+    def values(block):
+        tile, at = block * SIDE // TILE, block * SIDE % TILE
+        if tile not in done:
+            lanes = pl.ds(tile * TILE, TILE)
+            done[tile] = jnp.dot(operand[...], slab[:, lanes], preferred_element_type=jnp.float32)
+        return done[tile][:, at : at + SIDE]
+
+    outs = [(whole, ALL)] + [(part, blocks_of(j)) for j, part in enumerate(parts)]
+    put_coded(outs, [(b, functools.partial(values, b)) for b in ALL], counts_of(plan, shard))
+
+
+def plain_products(plain, nblocks, plan_ref, operand, *refs):
+    blocks, (*outs, slab) = refs[:nblocks], refs[nblocks:]
     outs, loads = outs[: len(plain)], outs[len(plain) :]
-
-    def one_shard(which, put):
+    plan = plan_of(plan_ref, operand)
+    for which, out, row in zip(plain, outs, loads):
         shard = which(lax.axis_index("col"))
         fill(slab, plan, shard, blocks)
 
-        def body(tile, lanes):
-            values = jnp.dot(operand[...], slab[:, lanes], preferred_element_type=jnp.float32)
-            put(lanes, values, counts_of(plan, shard, tile))
+        def body(tile, lanes, out=out):
+            out[:, lanes] = jnp.dot(operand[...], slab[:, lanes], preferred_element_type=jnp.float32)
 
         tiles(slab.shape[1], body)
-
-    one_shard(coded, functools.partial(put_coded, out_coded))
-    for which, out, row in zip(plain, outs, loads):
-
-        def put(lanes, values, counts, out=out, row=row):
-            out[:, lanes] = values
-            row[:, lanes] = jnp.broadcast_to(counts, (8, TILE))
-
-        one_shard(which, put)
-
-
-def relay(own, own_load, came, *outs):
+        row[...] = counts_of(plan, shard)
+
+
+def relay(part, own, own_load, came, out):
     place = lax.axis_index("col")
     inner = (place == 1) | (place == 2)
-    width = outs[0].shape[1]
-    for part, out in enumerate(outs):
-
-        def body(tile, lanes, part=part, out=out):
-            ats = [pl.ds(pl.multiple_of(j * width + tile * TILE, TILE), TILE) for j in range(len(outs))]
-            at = ats[part]
-
-            @pl.when(inner)
-            def _():
-                counts = [own_load[0:1, one] + head_counts(came, one) for one in ats]
-                put_coded(out, lanes, own[:, at] + decode(came, at), *counts)
-
-            @pl.when(jnp.logical_not(inner))
-            def _():
-                put_coded(out, lanes, own[:, at], *[own_load[0:1, one] for one in ats])
-
-        tiles(width, body)
+    held, rows = blocks_of(part), own.shape[0]
+
+    @pl.when(inner)
+    def _():
+        head = head_of(came)
+        values = [
+            (b, lambda at=at, b=b: own[:, lanes_of(b)] + decode(came, head, at, rows)) for at, b in enumerate(held)
+        ]
+        put_coded([(out, held)], values, own_load[...] + head)
+
+    @pl.when(jnp.logical_not(inner))
+    def _():
+        put_coded([(out, held)], [(b, lambda b=b: own[:, lanes_of(b)]) for b in held], own_load[...])
 
 
 def settle(own, own_load, came_b, came_f, out, out_load):
     place = lax.axis_index("col")
     inner = (place == 1) | (place == 2)
-
-    def body(tile, lanes):
-        out[:, lanes] = own[:, lanes] + decode(came_f, lanes)
-        out_load[:, lanes] = own_load[:, lanes] + head_counts(came_f, lanes)
-
-        @pl.when(inner)
-        def _():
-            out[:, lanes] = out[:, lanes] + decode(came_b, lanes)
-            out_load[:, lanes] = out_load[:, lanes] + head_counts(came_b, lanes)
-
-    tiles(own.shape[1], body)
+    rows, head = own.shape[0], head_of(came_f)
+    out_load[...] = own_load[...] + head
+    for b in ALL:
+        out[:, lanes_of(b)] = own[:, lanes_of(b)] + decode(came_f, head, b, rows)
+
+    @pl.when(inner)
+    def _():
+        head = head_of(came_b)
+        out_load[...] = out_load[...] + head
+        for b in ALL:
+            out[:, lanes_of(b)] = out[:, lanes_of(b)] + decode(came_b, head, b, rows)
 
 
 def inflate(part, own, came, out, totals):
-    width = out.shape[1]
-
-    def body(tile, lanes):
-        at = pl.ds(pl.multiple_of(part * width + tile * TILE, TILE), TILE)
-        expanded = own[:, at] + decode(came, lanes)
+    rows, head = own.shape[0], head_of(came)
+    for at, b in enumerate(blocks_of(part)):
+        expanded = own[:, lanes_of(b)] + decode(came, head, at, rows)
         inflated = expanded * expanded
-        out[:, lanes] = inflated
-        totals[:, lanes] = jnp.sum(inflated.reshape(-1, 8, TILE), axis=0)
-
-    tiles(width, body)
+        out[:, lanes_of(at)] = inflated
+        totals[:, lanes_of(at)] = jnp.sum(inflated.reshape(-1, 8, SIDE), axis=0)
 
 
 def count(own_load, came, load):
-    width = came.shape[1]
+    head = own_load[...] + head_of(came)
     for j in range(SLAB_DEV):
-        lanes, at = pl.ds(j * SIDE % width, SIDE), pl.ds(j * SIDE, SIDE)
-        load[j] = jnp.max(own_load[0:1, at] + head_counts(came, lanes, j * SIDE // width))
+        load[j] = jnp.max(head[SLAB_DEV + j : SLAB_DEV + j + 1])
 
 
 def scale(all_rows, part, inflated, *refs):
@@ -325,7 +329,7 @@
     shards = lax.axis_size("col")
     f32 = functools.partial(jax.ShapeDtypeStruct, dtype=jnp.float32)
     i32 = functools.partial(jax.ShapeDtypeStruct, dtype=jnp.int32)
-    coded = jax.ShapeDtypeStruct((HEAD + rows, width), jnp.int16)
+    coded = jax.ShapeDtypeStruct((SLAB_DEV * rows + HEAD, SIDE), jnp.int16)
 
     swap = [(a, a ^ 1) for a in range(2 * ny)]
 
@@ -345,7 +349,7 @@
     turned = [lax.ppermute(slot_blocks, "row", turn(by)) for by in range(1, ny)]
     twin = lax.ppermute(slot_blocks, "row", swap)
     plan, operand_near, own_near, total = call(
-        functools.partial(begin, ny, first),
+        functools.partial(begin, ny, second),
         [slot_columns.T, live_counts, operand_panel, slot_blocks, twin],
         [
             i32((Plan(None, here, slots, shards).size,)),
@@ -364,7 +368,7 @@
     blocks += [x for came in turned for x in (came, lax.ppermute(came, "row", swap))]
     for place in range(2, slots - 1):
         [total] = call(
-            functools.partial(go_on, first, place),
+            functools.partial(go_on, second, place),
             [plan, operand_near, blocks[place], total],
             [f32((rows, width))],
             [VMEM],
@@ -373,8 +377,8 @@
             1,
             onto={3: 0},
         )
-    [send_a] = call(
-        functools.partial(code_sum, first, slots - 1),
+    [send_f] = call(
+        functools.partial(code_sum, second, slots - 1),
         [plan, operand_near, blocks[-1], total],
         [coded],
         [VMEM],
@@ -382,28 +386,44 @@
         flops // 8,
         1,
     )
-    came_a = lax.ppermute(send_a, "col", [(0, 1), (1, 0), (2, 3), (3, 2)])
+    came_f = lax.ppermute(send_f, "col", [(0, 2), (1, 0), (2, 3), (3, 1)])
+    ins = [plan, operand_near, *blocks]
+    slab = [pltpu.VMEM((depth, width), jnp.bfloat16)]
+    part_coded = jax.ShapeDtypeStruct((SLAB_DEV // PARTS * rows + HEAD, SIDE), jnp.int16)
+    send_b, *send_a = call(
+        functools.partial(coded_product, first, len(blocks)),
+        ins,
+        [coded] + [part_coded] * PARTS,
+        [VMEM] * (1 + PARTS),
+        slab,
+        flops,
+        1,
+    )
+    came_a = [lax.ppermute(one, "col", [(0, 1), (1, 0), (2, 3), (3, 2)]) for one in send_a]
     came_b = lax.ppermute(
-        send_a,
+        send_b,
         ("row", "col"),
         [(4 * r + c, 4 * r + 3 - c if c in (1, 2) else 4 * (r ^ 1) + c) for r in range(2 * ny) for c in range(4)],
     )
-    send_f, passed, own, passed_load, own_load = call(
-        functools.partial(products, second, (third, lambda z: z), len(blocks)),
-        [plan, operand_near, *blocks],
-        [coded, f32((rows, width)), f32((rows, width)), i32((8, width)), i32((8, width))],
-        [VMEM] * 5,
-        [pltpu.VMEM((depth, width), jnp.bfloat16)],
-        3 * flops,
+    ins[0], came_f = lax.optimization_barrier((ins[0], came_f))
+    passed, own, passed_load, own_load = call(
+        functools.partial(plain_products, (third, lambda z: z), len(blocks)),
+        ins,
+        [f32((rows, width)), f32((rows, width)), i32((HEAD, SIDE)), i32((HEAD, SIDE))],
+        [VMEM] * 4,
+        slab,
+        2 * flops,
         1,
     )
-    came_f = lax.ppermute(send_f, "col", [(0, 2), (1, 0), (2, 3), (3, 1)])
-    came_a, came_b = lax.optimization_barrier((came_a, came_b))
-    sent = jax.ShapeDtypeStruct((HEAD + rows, width // PARTS), jnp.int16)
-    send_t = call(relay, [passed, passed_load, came_a], [sent] * PARTS, [VMEM] * PARTS)
-    came_t = [lax.ppermute(one, "col", [(0, 1), (1, 3), (3, 2), (2, 0)]) for one in send_t]
+    came_a[-1], came_b = lax.optimization_barrier((came_a[-1], came_b))
+    came_t = []
+    for part in range(PARTS):
+        [send_t] = call(
+            functools.partial(relay, part), [passed, passed_load, came_a[part]], [part_coded], [VMEM]
+        )
+        came_t.append(lax.ppermute(send_t, "col", [(0, 1), (1, 3), (3, 2), (2, 0)]))
     own, own_load = call(
-        settle, [own, own_load, came_b, came_f], [f32((rows, width)), i32((8, width))], [VMEM] * 2
+        settle, [own, own_load, came_b, came_f], [f32((rows, width)), i32((HEAD, SIDE))], [VMEM] * 2
     )
     all_rows = rows * lax.axis_size("row")
     hbm = pl.BlockSpec(memory_space=pl.ANY)

time: 66.1 us -> 64.8 us (0.980)
  waiting for transfers between devices: 30.9 us -> 26.6 us
  starting transfers between devices: 14.9 us -> 17.2 us
    ppermute x4 -> x5, waiting for transfers between devices: 15.5 us -> 11.9 us  [the longest x2 7.26 us: body_line(): came_t.append(lax.ppermute(send_t, 'col', [(0, 1), (1, 3), (3, 2), (2, 0)]))]
    ppermute x1, starting transfers between devices: 0.95 us -> 2.88 us  [body_line(): came_f = lax.ppermute(send_f, 'col', [(0, 2), (1, 0), (2, 3), (3, 1)])]
    ppermute x4 -> x5, starting transfers between devices: 6.6 us -> 7.4 us  [the longest x2 5.16 us: body_line(): came_t.append(lax.ppermute(send_t, 'col', [(0, 1), (1, 3), (3, 2), (2, 0)]))]
    pallas_call x11 -> x13, Pallas kernels: 15.5 us -> 16 us  [call(): pl.pallas_call(kernel, in_specs=[SMEM] * few + [pl.BlockSpec(memory_space...]
  transfers between devices with their start and end apart: 14 -> 15, of which waited for: 7 -> 8; matrix products, arithmetic and copies ran while one was open for 0% -> 0% of each run, Pallas kernels for 20% -> 21%
where the time goes in v5:
time: 64.8 us; the launch traced here: 64.6 us
  waiting for transfers between devices  26.6 us (41%)
  starting transfers between devices  17.2 us (27%)
  Pallas kernels  16 us (25%)
  local copies, waits for them, and re-layouts  3.97 us (6%)
  between operations  0.76 us (1%)
    pallas_call x13, Pallas kernels, call(): pl.pallas_call(kernel, in_specs=[SMEM] * few + [pl.BlockSpec(memory_space...  16 us
    ppermute x1, waiting for transfers between devices, body_line(): came_f = lax.ppermute(send_f, 'col', [(0, 2), (1, 0), (2, 3), (3, 1)])  7.66 us
    ppermute x2, waiting for transfers between devices, body_line(): came_t.append(lax.ppermute(send_t, 'col', [(0, 1), (1, 3), (3, 2), (2, 0)]))  7.26 us
    ppermute x2, starting transfers between devices, body_line(): came_t.append(lax.ppermute(send_t, 'col', [(0, 1), (1, 3), (3, 2), (2, 0)]))  5.16 us
    ppermute x1, waiting for transfers between devices, body_line(): turned = [lax.ppermute(slot_blocks, 'row', turn(by)) for by in range(1, ny)]  4.85 us
    ppermute x2, waiting for transfers between devices, body_line(): lax.ppermute(one, 'col', [(0, 1), (1, 0), (2, 3), (3, 2)])  4.6 us
    unnamed x8, local copies, waits for them, and re-layouts  3.97 us
    ppermute x6, starting transfers between devices, body_line(): others.append(lax.ppermute(totals, 'row', pairs))  3.84 us
  transfers between devices with their start and end apart: 15, of which 8 were waited for; matrix products, arithmetic and copies ran while one was open for 0% of the time, Pallas kernels for 21%

profile of v5, /device:TPU:0, one launch (start us, length us, event | category | flops | bytes accessed | tf_op | source)
XLA Modules:
  0.0 64.6 jit_solution(15074736700079335388)
XLA Ops:
  0.6 0.5 collective-permute-start.1
  1.1 2.6 %collective-permute-start = (bf16[16,1,128,128]{3,2,1,0:T(8,128)(2,1)}, bf16[16,1,128,128]{3,2,1,0:T(8,128)(2,1)S(1)}, u32[]{:S(2)}, u32[]{:S(2)}) collective-permute-start(bf16[16,1,128,128]{3,2,1,0:T(8,128)(2,1)} %own.1), channel_id=1, source_target_pairs={{0,8},{4,12},{8,0},{12,4},{1,9},{5,13},{9,1},{13,5},{2,10},{6,14},... | collective-permute-start | bytes 1572872 | tf_op jit(solution)/shard_map/ppermute | solution.py:349
  3.7 0.0 collective-permute-done.1.twin.refs_1_
  3.7 0.0 copy-start
  3.7 1.6 %copy-done = bf16[512,2048]{1,0:T(8,128)(2,1)S(1)} copy-done((bf16[512,2048]{1,0:T(8,128)(2,1)S(1)}, bf16[512,2048]{1,0:T(8,128)(2,1)}, u32[]{:S(2)}) %copy-start) | copy-done | bytes 2097176
  5.3 0.0 copy-start.1
  5.3 1.0 %copy-done.1 = bf16[16,1,128,128]{3,2,1,0:T(8,128)(2,1)S(1)} copy-done((bf16[16,1,128,128]{3,2,1,0:T(8,128)(2,1)S(1)}, bf16[16,1,128,128]{3,2,1,0:T(8,128)(2,1)}, u32[]{:S(2)}) %copy-start.1) | copy-done | bytes 524312
  6.4 0.0 copy-start.2
  6.4 0.7 %copy-done.2 = s32[16,4]{0,1:T(4,128)S(1)} copy-done((s32[16,4]{0,1:T(4,128)S(1)}, s32[16,4]{0,1:T(4,128)}, u32[]{:S(2)}) %copy-start.2) | copy-done | bytes 280
  7.1 0.0 copy-start.3
  7.1 0.7 %copy-done.3 = s32[16]{0:T(128)S(1)} copy-done((s32[16]{0:T(128)S(1)}, s32[16]{0:T(128)}, u32[]{:S(2)}) %copy-start.3) | copy-done | bytes 88
  7.7 3.9 %shard_map.59 = (s32[288]{0:T(512)S(1)}, bf16[512,2048]{1,0:T(8,128)(2,1)S(1)}, bf16[16,1,128,128]{3,2,1,0:T(8,128)(2,1)S(1)}, f32[512,512]{1,0:T(8,128)S(1)}) custom-call(s32[4,16]{1,0:T(4,128)S(1)} %bitcast.1, s32[16]{0:T(128)S(1)} %copy-done.3, bf16[512,2048]{1,0:T(8,128)(2,1)S(1)} %copy-done, bf16[16,1,128,128]{3,2,1,0:T(8,128)(2,1)S(1)} %copy-done.1, ...), custom_call_target="tpu_custom_call" | custom-call | flops 268435456 | bytes 6817216 | tf_op jit(solution)/shard_map/pallas_call | solution.py:312
  11.6 4.9 %collective-permute-done.held.refs_2_ = bf16[16,1,128,128]{3,2,1,0:T(8,128)(2,1)S(1)} collective-permute-done((bf16[16,1,128,128]{3,2,1,0:T(8,128)(2,1)}, bf16[16,1,128,128]{3,2,1,0:T(8,128)(2,1)S(1)}, u32[]{:S(2)}, u32[]{:S(2)}) %collective-permute-start) | collective-permute-done | bytes 524320 | tf_op jit(solution)/shard_map/ppermute | solution.py:349
  16.5 0.0 collective-permute-start.2
  16.5 1.0 %shard_map.60.total = f32[512,512]{1,0:T(8,128)S(1)} custom-call(s32[288]{0:T(512)S(1)} %get-tuple-element.30.plan_ref, bf16[512,2048]{1,0:T(8,128)(2,1)S(1)} %get-tuple-element.27.operand, bf16[16,1,128,128]{3,2,1,0:T(8,128)(2,1)S(1)} %collective-permute-done.held.refs_2_, f32[512,512]{1,0:T(8,128)S(1)} %get-tuple-element.29._), custom_call_target="tpu_custom_call", output_to_operand_aliasing={{}: (3, {})} | custom-call | flops 134217728 | bytes 4719744 | tf_op jit(solution)/shard_map/pallas_call | solution.py:312
  17.5 0.9 %collective-permute-done.2.held.refs_3_ = bf16[16,1,128,128]{3,2,1,0:T(8,128)(2,1)S(1)} collective-permute-done((bf16[16,1,128,128]{3,2,1,0:T(8,128)(2,1)S(1)}, bf16[16,1,128,128]{3,2,1,0:T(8,128)(2,1)S(1)}, u32[]{:S(2)}, u32[]{:S(2)}) %collective-permute-start.2) | collective-permute-done | bytes 524320 | tf_op jit(solution)/shard_map/ppermute | solution.py:368
  18.4 1.4 %shard_map.61 = s16[2064,128]{1,0:T(8,128)(2,1)S(1)} custom-call(s32[288]{0:T(512)S(1)} %get-tuple-element.30.plan_ref, bf16[512,2048]{1,0:T(8,128)(2,1)S(1)} %get-tuple-element.27.operand, bf16[16,1,128,128]{3,2,1,0:T(8,128)(2,1)S(1)} %collective-permute-done.2.held.refs_3_, f32[512,512]{1,0:T(8,128)S(1)} %shard_map.60.total), custom_call_target="tpu_custom_call" | custom-call | flops 134217728 | bytes 4199552 | tf_op jit(solution)/shard_map/pallas_call | solution.py:312
  19.8 2.9 %collective-permute-start.3 = (s16[2064,128]{1,0:T(8,128)(2,1)S(1)}, s16[2064,128]{1,0:T(8,128)(2,1)S(1)}, u32[]{:S(2)}, u32[]{:S(2)}) collective-permute-start(s16[2064,128]{1,0:T(8,128)(2,1)S(1)} %shard_map.61), channel_id=1, source_target_pairs={{0,2},{1,0},{2,3},{3,1},{4,6},{5,4},{6,7},{7,5},{8,10},{9,8},{10,1... | collective-permute-start | bytes 1585160 | tf_op jit(solution)/shard_map/ppermute | solution.py:389
  22.7 2.5 %shard_map.63 = (s16[2064,128]{1,0:T(8,128)(2,1)S(1)}, s16[1040,128]{1,0:T(8,128)(2,1)S(1)}, s16[1040,128]{1,0:T(8,128)(2,1)S(1)}) custom-call(s32[288]{0:T(512)S(1)} %get-tuple-element.30.plan_ref, bf16[512,2048]{1,0:T(8,128)(2,1)S(1)} %get-tuple-element.27.operand, bf16[16,1,128,128]{3,2,1,0:T(8,128)(2,1)S(1)} %get-tuple-element.31.refs_0_, ...), custom_call_target="tpu_custom_call" | custom-call | flops 1073741824 | bytes 5256320 | tf_op jit(solution)/shard_map/pallas_call | solution.py:312
  25.2 0.1 collective-permute-start.5
  25.3 2.1 %collective-permute-start.10 = (s16[1040,128]{1,0:T(8,128)(2,1)S(1)}, s16[1040,128]{1,0:T(8,128)(2,1)S(1)}, u32[]{:S(2)}, u32[]{:S(2)}) collective-permute-start(s16[1040,128]{1,0:T(8,128)(2,1)S(1)} %get-tuple-element.44), channel_id=1, source_target_pairs={{0,1},{1,0},{2,3},{3,2},{4,5},{5,4},{6,7},{7,6},{8,9},{9,8},{10,11... | collective-permute-start | bytes 798728 | tf_op jit(solution)/shard_map/ppermute | solution.py:402
  27.4 0.0 collective-permute-start.4
  27.4 7.7 %collective-permute-done.3.came_f = s16[2064,128]{1,0:T(8,128)(2,1)S(1)} collective-permute-done((s16[2064,128]{1,0:T(8,128)(2,1)S(1)}, s16[2064,128]{1,0:T(8,128)(2,1)S(1)}, u32[]{:S(2)}, u32[]{:S(2)}) %collective-permute-start.3) | collective-permute-done | bytes 528416 | tf_op jit(solution)/shard_map/ppermute | solution.py:389
  35.1 4.0 %shard_map.62 = (f32[512,512]{1,0:T(8,128)S(1)}, f32[512,512]{1,0:T(8,128)S(1)}, s32[16,128]{1,0:T(8,128)S(1)}, s32[16,128]{1,0:T(8,128)S(1)}) custom-call(s32[288]{0:T(512)S(1)} %get-tuple-element.30.plan_ref, bf16[512,2048]{1,0:T(8,128)(2,1)S(1)} %get-tuple-element.27.operand, bf16[16,1,128,128]{3,2,1,0:T(8,128)(2,1)S(1)} %get-tuple-element.31.refs_0_, ...), custom_call_target="tpu_custom_call" | custom-call | flops 2147483648 | bytes 6308992 | tf_op jit(solution)/shard_map/pallas_call | solution.py:312
  39.1 1.7 %collective-permute-done.10.came = s16[1040,128]{1,0:T(8,128)(2,1)S(1)} collective-permute-done((s16[1040,128]{1,0:T(8,128)(2,1)S(1)}, s16[1040,128]{1,0:T(8,128)(2,1)S(1)}, u32[]{:S(2)}, u32[]{:S(2)}) %collective-permute-start.10) | collective-permute-done | bytes 266272 | tf_op jit(solution)/shard_map/ppermute | solution.py:402
  40.8 0.2 shard_map.67
  41.0 2.6 %collective-permute-start.11 = (s16[1040,128]{1,0:T(8,128)(2,1)S(1)}, s16[1040,128]{1,0:T(8,128)(2,1)S(1)}, u32[]{:S(2)}, u32[]{:S(2)}) collective-permute-start(s16[1040,128]{1,0:T(8,128)(2,1)S(1)} %shard_map.67), channel_id=1, source_target_pairs={{0,1},{1,3},{3,2},{2,0},{4,5},{5,7},{7,6},{6,4},{8,9},{9,11},{11,1... | collective-permute-start | bytes 798728 | tf_op jit(solution)/shard_map/ppermute | solution.py:424
  43.6 2.9 %collective-permute-done.4.came = s16[1040,128]{1,0:T(8,128)(2,1)S(1)} collective-permute-done((s16[1040,128]{1,0:T(8,128)(2,1)S(1)}, s16[1040,128]{1,0:T(8,128)(2,1)S(1)}, u32[]{:S(2)}, u32[]{:S(2)}) %collective-permute-start.4) | collective-permute-done | bytes 266272 | tf_op jit(solution)/shard_map/ppermute | solution.py:402
  46.5 0.0 collective-permute-done.5.came_b
  46.5 0.2 shard_map.65
  46.7 2.6 %collective-permute-start.6 = (s16[1040,128]{1,0:T(8,128)(2,1)S(1)}, s16[1040,128]{1,0:T(8,128)(2,1)S(1)}, u32[]{:S(2)}, u32[]{:S(2)}) collective-permute-start(s16[1040,128]{1,0:T(8,128)(2,1)S(1)} %shard_map.65), channel_id=1, source_target_pairs={{0,1},{1,3},{3,2},{2,0},{4,5},{5,7},{7,6},{6,4},{8,9},{9,11},{11,1... | collective-permute-start | bytes 798728 | tf_op jit(solution)/shard_map/ppermute | solution.py:424
  49.3 0.2 shard_map.64
  49.5 3.7 %collective-permute-done.11.came = s16[1040,128]{1,0:T(8,128)(2,1)S(1)} collective-permute-done((s16[1040,128]{1,0:T(8,128)(2,1)S(1)}, s16[1040,128]{1,0:T(8,128)(2,1)S(1)}, u32[]{:S(2)}, u32[]{:S(2)}) %collective-permute-start.11) | collective-permute-done | bytes 266272 | tf_op jit(solution)/shard_map/ppermute | solution.py:424
  53.1 0.1 shard_map.68
  53.3 1.1 %collective-permute-start.14 = (f32[8,256]{1,0:T(8,128)S(1)}, f32[8,256]{1,0:T(8,128)S(1)}, u32[]{:S(2)}, u32[]{:S(2)}) collective-permute-start(f32[8,256]{1,0:T(8,128)S(1)} %get-tuple-element.46.refs_0_), channel_id=1, source_target_pairs={{0,12},{4,8},{8,4},{12,0},{1,13},{5,9},{9,5},{13,1},{2,14},{6,10},... | collective-permute-start | bytes 24584 | tf_op jit(solution)/shard_map/ppermute | solution.py:444
  54.4 0.5 collective-permute-start.13
  54.9 0.3 collective-permute-start.12
  55.2 3.6 %collective-permute-done.6.came = s16[1040,128]{1,0:T(8,128)(2,1)S(1)} collective-permute-done((s16[1040,128]{1,0:T(8,128)(2,1)S(1)}, s16[1040,128]{1,0:T(8,128)(2,1)S(1)}, u32[]{:S(2)}, u32[]{:S(2)}) %collective-permute-start.6) | collective-permute-done | bytes 266272 | tf_op jit(solution)/shard_map/ppermute | solution.py:424
  58.8 0.1 shard_map.66
  58.9 1.2 %collective-permute-start.9 = (f32[8,256]{1,0:T(8,128)S(1)}, f32[8,256]{1,0:T(8,128)S(1)}, u32[]{:S(2)}, u32[]{:S(2)}) collective-permute-start(f32[8,256]{1,0:T(8,128)S(1)} %get-tuple-element.43.refs_0_), channel_id=1, source_target_pairs={{0,12},{4,8},{8,4},{12,0},{1,13},{5,9},{9,5},{13,1},{2,14},{6,10},... | collective-permute-start | bytes 24584 | tf_op jit(solution)/shard_map/ppermute | solution.py:444
  60.1 0.5 collective-permute-start.8
  60.6 0.0 collective-permute-done.14.refs_3_
  60.6 0.2 collective-permute-start.7
  60.8 0.7 %shard_map.71 = s32[4]{0:T(128)} custom-call(s32[16,128]{1,0:T(8,128)S(1)} %get-tuple-element.47.own_load, s16[1040,128]{1,0:T(8,128)(2,1)S(1)} %collective-permute-done.11.came), custom_call_target="tpu_custom_call" | custom-call | bytes 274448 | tf_op jit(solution)/shard_map/pallas_call | solution.py:312
  61.5 0.0 collective-permute-done.13.refs_2_
  61.6 0.0 collective-permute-done.12.refs_1_
  61.6 0.8 %shard_map.69.refs_4_ = f32[512,512]{1,0:T(8,128)} custom-call(f32[512,256]{1,0:T(8,128)S(1)} %get-tuple-element.45.inflated, f32[8,256]{1,0:T(8,128)S(1)} %get-tuple-element.46.refs_0_, f32[8,256]{1,0:T(8,128)S(1)} %collective-permute-done.12.refs_1_, f32[8,256]{1,0:T(8,128)S(1)} %collective-permute-done.13.refs_2_, ...), custom_call_target="tpu_custom_call" | custom-call | bytes 1605632 | tf_op jit(solution)/shard_map/pallas_call | solution.py:312
  62.4 0.0 collective-permute-done.9.refs_3_
  62.4 1.3 %collective-permute-done.8.refs_2_ = f32[8,256]{1,0:T(8,128)S(1)} collective-permute-done((f32[8,256]{1,0:T(8,128)S(1)}, f32[8,256]{1,0:T(8,128)S(1)}, u32[]{:S(2)}, u32[]{:S(2)}) %collective-permute-start.8) | collective-permute-done | bytes 8224 | tf_op jit(solution)/shard_map/ppermute | solution.py:444
  63.8 0.0 collective-permute-done.7.refs_1_
  63.8 0.8 %shard_map.70 = f32[512,512]{1,0:T(8,128)} custom-call(f32[512,256]{1,0:T(8,128)S(1)} %get-tuple-element.42.inflated, f32[8,256]{1,0:T(8,128)S(1)} %get-tuple-element.43.refs_0_, f32[8,256]{1,0:T(8,128)S(1)} %collective-permute-done.7.refs_1_, f32[8,256]{1,0:T(8,128)S(1)} %collective-permute-done.8.refs_2_, ...), custom_call_target="tpu_custom_call", output_to_operand_aliasing={{}: (5, {})} | custom-call | bytes 2654208 | tf_op jit(solution)/shard_map/pallas_call | solution.py:312
Async XLA Ops:
  0.6 3.1 %collective-permute-start.1 = (bf16[16,1,128,128]{3,2,1,0:T(8,128)(2,1)}, bf16[16,1,128,128]{3,2,1,0:T(8,128)(2,1)S(1)}, u32[]{:S(2)}, u32[]{:S(2)}) collective-permute-start(bf16[16,1,128,128]{3,2,1,0:T(8,128)(2,1)} %own.1), channel_id=1, source_target_pairs={{0,4},{4,0},{8,12},{12,8},{1,5},{5,1},{9,13},{13,9},{2,6},{6,2},{1... | collective-permute-start | bytes 1572872 | tf_op jit(solution)/shard_map/ppermute | solution.py:350
  1.1 15.3 %collective-permute-start = (bf16[16,1,128,128]{3,2,1,0:T(8,128)(2,1)}, bf16[16,1,128,128]{3,2,1,0:T(8,128)(2,1)S(1)}, u32[]{:S(2)}, u32[]{:S(2)}) collective-permute-start(bf16[16,1,128,128]{3,2,1,0:T(8,128)(2,1)} %own.1), channel_id=1, source_target_pairs={{0,8},{4,12},{8,0},{12,4},{1,9},{5,13},{9,1},{13,5},{2,10},{6,14},... | collective-permute-start | bytes 1572872 | tf_op jit(solution)/shard_map/ppermute | solution.py:349
  3.7 1.6 %copy-start = (bf16[512,2048]{1,0:T(8,128)(2,1)S(1)}, bf16[512,2048]{1,0:T(8,128)(2,1)}, u32[]{:S(2)}) copy-start(bf16[512,2048]{1,0:T(8,128)(2,1)} %operand.1) | copy-start | bytes 6291460
  5.3 1.0 %copy-start.1 = (bf16[16,1,128,128]{3,2,1,0:T(8,128)(2,1)S(1)}, bf16[16,1,128,128]{3,2,1,0:T(8,128)(2,1)}, u32[]{:S(2)}) copy-start(bf16[16,1,128,128]{3,2,1,0:T(8,128)(2,1)} %own.1) | copy-start | bytes 1572868
  6.4 0.7 %copy-start.2 = (s32[16,4]{0,1:T(4,128)S(1)}, s32[16,4]{0,1:T(4,128)}, u32[]{:S(2)}) copy-start(s32[16,4]{0,1:T(4,128)} %param.6) | copy-start | bytes 772
  7.1 0.7 %copy-start.3 = (s32[16]{0:T(128)S(1)}, s32[16]{0:T(128)}, u32[]{:S(2)}) copy-start(s32[16]{0:T(128)} %counts.1) | copy-start | bytes 196
  16.5 1.9 %collective-permute-start.2 = (bf16[16,1,128,128]{3,2,1,0:T(8,128)(2,1)S(1)}, bf16[16,1,128,128]{3,2,1,0:T(8,128)(2,1)S(1)}, u32[]{:S(2)}, u32[]{:S(2)}) collective-permute-start(bf16[16,1,128,128]{3,2,1,0:T(8,128)(2,1)S(1)} %collective-permute-done.held.refs_2_), channel_id=1, source_target_pairs={{0,4},{4,0},{8,12},{12,8},{1,5},{5,1},{9,13},{13,9},{2,6},{6,2},{1... | collective-permute-start | bytes 1572872 | tf_op jit(solution)/shard_map/ppermute | solution.py:368
  19.8 15.3 %collective-permute-start.3 = (s16[2064,128]{1,0:T(8,128)(2,1)S(1)}, s16[2064,128]{1,0:T(8,128)(2,1)S(1)}, u32[]{:S(2)}, u32[]{:S(2)}) collective-permute-start(s16[2064,128]{1,0:T(8,128)(2,1)S(1)} %shard_map.61), channel_id=1, source_target_pairs={{0,2},{1,0},{2,3},{3,1},{4,6},{5,4},{6,7},{7,5},{8,10},{9,8},{10,1... | collective-permute-start | bytes 1585160 | tf_op jit(solution)/shard_map/ppermute | solution.py:389
  25.2 21.3 %collective-permute-start.5 = (s16[2064,128]{1,0:T(8,128)(2,1)S(1)}, s16[2064,128]{1,0:T(8,128)(2,1)S(1)}, u32[]{:S(2)}, u32[]{:S(2)}) collective-permute-start(s16[2064,128]{1,0:T(8,128)(2,1)S(1)} %get-tuple-element.35), channel_id=1, source_target_pairs={{0,4},{1,2},{2,1},{3,7},{4,0},{5,6},{6,5},{7,3},{8,12},{9,10},{10,... | collective-permute-start | bytes 1585160 | tf_op jit(solution)/shard_map/ppermute | solution.py:403
  25.3 15.5 %collective-permute-start.10 = (s16[1040,128]{1,0:T(8,128)(2,1)S(1)}, s16[1040,128]{1,0:T(8,128)(2,1)S(1)}, u32[]{:S(2)}, u32[]{:S(2)}) collective-permute-start(s16[1040,128]{1,0:T(8,128)(2,1)S(1)} %get-tuple-element.44), channel_id=1, source_target_pairs={{0,1},{1,0},{2,3},{3,2},{4,5},{5,4},{6,7},{7,6},{8,9},{9,8},{10,11... | collective-permute-start | bytes 798728 | tf_op jit(solution)/shard_map/ppermute | solution.py:402
  27.4 19.1 %collective-permute-start.4 = (s16[1040,128]{1,0:T(8,128)(2,1)S(1)}, s16[1040,128]{1,0:T(8,128)(2,1)S(1)}, u32[]{:S(2)}, u32[]{:S(2)}) collective-permute-start(s16[1040,128]{1,0:T(8,128)(2,1)S(1)} %get-tuple-element.34), channel_id=1, source_target_pairs={{0,1},{1,0},{2,3},{3,2},{4,5},{5,4},{6,7},{7,6},{8,9},{9,8},{10,11... | collective-permute-start | bytes 798728 | tf_op jit(solution)/shard_map/ppermute | solution.py:402
  41.0 12.1 %collective-permute-start.11 = (s16[1040,128]{1,0:T(8,128)(2,1)S(1)}, s16[1040,128]{1,0:T(8,128)(2,1)S(1)}, u32[]{:S(2)}, u32[]{:S(2)}) collective-permute-start(s16[1040,128]{1,0:T(8,128)(2,1)S(1)} %shard_map.67), channel_id=1, source_target_pairs={{0,1},{1,3},{3,2},{2,0},{4,5},{5,7},{7,6},{6,4},{8,9},{9,11},{11,1... | collective-permute-start | bytes 798728 | tf_op jit(solution)/shard_map/ppermute | solution.py:424
  46.7 12.1 %collective-permute-start.6 = (s16[1040,128]{1,0:T(8,128)(2,1)S(1)}, s16[1040,128]{1,0:T(8,128)(2,1)S(1)}, u32[]{:S(2)}, u32[]{:S(2)}) collective-permute-start(s16[1040,128]{1,0:T(8,128)(2,1)S(1)} %shard_map.65), channel_id=1, source_target_pairs={{0,1},{1,3},{3,2},{2,0},{4,5},{5,7},{7,6},{6,4},{8,9},{9,11},{11,1... | collective-permute-start | bytes 798728 | tf_op jit(solution)/shard_map/ppermute | solution.py:424
  53.3 7.4 %collective-permute-start.14 = (f32[8,256]{1,0:T(8,128)S(1)}, f32[8,256]{1,0:T(8,128)S(1)}, u32[]{:S(2)}, u32[]{:S(2)}) collective-permute-start(f32[8,256]{1,0:T(8,128)S(1)} %get-tuple-element.46.refs_0_), channel_id=1, source_target_pairs={{0,12},{4,8},{8,4},{12,0},{1,13},{5,9},{9,5},{13,1},{2,14},{6,10},... | collective-permute-start | bytes 24584 | tf_op jit(solution)/shard_map/ppermute | solution.py:444
  54.4 7.1 %collective-permute-start.13 = (f32[8,256]{1,0:T(8,128)S(1)}, f32[8,256]{1,0:T(8,128)S(1)}, u32[]{:S(2)}, u32[]{:S(2)}) collective-permute-start(f32[8,256]{1,0:T(8,128)S(1)} %get-tuple-element.46.refs_0_), channel_id=1, source_target_pairs={{0,8},{4,12},{8,0},{12,4},{1,9},{5,13},{9,1},{13,5},{2,10},{6,14},... | collective-permute-start | bytes 24584 | tf_op jit(solution)/shard_map/ppermute | solution.py:444
  54.9 6.6 %collective-permute-start.12 = (f32[8,256]{1,0:T(8,128)S(1)}, f32[8,256]{1,0:T(8,128)S(1)}, u32[]{:S(2)}, u32[]{:S(2)}) collective-permute-start(f32[8,256]{1,0:T(8,128)S(1)} %get-tuple-element.46.refs_0_), channel_id=1, source_target_pairs={{0,4},{4,0},{8,12},{12,8},{1,5},{5,1},{9,13},{13,9},{2,6},{6,2},{1... | collective-permute-start | bytes 24584 | tf_op jit(solution)/shard_map/ppermute | solution.py:444
  58.9 3.5 %collective-permute-start.9 = (f32[8,256]{1,0:T(8,128)S(1)}, f32[8,256]{1,0:T(8,128)S(1)}, u32[]{:S(2)}, u32[]{:S(2)}) collective-permute-start(f32[8,256]{1,0:T(8,128)S(1)} %get-tuple-element.43.refs_0_), channel_id=1, source_target_pairs={{0,12},{4,8},{8,4},{12,0},{1,13},{5,9},{9,5},{13,1},{2,14},{6,10},... | collective-permute-start | bytes 24584 | tf_op jit(solution)/shard_map/ppermute | solution.py:444
  60.1 3.7 %collective-permute-start.8 = (f32[8,256]{1,0:T(8,128)S(1)}, f32[8,256]{1,0:T(8,128)S(1)}, u32[]{:S(2)}, u32[]{:S(2)}) collective-permute-start(f32[8,256]{1,0:T(8,128)S(1)} %get-tuple-element.43.refs_0_), channel_id=1, source_target_pairs={{0,8},{4,12},{8,0},{12,4},{1,9},{5,13},{9,1},{13,5},{2,10},{6,14},... | collective-permute-start | bytes 24584 | tf_op jit(solution)/shard_map/ppermute | solution.py:444
  60.6 3.2 %collective-permute-start.7 = (f32[8,256]{1,0:T(8,128)S(1)}, f32[8,256]{1,0:T(8,128)S(1)}, u32[]{:S(2)}, u32[]{:S(2)}) collective-permute-start(f32[8,256]{1,0:T(8,128)S(1)} %get-tuple-element.43.refs_0_), channel_id=1, source_target_pairs={{0,4},{4,0},{8,12},{12,8},{1,5},{5,1},{9,13},{13,9},{2,6},{6,2},{1... | collective-permute-start | bytes 24584 | tf_op jit(solution)/shard_map/ppermute | solution.py:444

commit v6 on v5

--- a/solution.py
+++ b/solution.py
@@ -26,6 +26,11 @@
 
 def blocks_of(part):
     return ALL[part * SLAB_DEV // PARTS : (part + 1) * SLAB_DEV // PARTS]
+
+
+def is_inner():
+    place = lax.axis_index("col")
+    return (place == 1) | (place == 2)
 
 
 def code_scale(values):
@@ -139,8 +144,11 @@
     for copy in copies:
         copy.wait()
     total[...] = jnp.zeros_like(total)
-    for place, held in enumerate((own_near, twin)):
-        add_terms(plan, which(lax.axis_index("col")), place, held, total, operand_near)
+
+    @pl.when(jnp.logical_not(is_inner()))
+    def _():
+        for place, held in enumerate((own_near, twin)):
+            add_terms(plan, which(lax.axis_index("col")), place, held, total, operand_near)
 
 
 def add_terms(plan, shard, place, held, total, operand):
@@ -164,15 +172,24 @@
 
 
 def go_on(which, place, plan_ref, operand, held, _, total):
-    add_terms(plan_of(plan_ref, operand), which(lax.axis_index("col")), place, held, total, operand)
+    @pl.when(jnp.logical_not(is_inner()))
+    def _():
+        add_terms(plan_of(plan_ref, operand), which(lax.axis_index("col")), place, held, total, operand)
 
 
 def code_sum(which, place, plan_ref, operand, held, total, out):
     plan = plan_of(plan_ref, operand)
     shard = which(lax.axis_index("col"))
-    add_terms(plan, shard, place, held, total, operand)
-    values = [(b, lambda b=b: total[:, lanes_of(b)]) for b in range(SLAB_DEV)]
-    put_coded([(out, ALL)], values, counts_of(plan, shard))
+
+    @pl.when(is_inner())
+    def _():
+        out[...] = jnp.zeros_like(out)
+
+    @pl.when(jnp.logical_not(is_inner()))
+    def _():
+        add_terms(plan, shard, place, held, total, operand)
+        values = [(b, lambda b=b: total[:, lanes_of(b)]) for b in range(SLAB_DEV)]
+        put_coded([(out, ALL)], values, counts_of(plan, shard))
 
 
 def fill(slab, plan, shard, blocks):
@@ -205,8 +222,8 @@
     lax.fori_loop(0, width // TILE, step, 0)
 
 
-def coded_product(which, nblocks, plan_ref, operand, *refs):
-    blocks, (whole, *parts, slab) = refs[:nblocks], refs[nblocks:]
+def coded_product(which, helds, nblocks, plan_ref, operand, *refs):
+    blocks, (*outs, slab) = refs[:nblocks], refs[nblocks:]
     plan = plan_of(plan_ref, operand)
     shard = which(lax.axis_index("col"))
     fill(slab, plan, shard, blocks)
@@ -219,8 +236,7 @@
             done[tile] = jnp.dot(operand[...], slab[:, lanes], preferred_element_type=jnp.float32)
         return done[tile][:, at : at + SIDE]
 
-    outs = [(whole, ALL)] + [(part, blocks_of(j)) for j, part in enumerate(parts)]
-    put_coded(outs, [(b, functools.partial(values, b)) for b in ALL], counts_of(plan, shard))
+    put_coded(list(zip(outs, helds)), [(b, functools.partial(values, b)) for b in ALL], counts_of(plan, shard))
 
 
 def plain_products(plain, nblocks, plan_ref, operand, *refs):
@@ -239,8 +255,7 @@
 
 
 def relay(part, own, own_load, came, out):
-    place = lax.axis_index("col")
-    inner = (place == 1) | (place == 2)
+    inner = is_inner()
     held, rows = blocks_of(part), own.shape[0]
 
     @pl.when(inner)
@@ -256,20 +271,25 @@
         put_coded([(out, held)], [(b, lambda b=b: own[:, lanes_of(b)]) for b in held], own_load[...])
 
 
-def settle(own, own_load, came_b, came_f, out, out_load):
-    place = lax.axis_index("col")
-    inner = (place == 1) | (place == 2)
-    rows, head = own.shape[0], head_of(came_f)
-    out_load[...] = own_load[...] + head
-    for b in ALL:
-        out[:, lanes_of(b)] = own[:, lanes_of(b)] + decode(came_f, head, b, rows)
-
-    @pl.when(inner)
-    def _():
-        head = head_of(came_b)
-        out_load[...] = out_load[...] + head
+def settle(own, own_load, *refs):
+    *came_a, came_b, came_f, out, out_load = refs
+    rows = own.shape[0]
+
+    @pl.when(is_inner())
+    def _():
+        head_b, head_f = head_of(came_b), head_of(came_f)
+        out_load[...] = own_load[...] + head_b + head_f
         for b in ALL:
-            out[:, lanes_of(b)] = out[:, lanes_of(b)] + decode(came_b, head, b, rows)
+            came = decode(came_b, head_b, b, rows) + decode(came_f, head_f, b, rows)
+            out[:, lanes_of(b)] = own[:, lanes_of(b)] + came
+
+    @pl.when(jnp.logical_not(is_inner()))
+    def _():
+        out_load[...] = own_load[...] + head_of(came_a[0])
+        for part, came in enumerate(came_a):
+            head = head_of(came)
+            for at, b in enumerate(blocks_of(part)):
+                out[:, lanes_of(b)] = own[:, lanes_of(b)] + decode(came, head, at, rows)
 
 
 def inflate(part, own, came, out, totals):
@@ -337,19 +357,22 @@
         return [(a, ((a // 2 + by) % ny) * 2 + a % 2) for a in range(2 * ny)]
 
     def first(z):
-        return 3 - z
+        return jnp.where(z == 0, 2, 1)
 
     def second(z):
-        return jnp.where(z == 0, 2, jnp.where(z == 1, 0, jnp.where(z == 2, 3, 1)))
+        return jnp.where(lax.rem(z, 2) == 0, 3, 0)
+
+    def inner(z):
+        return jnp.where(z < 2, 2, 1)
 
     def third(z):
-        return 3 - second(z)
+        return jnp.where(z == 0, 1, jnp.where(z == 1, 3, jnp.where(z == 2, 0, 2)))
 
     flops = 2 * rows * depth * width
     turned = [lax.ppermute(slot_blocks, "row", turn(by)) for by in range(1, ny)]
     twin = lax.ppermute(slot_blocks, "row", swap)
     plan, operand_near, own_near, total = call(
-        functools.partial(begin, ny, second),
+        functools.partial(begin, ny, first),
         [slot_columns.T, live_counts, operand_panel, slot_blocks, twin],
         [
             i32((Plan(None, here, slots, shards).size,)),
@@ -368,7 +391,7 @@
     blocks += [x for came in turned for x in (came, lax.ppermute(came, "row", swap))]
     for place in range(2, slots - 1):
         [total] = call(
-            functools.partial(go_on, second, place),
+            functools.partial(go_on, first, place),
             [plan, operand_near, blocks[place], total],
             [f32((rows, width))],
             [VMEM],
@@ -378,7 +401,7 @@
             onto={3: 0},
         )
     [send_f] = call(
-        functools.partial(code_sum, second, slots - 1),
+        functools.partial(code_sum, first, slots - 1),
         [plan, operand_near, blocks[-1], total],
         [coded],
         [VMEM],
@@ -390,16 +413,19 @@
     ins = [plan, operand_near, *blocks]
     slab = [pltpu.VMEM((depth, width), jnp.bfloat16)]
     part_coded = jax.ShapeDtypeStruct((SLAB_DEV // PARTS * rows + HEAD, SIDE), jnp.int16)
-    send_b, *send_a = call(
-        functools.partial(coded_product, first, len(blocks)),
+    send_a = call(
+        functools.partial(coded_product, second, [blocks_of(j) for j in range(PARTS)], len(blocks)),
         ins,
-        [coded] + [part_coded] * PARTS,
-        [VMEM] * (1 + PARTS),
+        [part_coded] * PARTS,
+        [VMEM] * PARTS,
         slab,
         flops,
         1,
     )
     came_a = [lax.ppermute(one, "col", [(0, 1), (1, 0), (2, 3), (3, 2)]) for one in send_a]
+    [send_b] = call(
+        functools.partial(coded_product, inner, [ALL], len(blocks)), ins, [coded], [VMEM], slab, flops, 1
+    )
     came_b = lax.ppermute(
         send_b,
         ("row", "col"),
@@ -423,7 +449,7 @@
         )
         came_t.append(lax.ppermute(send_t, "col", [(0, 1), (1, 3), (3, 2), (2, 0)]))
     own, own_load = call(
-        settle, [own, own_load, came_b, came_f], [f32((rows, width)), i32((HEAD, SIDE))], [VMEM] * 2
+        settle, [own, own_load, *came_a, came_b, came_f], [f32((rows, width)), i32((HEAD, SIDE))], [VMEM] * 2
     )
     all_rows = rows * lax.axis_size("row")
     hbm = pl.BlockSpec(memory_space=pl.ANY)

time: 64.8 us -> 64.8 us (level)
  waiting for transfers between devices: 26.6 us -> 23.3 us
  Pallas kernels: 16 us -> 18.8 us
    ppermute x1, waiting for transfers between devices: 7.66 us -> 4.41 us  [body_line(): came_f = lax.ppermute(send_f, 'col', [(0, 2), (1, 0), (2, 3), (3, 1)])]
    pallas_call x13 -> x14, Pallas kernels: 16 us -> 18.8 us  [call(): pl.pallas_call(kernel, in_specs=[SMEM] * few + [pl.BlockSpec(memory_space...]
    ppermute x1, waiting for transfers between devices: 4.85 us -> 3.96 us  [body_line(): turned = [lax.ppermute(slot_blocks, 'row', turn(by)) for by in range(1, ny)]]
    ppermute x2, starting transfers between devices: 2.17 us -> 2.99 us  [body_line(): lax.ppermute(one, 'col', [(0, 1), (1, 0), (2, 3), (3, 2)])]
    ppermute x2, waiting for transfers between devices: 7.26 us -> 7.96 us  [body_line(): came_t.append(lax.ppermute(send_t, 'col', [(0, 1), (1, 3), (3, 2), (2, 0)]))]
  transfers between devices with their start and end apart: 15 -> 15, of which waited for: 8 -> 8; matrix products, arithmetic and copies ran while one was open for 0% -> 0% of each run, Pallas kernels for 21% -> 26%
where the time goes in v6:
time: 64.8 us; the launch traced here: 64.6 us
  waiting for transfers between devices  23.3 us (36%)
  Pallas kernels  18.8 us (29%)
  starting transfers between devices  17.7 us (27%)
  local copies, waits for them, and re-layouts  3.97 us (6%)
  between operations  0.77 us (1%)
    pallas_call x14, Pallas kernels, call(): pl.pallas_call(kernel, in_specs=[SMEM] * few + [pl.BlockSpec(memory_space...  18.8 us
    ppermute x2, waiting for transfers between devices, body_line(): came_t.append(lax.ppermute(send_t, 'col', [(0, 1), (1, 3), (3, 2), (2, 0)]))  7.96 us
    ppermute x2, starting transfers between devices, body_line(): came_t.append(lax.ppermute(send_t, 'col', [(0, 1), (1, 3), (3, 2), (2, 0)]))  5.16 us
    ppermute x2, waiting for transfers between devices, body_line(): lax.ppermute(one, 'col', [(0, 1), (1, 0), (2, 3), (3, 2)])  4.69 us
    ppermute x1, waiting for transfers between devices, body_line(): came_f = lax.ppermute(send_f, 'col', [(0, 2), (1, 0), (2, 3), (3, 1)])  4.41 us
    unnamed x8, local copies, waits for them, and re-layouts  3.97 us
    ppermute x1, waiting for transfers between devices, body_line(): turned = [lax.ppermute(slot_blocks, 'row', turn(by)) for by in range(1, ny)]  3.96 us
    ppermute x6, starting transfers between devices, body_line(): others.append(lax.ppermute(totals, 'row', pairs))  3.84 us
  transfers between devices with their start and end apart: 15, of which 8 were waited for; matrix products, arithmetic and copies ran while one was open for 0% of the time, Pallas kernels for 26%

profile of v6, /device:TPU:0, one launch (start us, length us, event | category | flops | bytes accessed | tf_op | source)
XLA Modules:
  0.0 64.6 jit_solution(14837443373790084891)
XLA Ops:
  0.6 0.5 collective-permute-start.1
  1.1 2.6 %collective-permute-start = (bf16[16,1,128,128]{3,2,1,0:T(8,128)(2,1)}, bf16[16,1,128,128]{3,2,1,0:T(8,128)(2,1)S(1)}, u32[]{:S(2)}, u32[]{:S(2)}) collective-permute-start(bf16[16,1,128,128]{3,2,1,0:T(8,128)(2,1)} %own.1), channel_id=1, source_target_pairs={{0,8},{4,12},{8,0},{12,4},{1,9},{5,13},{9,1},{13,5},{2,10},{6,14},... | collective-permute-start | bytes 1572872 | tf_op jit(solution)/shard_map/ppermute | solution.py:372
  3.7 0.0 collective-permute-done.1.twin.refs_1_
  3.7 0.0 copy-start
  3.7 1.6 %copy-done = bf16[512,2048]{1,0:T(8,128)(2,1)S(1)} copy-done((bf16[512,2048]{1,0:T(8,128)(2,1)S(1)}, bf16[512,2048]{1,0:T(8,128)(2,1)}, u32[]{:S(2)}) %copy-start) | copy-done | bytes 2097176
  5.3 0.0 copy-start.1
  5.3 1.0 %copy-done.1 = bf16[16,1,128,128]{3,2,1,0:T(8,128)(2,1)S(1)} copy-done((bf16[16,1,128,128]{3,2,1,0:T(8,128)(2,1)S(1)}, bf16[16,1,128,128]{3,2,1,0:T(8,128)(2,1)}, u32[]{:S(2)}) %copy-start.1) | copy-done | bytes 524312
  6.4 0.0 copy-start.2
  6.4 0.7 %copy-done.2 = s32[16,4]{0,1:T(4,128)S(1)} copy-done((s32[16,4]{0,1:T(4,128)S(1)}, s32[16,4]{0,1:T(4,128)}, u32[]{:S(2)}) %copy-start.2) | copy-done | bytes 280
  7.1 0.0 copy-start.3
  7.1 0.7 %copy-done.3 = s32[16]{0:T(128)S(1)} copy-done((s32[16]{0:T(128)S(1)}, s32[16]{0:T(128)}, u32[]{:S(2)}) %copy-start.3) | copy-done | bytes 88
  7.7 4.8 %shard_map.59 = (s32[288]{0:T(512)S(1)}, bf16[512,2048]{1,0:T(8,128)(2,1)S(1)}, bf16[16,1,128,128]{3,2,1,0:T(8,128)(2,1)S(1)}, f32[512,512]{1,0:T(8,128)S(1)}) custom-call(s32[4,16]{1,0:T(4,128)S(1)} %bitcast.1, s32[16]{0:T(128)S(1)} %copy-done.3, bf16[512,2048]{1,0:T(8,128)(2,1)S(1)} %copy-done, bf16[16,1,128,128]{3,2,1,0:T(8,128)(2,1)S(1)} %copy-done.1, ...), custom_call_target="tpu_custom_call" | custom-call | flops 268435456 | bytes 6817216 | tf_op jit(solution)/shard_map/pallas_call | solution.py:332
  12.5 4.0 %collective-permute-done.held.refs_2_ = bf16[16,1,128,128]{3,2,1,0:T(8,128)(2,1)S(1)} collective-permute-done((bf16[16,1,128,128]{3,2,1,0:T(8,128)(2,1)}, bf16[16,1,128,128]{3,2,1,0:T(8,128)(2,1)S(1)}, u32[]{:S(2)}, u32[]{:S(2)}) %collective-permute-start) | collective-permute-done | bytes 524320 | tf_op jit(solution)/shard_map/ppermute | solution.py:372
  16.5 0.0 collective-permute-start.2
  16.5 1.0 %shard_map.60.total = f32[512,512]{1,0:T(8,128)S(1)} custom-call(s32[288]{0:T(512)S(1)} %get-tuple-element.29.plan_ref, bf16[512,2048]{1,0:T(8,128)(2,1)S(1)} %get-tuple-element.26.operand, bf16[16,1,128,128]{3,2,1,0:T(8,128)(2,1)S(1)} %collective-permute-done.held.refs_2_, f32[512,512]{1,0:T(8,128)S(1)} %get-tuple-element.28._), custom_call_target="tpu_custom_call", output_to_operand_aliasing={{}: (3, {})} | custom-call | flops 134217728 | bytes 4719744 | tf_op jit(solution)/shard_map/pallas_call | solution.py:332
  17.5 0.9 %collective-permute-done.2.held.refs_3_ = bf16[16,1,128,128]{3,2,1,0:T(8,128)(2,1)S(1)} collective-permute-done((bf16[16,1,128,128]{3,2,1,0:T(8,128)(2,1)S(1)}, bf16[16,1,128,128]{3,2,1,0:T(8,128)(2,1)S(1)}, u32[]{:S(2)}, u32[]{:S(2)}) %collective-permute-start.2) | collective-permute-done | bytes 524320 | tf_op jit(solution)/shard_map/ppermute | solution.py:391
  18.4 1.0 %shard_map.61 = s16[2064,128]{1,0:T(8,128)(2,1)S(1)} custom-call(s32[288]{0:T(512)S(1)} %get-tuple-element.29.plan_ref, bf16[512,2048]{1,0:T(8,128)(2,1)S(1)} %get-tuple-element.26.operand, bf16[16,1,128,128]{3,2,1,0:T(8,128)(2,1)S(1)} %collective-permute-done.2.held.refs_3_, f32[512,512]{1,0:T(8,128)S(1)} %shard_map.60.total), custom_call_target="tpu_custom_call" | custom-call | flops 134217728 | bytes 4199552 | tf_op jit(solution)/shard_map/pallas_call | solution.py:332
  19.3 2.6 %collective-permute-start.3 = (s16[2064,128]{1,0:T(8,128)(2,1)S(1)}, s16[2064,128]{1,0:T(8,128)(2,1)S(1)}, u32[]{:S(2)}, u32[]{:S(2)}) collective-permute-start(s16[2064,128]{1,0:T(8,128)(2,1)S(1)} %shard_map.61), channel_id=1, source_target_pairs={{0,2},{1,0},{2,3},{3,1},{4,6},{5,4},{6,7},{7,5},{8,10},{9,8},{10,1... | collective-permute-start | bytes 1585160 | tf_op jit(solution)/shard_map/ppermute | solution.py:412
  21.9 2.5 %shard_map.64 = s16[2064,128]{1,0:T(8,128)(2,1)S(1)} custom-call(s32[288]{0:T(512)S(1)} %get-tuple-element.29.plan_ref, bf16[512,2048]{1,0:T(8,128)(2,1)S(1)} %get-tuple-element.26.operand, bf16[16,1,128,128]{3,2,1,0:T(8,128)(2,1)S(1)} %get-tuple-element.30.refs_0_, bf16[16,1,128,128]{3,2,1,0:T(8,128)(2,1)S(1)} %collective-permute-done.1.twin.refs_1_, ...), custom_call_target="tpu_custom_call" | custom-call | flops 1073741824 | bytes 4723840 | tf_op jit(solution)/shard_map/pallas_call | solution.py:332
  24.4 0.1 collective-permute-start.6
  24.5 2.4 %shard_map.63 = (s16[1040,128]{1,0:T(8,128)(2,1)S(1)}, s16[1040,128]{1,0:T(8,128)(2,1)S(1)}) custom-call(s32[288]{0:T(512)S(1)} %get-tuple-element.29.plan_ref, bf16[512,2048]{1,0:T(8,128)(2,1)S(1)} %get-tuple-element.26.operand, bf16[16,1,128,128]{3,2,1,0:T(8,128)(2,1)S(1)} %get-tuple-element.30.refs_0_, ...), custom_call_target="tpu_custom_call" | custom-call | flops 1073741824 | bytes 4727936 | tf_op jit(solution)/shard_map/pallas_call | solution.py:332
  26.9 2.9 %collective-permute-start.4 = (s16[1040,128]{1,0:T(8,128)(2,1)S(1)}, s16[1040,128]{1,0:T(8,128)(2,1)S(1)}, u32[]{:S(2)}, u32[]{:S(2)}) collective-permute-start(s16[1040,128]{1,0:T(8,128)(2,1)S(1)} %get-tuple-element.33), channel_id=1, source_target_pairs={{0,1},{1,0},{2,3},{3,2},{4,5},{5,4},{6,7},{7,6},{8,9},{9,8},{10,11... | collective-permute-start | bytes 798728 | tf_op jit(solution)/shard_map/ppermute | solution.py:425
  29.8 0.1 collective-permute-start.5
  29.9 4.4 %collective-permute-done.3.refs_3_ = s16[2064,128]{1,0:T(8,128)(2,1)S(1)} collective-permute-done((s16[2064,128]{1,0:T(8,128)(2,1)S(1)}, s16[2064,128]{1,0:T(8,128)(2,1)S(1)}, u32[]{:S(2)}, u32[]{:S(2)}) %collective-permute-start.3) | collective-permute-done | bytes 528416 | tf_op jit(solution)/shard_map/ppermute | solution.py:412
  34.3 3.9 %shard_map.62 = (f32[512,512]{1,0:T(8,128)S(1)}, f32[512,512]{1,0:T(8,128)S(1)}, s32[16,128]{1,0:T(8,128)S(1)}, s32[16,128]{1,0:T(8,128)S(1)}) custom-call(s32[288]{0:T(512)S(1)} %get-tuple-element.29.plan_ref, bf16[512,2048]{1,0:T(8,128)(2,1)S(1)} %get-tuple-element.26.operand, bf16[16,1,128,128]{3,2,1,0:T(8,128)(2,1)S(1)} %get-tuple-element.30.refs_0_, ...), custom_call_target="tpu_custom_call" | custom-call | flops 2147483648 | bytes 6308992 | tf_op jit(solution)/shard_map/pallas_call | solution.py:332
  38.3 1.8 %collective-permute-done.4.refs_0_.came = s16[1040,128]{1,0:T(8,128)(2,1)S(1)} collective-permute-done((s16[1040,128]{1,0:T(8,128)(2,1)S(1)}, s16[1040,128]{1,0:T(8,128)(2,1)S(1)}, u32[]{:S(2)}, u32[]{:S(2)}) %collective-permute-start.4) | collective-permute-done | bytes 266272 | tf_op jit(solution)/shard_map/ppermute | solution.py:425
  40.0 0.2 shard_map.68
  40.2 2.6 %collective-permute-start.11 = (s16[1040,128]{1,0:T(8,128)(2,1)S(1)}, s16[1040,128]{1,0:T(8,128)(2,1)S(1)}, u32[]{:S(2)}, u32[]{:S(2)}) collective-permute-start(s16[1040,128]{1,0:T(8,128)(2,1)S(1)} %shard_map.68), channel_id=1, source_target_pairs={{0,1},{1,3},{3,2},{2,0},{4,5},{5,7},{7,6},{6,4},{8,9},{9,11},{11,1... | collective-permute-start | bytes 798728 | tf_op jit(solution)/shard_map/ppermute | solution.py:450
  42.8 2.9 %collective-permute-done.5.refs_1_.came = s16[1040,128]{1,0:T(8,128)(2,1)S(1)} collective-permute-done((s16[1040,128]{1,0:T(8,128)(2,1)S(1)}, s16[1040,128]{1,0:T(8,128)(2,1)S(1)}, u32[]{:S(2)}, u32[]{:S(2)}) %collective-permute-start.5) | collective-permute-done | bytes 266272 | tf_op jit(solution)/shard_map/ppermute | solution.py:425
  45.7 0.0 collective-permute-done.6.refs_2_
  45.7 0.2 shard_map.66
  45.9 2.6 %collective-permute-start.7 = (s16[1040,128]{1,0:T(8,128)(2,1)S(1)}, s16[1040,128]{1,0:T(8,128)(2,1)S(1)}, u32[]{:S(2)}, u32[]{:S(2)}) collective-permute-start(s16[1040,128]{1,0:T(8,128)(2,1)S(1)} %shard_map.66), channel_id=1, source_target_pairs={{0,1},{1,3},{3,2},{2,0},{4,5},{5,7},{7,6},{6,4},{8,9},{9,11},{11,1... | collective-permute-start | bytes 798728 | tf_op jit(solution)/shard_map/ppermute | solution.py:450
  48.5 0.2 shard_map.65
  48.7 4.4 %collective-permute-done.11.came = s16[1040,128]{1,0:T(8,128)(2,1)S(1)} collective-permute-done((s16[1040,128]{1,0:T(8,128)(2,1)S(1)}, s16[1040,128]{1,0:T(8,128)(2,1)S(1)}, u32[]{:S(2)}, u32[]{:S(2)}) %collective-permute-start.11) | collective-permute-done | bytes 266272 | tf_op jit(solution)/shard_map/ppermute | solution.py:450
  53.1 0.1 shard_map.69
  53.2 1.2 %collective-permute-start.14 = (f32[8,256]{1,0:T(8,128)S(1)}, f32[8,256]{1,0:T(8,128)S(1)}, u32[]{:S(2)}, u32[]{:S(2)}) collective-permute-start(f32[8,256]{1,0:T(8,128)S(1)} %get-tuple-element.44.refs_0_), channel_id=1, source_target_pairs={{0,12},{4,8},{8,4},{12,0},{1,13},{5,9},{9,5},{13,1},{2,14},{6,10},... | collective-permute-start | bytes 24584 | tf_op jit(solution)/shard_map/ppermute | solution.py:470
  54.4 0.5 collective-permute-start.13
  54.9 0.3 collective-permute-start.12
  55.1 3.6 %collective-permute-done.7.came = s16[1040,128]{1,0:T(8,128)(2,1)S(1)} collective-permute-done((s16[1040,128]{1,0:T(8,128)(2,1)S(1)}, s16[1040,128]{1,0:T(8,128)(2,1)S(1)}, u32[]{:S(2)}, u32[]{:S(2)}) %collective-permute-start.7) | collective-permute-done | bytes 266272 | tf_op jit(solution)/shard_map/ppermute | solution.py:450
  58.7 0.1 shard_map.67
  58.8 1.2 %collective-permute-start.10 = (f32[8,256]{1,0:T(8,128)S(1)}, f32[8,256]{1,0:T(8,128)S(1)}, u32[]{:S(2)}, u32[]{:S(2)}) collective-permute-start(f32[8,256]{1,0:T(8,128)S(1)} %get-tuple-element.42.refs_0_), channel_id=1, source_target_pairs={{0,12},{4,8},{8,4},{12,0},{1,13},{5,9},{9,5},{13,1},{2,14},{6,10},... | collective-permute-start | bytes 24584 | tf_op jit(solution)/shard_map/ppermute | solution.py:470
  60.1 0.5 collective-permute-start.9
  60.6 0.0 collective-permute-done.14.refs_3_
  60.6 0.2 collective-permute-start.8
  60.8 0.7 %shard_map.72 = s32[4]{0:T(128)} custom-call(s32[16,128]{1,0:T(8,128)S(1)} %get-tuple-element.45.own_load, s16[1040,128]{1,0:T(8,128)(2,1)S(1)} %collective-permute-done.11.came), custom_call_target="tpu_custom_call" | custom-call | bytes 274448 | tf_op jit(solution)/shard_map/pallas_call | solution.py:332
  61.5 0.0 collective-permute-done.13.refs_2_
  61.5 0.0 collective-permute-done.12.refs_1_
  61.5 0.8 %shard_map.70.refs_4_ = f32[512,512]{1,0:T(8,128)} custom-call(f32[512,256]{1,0:T(8,128)S(1)} %get-tuple-element.43.inflated, f32[8,256]{1,0:T(8,128)S(1)} %get-tuple-element.44.refs_0_, f32[8,256]{1,0:T(8,128)S(1)} %collective-permute-done.12.refs_1_, f32[8,256]{1,0:T(8,128)S(1)} %collective-permute-done.13.refs_2_, ...), custom_call_target="tpu_custom_call" | custom-call | bytes 1605632 | tf_op jit(solution)/shard_map/pallas_call | solution.py:332
  62.4 0.0 collective-permute-done.10.refs_3_
  62.4 1.4 %collective-permute-done.9.refs_2_ = f32[8,256]{1,0:T(8,128)S(1)} collective-permute-done((f32[8,256]{1,0:T(8,128)S(1)}, f32[8,256]{1,0:T(8,128)S(1)}, u32[]{:S(2)}, u32[]{:S(2)}) %collective-permute-start.9) | collective-permute-done | bytes 8224 | tf_op jit(solution)/shard_map/ppermute | solution.py:470
  63.7 0.0 collective-permute-done.8.refs_1_
  63.7 0.8 %shard_map.71 = f32[512,512]{1,0:T(8,128)} custom-call(f32[512,256]{1,0:T(8,128)S(1)} %get-tuple-element.41.inflated, f32[8,256]{1,0:T(8,128)S(1)} %get-tuple-element.42.refs_0_, f32[8,256]{1,0:T(8,128)S(1)} %collective-permute-done.8.refs_1_, f32[8,256]{1,0:T(8,128)S(1)} %collective-permute-done.9.refs_2_, ...), custom_call_target="tpu_custom_call", output_to_operand_aliasing={{}: (5, {})} | custom-call | bytes 2654208 | tf_op jit(solution)/shard_map/pallas_call | solution.py:332
Async XLA Ops:
  0.6 3.1 %collective-permute-start.1 = (bf16[16,1,128,128]{3,2,1,0:T(8,128)(2,1)}, bf16[16,1,128,128]{3,2,1,0:T(8,128)(2,1)S(1)}, u32[]{:S(2)}, u32[]{:S(2)}) collective-permute-start(bf16[16,1,128,128]{3,2,1,0:T(8,128)(2,1)} %own.1), channel_id=1, source_target_pairs={{0,4},{4,0},{8,12},{12,8},{1,5},{5,1},{9,13},{13,9},{2,6},{6,2},{1... | collective-permute-start | bytes 1572872 | tf_op jit(solution)/shard_map/ppermute | solution.py:373
  1.1 15.3 %collective-permute-start = (bf16[16,1,128,128]{3,2,1,0:T(8,128)(2,1)}, bf16[16,1,128,128]{3,2,1,0:T(8,128)(2,1)S(1)}, u32[]{:S(2)}, u32[]{:S(2)}) collective-permute-start(bf16[16,1,128,128]{3,2,1,0:T(8,128)(2,1)} %own.1), channel_id=1, source_target_pairs={{0,8},{4,12},{8,0},{12,4},{1,9},{5,13},{9,1},{13,5},{2,10},{6,14},... | collective-permute-start | bytes 1572872 | tf_op jit(solution)/shard_map/ppermute | solution.py:372
  3.7 1.6 %copy-start = (bf16[512,2048]{1,0:T(8,128)(2,1)S(1)}, bf16[512,2048]{1,0:T(8,128)(2,1)}, u32[]{:S(2)}) copy-start(bf16[512,2048]{1,0:T(8,128)(2,1)} %operand.1) | copy-start | bytes 6291460
  5.3 1.0 %copy-start.1 = (bf16[16,1,128,128]{3,2,1,0:T(8,128)(2,1)S(1)}, bf16[16,1,128,128]{3,2,1,0:T(8,128)(2,1)}, u32[]{:S(2)}) copy-start(bf16[16,1,128,128]{3,2,1,0:T(8,128)(2,1)} %own.1) | copy-start | bytes 1572868
  6.4 0.7 %copy-start.2 = (s32[16,4]{0,1:T(4,128)S(1)}, s32[16,4]{0,1:T(4,128)}, u32[]{:S(2)}) copy-start(s32[16,4]{0,1:T(4,128)} %param.6) | copy-start | bytes 772
  7.1 0.7 %copy-start.3 = (s32[16]{0:T(128)S(1)}, s32[16]{0:T(128)}, u32[]{:S(2)}) copy-start(s32[16]{0:T(128)} %counts.1) | copy-start | bytes 196
  16.5 1.9 %collective-permute-start.2 = (bf16[16,1,128,128]{3,2,1,0:T(8,128)(2,1)S(1)}, bf16[16,1,128,128]{3,2,1,0:T(8,128)(2,1)S(1)}, u32[]{:S(2)}, u32[]{:S(2)}) collective-permute-start(bf16[16,1,128,128]{3,2,1,0:T(8,128)(2,1)S(1)} %collective-permute-done.held.refs_2_), channel_id=1, source_target_pairs={{0,4},{4,0},{8,12},{12,8},{1,5},{5,1},{9,13},{13,9},{2,6},{6,2},{1... | collective-permute-start | bytes 1572872 | tf_op jit(solution)/shard_map/ppermute | solution.py:391
  19.3 15.0 %collective-permute-start.3 = (s16[2064,128]{1,0:T(8,128)(2,1)S(1)}, s16[2064,128]{1,0:T(8,128)(2,1)S(1)}, u32[]{:S(2)}, u32[]{:S(2)}) collective-permute-start(s16[2064,128]{1,0:T(8,128)(2,1)S(1)} %shard_map.61), channel_id=1, source_target_pairs={{0,2},{1,0},{2,3},{3,1},{4,6},{5,4},{6,7},{7,5},{8,10},{9,8},{10,1... | collective-permute-start | bytes 1585160 | tf_op jit(solution)/shard_map/ppermute | solution.py:412
  24.4 21.3 %collective-permute-start.6 = (s16[2064,128]{1,0:T(8,128)(2,1)S(1)}, s16[2064,128]{1,0:T(8,128)(2,1)S(1)}, u32[]{:S(2)}, u32[]{:S(2)}) collective-permute-start(s16[2064,128]{1,0:T(8,128)(2,1)S(1)} %shard_map.64), channel_id=1, source_target_pairs={{0,4},{1,2},{2,1},{3,7},{4,0},{5,6},{6,5},{7,3},{8,12},{9,10},{10,... | collective-permute-start | bytes 1585160 | tf_op jit(solution)/shard_map/ppermute | solution.py:429
  26.9 13.1 %collective-permute-start.4 = (s16[1040,128]{1,0:T(8,128)(2,1)S(1)}, s16[1040,128]{1,0:T(8,128)(2,1)S(1)}, u32[]{:S(2)}, u32[]{:S(2)}) collective-permute-start(s16[1040,128]{1,0:T(8,128)(2,1)S(1)} %get-tuple-element.33), channel_id=1, source_target_pairs={{0,1},{1,0},{2,3},{3,2},{4,5},{5,4},{6,7},{7,6},{8,9},{9,8},{10,11... | collective-permute-start | bytes 798728 | tf_op jit(solution)/shard_map/ppermute | solution.py:425
  29.8 15.9 %collective-permute-start.5 = (s16[1040,128]{1,0:T(8,128)(2,1)S(1)}, s16[1040,128]{1,0:T(8,128)(2,1)S(1)}, u32[]{:S(2)}, u32[]{:S(2)}) collective-permute-start(s16[1040,128]{1,0:T(8,128)(2,1)S(1)} %get-tuple-element.34), channel_id=1, source_target_pairs={{0,1},{1,0},{2,3},{3,2},{4,5},{5,4},{6,7},{7,6},{8,9},{9,8},{10,11... | collective-permute-start | bytes 798728 | tf_op jit(solution)/shard_map/ppermute | solution.py:425
  40.2 12.9 %collective-permute-start.11 = (s16[1040,128]{1,0:T(8,128)(2,1)S(1)}, s16[1040,128]{1,0:T(8,128)(2,1)S(1)}, u32[]{:S(2)}, u32[]{:S(2)}) collective-permute-start(s16[1040,128]{1,0:T(8,128)(2,1)S(1)} %shard_map.68), channel_id=1, source_target_pairs={{0,1},{1,3},{3,2},{2,0},{4,5},{5,7},{7,6},{6,4},{8,9},{9,11},{11,1... | collective-permute-start | bytes 798728 | tf_op jit(solution)/shard_map/ppermute | solution.py:450
  45.9 12.8 %collective-permute-start.7 = (s16[1040,128]{1,0:T(8,128)(2,1)S(1)}, s16[1040,128]{1,0:T(8,128)(2,1)S(1)}, u32[]{:S(2)}, u32[]{:S(2)}) collective-permute-start(s16[1040,128]{1,0:T(8,128)(2,1)S(1)} %shard_map.66), channel_id=1, source_target_pairs={{0,1},{1,3},{3,2},{2,0},{4,5},{5,7},{7,6},{6,4},{8,9},{9,11},{11,1... | collective-permute-start | bytes 798728 | tf_op jit(solution)/shard_map/ppermute | solution.py:450
  53.2 7.4 %collective-permute-start.14 = (f32[8,256]{1,0:T(8,128)S(1)}, f32[8,256]{1,0:T(8,128)S(1)}, u32[]{:S(2)}, u32[]{:S(2)}) collective-permute-start(f32[8,256]{1,0:T(8,128)S(1)} %get-tuple-element.44.refs_0_), channel_id=1, source_target_pairs={{0,12},{4,8},{8,4},{12,0},{1,13},{5,9},{9,5},{13,1},{2,14},{6,10},... | collective-permute-start | bytes 24584 | tf_op jit(solution)/shard_map/ppermute | solution.py:470
  54.4 7.1 %collective-permute-start.13 = (f32[8,256]{1,0:T(8,128)S(1)}, f32[8,256]{1,0:T(8,128)S(1)}, u32[]{:S(2)}, u32[]{:S(2)}) collective-permute-start(f32[8,256]{1,0:T(8,128)S(1)} %get-tuple-element.44.refs_0_), channel_id=1, source_target_pairs={{0,8},{4,12},{8,0},{12,4},{1,9},{5,13},{9,1},{13,5},{2,10},{6,14},... | collective-permute-start | bytes 24584 | tf_op jit(solution)/shard_map/ppermute | solution.py:470
  54.9 6.6 %collective-permute-start.12 = (f32[8,256]{1,0:T(8,128)S(1)}, f32[8,256]{1,0:T(8,128)S(1)}, u32[]{:S(2)}, u32[]{:S(2)}) collective-permute-start(f32[8,256]{1,0:T(8,128)S(1)} %get-tuple-element.44.refs_0_), channel_id=1, source_target_pairs={{0,4},{4,0},{8,12},{12,8},{1,5},{5,1},{9,13},{13,9},{2,6},{6,2},{1... | collective-permute-start | bytes 24584 | tf_op jit(solution)/shard_map/ppermute | solution.py:470
  58.8 3.5 %collective-permute-start.10 = (f32[8,256]{1,0:T(8,128)S(1)}, f32[8,256]{1,0:T(8,128)S(1)}, u32[]{:S(2)}, u32[]{:S(2)}) collective-permute-start(f32[8,256]{1,0:T(8,128)S(1)} %get-tuple-element.42.refs_0_), channel_id=1, source_target_pairs={{0,12},{4,8},{8,4},{12,0},{1,13},{5,9},{9,5},{13,1},{2,14},{6,10},... | collective-permute-start | bytes 24584 | tf_op jit(solution)/shard_map/ppermute | solution.py:470
  60.1 3.7 %collective-permute-start.9 = (f32[8,256]{1,0:T(8,128)S(1)}, f32[8,256]{1,0:T(8,128)S(1)}, u32[]{:S(2)}, u32[]{:S(2)}) collective-permute-start(f32[8,256]{1,0:T(8,128)S(1)} %get-tuple-element.42.refs_0_), channel_id=1, source_target_pairs={{0,8},{4,12},{8,0},{12,4},{1,9},{5,13},{9,1},{13,5},{2,10},{6,14},... | collective-permute-start | bytes 24584 | tf_op jit(solution)/shard_map/ppermute | solution.py:470
  60.6 3.2 %collective-permute-start.8 = (f32[8,256]{1,0:T(8,128)S(1)}, f32[8,256]{1,0:T(8,128)S(1)}, u32[]{:S(2)}, u32[]{:S(2)}) collective-permute-start(f32[8,256]{1,0:T(8,128)S(1)} %get-tuple-element.42.refs_0_), channel_id=1, source_target_pairs={{0,4},{4,0},{8,12},{12,8},{1,5},{5,1},{9,13},{13,9},{2,6},{6,2},{1... | collective-permute-start | bytes 24584 | tf_op jit(solution)/shard_map/ppermute | solution.py:470

commit v7 on v5

--- a/solution.py
+++ b/solution.py
@@ -437,11 +437,10 @@
             [VMEM] * 2,
         )
         others = [totals]
-        for by in range(ny):
-            for flip in (0, 1):
-                if by or flip:
-                    pairs = [(a, ((a // 2 + by) % ny) * 2 + (a % 2 ^ flip)) for a in range(2 * ny)]
-                    others.append(lax.ppermute(totals, "row", pairs))
+        steps = [(by, 1) for by in range(1, ny)] + [(by, 0) for by in range(1, ny)] + [(0, 1)]
+        for by, flip in steps:
+            pairs = [(a, ((a // 2 + by) % ny) * 2 + (a % 2 ^ flip)) for a in range(2 * ny)]
+            others.append(lax.ppermute(totals, "row", pairs))
         result = call(
             functools.partial(scale, all_rows, part),
             [inflated, *others, *result],

time: 64.8 us -> 64.7 us (level)
  transfers between devices with their start and end apart: 15 -> 15, of which waited for: 8 -> 9; matrix products, arithmetic and copies ran while one was open for 0% -> 0% of each run, Pallas kernels for 21% -> 21%
where the time goes in v7:
time: 64.7 us; the launch traced here: 64.5 us
  waiting for transfers between devices  26.6 us (41%)
  starting transfers between devices  17.3 us (27%)
  Pallas kernels  15.8 us (24%)
  local copies, waits for them, and re-layouts  3.97 us (6%)
  between operations  0.77 us (1%)
    pallas_call x13, Pallas kernels, call(): pl.pallas_call(kernel, in_specs=[SMEM] * few + [pl.BlockSpec(memory_space...  15.8 us
    ppermute x1, waiting for transfers between devices, body_line(): came_f = lax.ppermute(send_f, 'col', [(0, 2), (1, 0), (2, 3), (3, 1)])  7.68 us
    ppermute x2, waiting for transfers between devices, body_line(): came_t.append(lax.ppermute(send_t, 'col', [(0, 1), (1, 3), (3, 2), (2, 0)]))  7.25 us
    ppermute x2, starting transfers between devices, body_line(): came_t.append(lax.ppermute(send_t, 'col', [(0, 1), (1, 3), (3, 2), (2, 0)]))  5.16 us
    ppermute x1, waiting for transfers between devices, body_line(): turned = [lax.ppermute(slot_blocks, 'row', turn(by)) for by in range(1, ny)]  4.85 us
    ppermute x2, waiting for transfers between devices, body_line(): lax.ppermute(one, 'col', [(0, 1), (1, 0), (2, 3), (3, 2)])  4.74 us
    unnamed x8, local copies, waits for them, and re-layouts  3.97 us
    ppermute x6, starting transfers between devices, body_line(): others.append(lax.ppermute(totals, 'row', pairs))  3.86 us
  transfers between devices with their start and end apart: 15, of which 9 were waited for; matrix products, arithmetic and copies ran while one was open for 0% of the time, Pallas kernels for 21%

profile of v7, /device:TPU:0, one launch (start us, length us, event | category | flops | bytes accessed | tf_op | source)
XLA Modules:
  0.0 64.5 jit_solution(8002725672104076302)
XLA Ops:
  0.6 0.5 collective-permute-start.1
  1.1 2.6 %collective-permute-start = (bf16[16,1,128,128]{3,2,1,0:T(8,128)(2,1)}, bf16[16,1,128,128]{3,2,1,0:T(8,128)(2,1)S(1)}, u32[]{:S(2)}, u32[]{:S(2)}) collective-permute-start(bf16[16,1,128,128]{3,2,1,0:T(8,128)(2,1)} %own.1), channel_id=1, source_target_pairs={{0,8},{4,12},{8,0},{12,4},{1,9},{5,13},{9,1},{13,5},{2,10},{6,14},... | collective-permute-start | bytes 1572872 | tf_op jit(solution)/shard_map/ppermute | solution.py:349
  3.7 0.0 collective-permute-done.1.twin.refs_1_
  3.7 0.0 copy-start
  3.7 1.6 %copy-done = bf16[512,2048]{1,0:T(8,128)(2,1)S(1)} copy-done((bf16[512,2048]{1,0:T(8,128)(2,1)S(1)}, bf16[512,2048]{1,0:T(8,128)(2,1)}, u32[]{:S(2)}) %copy-start) | copy-done | bytes 2097176
  5.3 0.0 copy-start.1
  5.3 1.0 %copy-done.1 = bf16[16,1,128,128]{3,2,1,0:T(8,128)(2,1)S(1)} copy-done((bf16[16,1,128,128]{3,2,1,0:T(8,128)(2,1)S(1)}, bf16[16,1,128,128]{3,2,1,0:T(8,128)(2,1)}, u32[]{:S(2)}) %copy-start.1) | copy-done | bytes 524312
  6.4 0.0 copy-start.2
  6.4 0.7 %copy-done.2 = s32[16,4]{0,1:T(4,128)S(1)} copy-done((s32[16,4]{0,1:T(4,128)S(1)}, s32[16,4]{0,1:T(4,128)}, u32[]{:S(2)}) %copy-start.2) | copy-done | bytes 280
  7.1 0.0 copy-start.3
  7.1 0.7 %copy-done.3 = s32[16]{0:T(128)S(1)} copy-done((s32[16]{0:T(128)S(1)}, s32[16]{0:T(128)}, u32[]{:S(2)}) %copy-start.3) | copy-done | bytes 88
  7.7 3.9 %shard_map.59 = (s32[288]{0:T(512)S(1)}, bf16[512,2048]{1,0:T(8,128)(2,1)S(1)}, bf16[16,1,128,128]{3,2,1,0:T(8,128)(2,1)S(1)}, f32[512,512]{1,0:T(8,128)S(1)}) custom-call(s32[4,16]{1,0:T(4,128)S(1)} %bitcast.1, s32[16]{0:T(128)S(1)} %copy-done.3, bf16[512,2048]{1,0:T(8,128)(2,1)S(1)} %copy-done, bf16[16,1,128,128]{3,2,1,0:T(8,128)(2,1)S(1)} %copy-done.1, ...), custom_call_target="tpu_custom_call" | custom-call | flops 268435456 | bytes 6817216 | tf_op jit(solution)/shard_map/pallas_call | solution.py:312
  11.6 4.9 %collective-permute-done.held.refs_2_ = bf16[16,1,128,128]{3,2,1,0:T(8,128)(2,1)S(1)} collective-permute-done((bf16[16,1,128,128]{3,2,1,0:T(8,128)(2,1)}, bf16[16,1,128,128]{3,2,1,0:T(8,128)(2,1)S(1)}, u32[]{:S(2)}, u32[]{:S(2)}) %collective-permute-start) | collective-permute-done | bytes 524320 | tf_op jit(solution)/shard_map/ppermute | solution.py:349
  16.5 0.0 collective-permute-start.2
  16.5 1.0 %shard_map.60.total = f32[512,512]{1,0:T(8,128)S(1)} custom-call(s32[288]{0:T(512)S(1)} %get-tuple-element.30.plan_ref, bf16[512,2048]{1,0:T(8,128)(2,1)S(1)} %get-tuple-element.27.operand, bf16[16,1,128,128]{3,2,1,0:T(8,128)(2,1)S(1)} %collective-permute-done.held.refs_2_, f32[512,512]{1,0:T(8,128)S(1)} %get-tuple-element.29._), custom_call_target="tpu_custom_call", output_to_operand_aliasing={{}: (3, {})} | custom-call | flops 134217728 | bytes 4719744 | tf_op jit(solution)/shard_map/pallas_call | solution.py:312
  17.5 0.9 %collective-permute-done.2.held.refs_3_ = bf16[16,1,128,128]{3,2,1,0:T(8,128)(2,1)S(1)} collective-permute-done((bf16[16,1,128,128]{3,2,1,0:T(8,128)(2,1)S(1)}, bf16[16,1,128,128]{3,2,1,0:T(8,128)(2,1)S(1)}, u32[]{:S(2)}, u32[]{:S(2)}) %collective-permute-start.2) | collective-permute-done | bytes 524320 | tf_op jit(solution)/shard_map/ppermute | solution.py:368
  18.4 1.4 %shard_map.61 = s16[2064,128]{1,0:T(8,128)(2,1)S(1)} custom-call(s32[288]{0:T(512)S(1)} %get-tuple-element.30.plan_ref, bf16[512,2048]{1,0:T(8,128)(2,1)S(1)} %get-tuple-element.27.operand, bf16[16,1,128,128]{3,2,1,0:T(8,128)(2,1)S(1)} %collective-permute-done.2.held.refs_3_, f32[512,512]{1,0:T(8,128)S(1)} %shard_map.60.total), custom_call_target="tpu_custom_call" | custom-call | flops 134217728 | bytes 4199552 | tf_op jit(solution)/shard_map/pallas_call | solution.py:312
  19.8 2.9 %collective-permute-start.3 = (s16[2064,128]{1,0:T(8,128)(2,1)S(1)}, s16[2064,128]{1,0:T(8,128)(2,1)S(1)}, u32[]{:S(2)}, u32[]{:S(2)}) collective-permute-start(s16[2064,128]{1,0:T(8,128)(2,1)S(1)} %shard_map.61), channel_id=1, source_target_pairs={{0,2},{1,0},{2,3},{3,1},{4,6},{5,4},{6,7},{7,5},{8,10},{9,8},{10,1... | collective-permute-start | bytes 1585160 | tf_op jit(solution)/shard_map/ppermute | solution.py:389
  22.7 2.5 %shard_map.63 = (s16[2064,128]{1,0:T(8,128)(2,1)S(1)}, s16[1040,128]{1,0:T(8,128)(2,1)S(1)}, s16[1040,128]{1,0:T(8,128)(2,1)S(1)}) custom-call(s32[288]{0:T(512)S(1)} %get-tuple-element.30.plan_ref, bf16[512,2048]{1,0:T(8,128)(2,1)S(1)} %get-tuple-element.27.operand, bf16[16,1,128,128]{3,2,1,0:T(8,128)(2,1)S(1)} %get-tuple-element.31.refs_0_, ...), custom_call_target="tpu_custom_call" | custom-call | flops 1073741824 | bytes 5256320 | tf_op jit(solution)/shard_map/pallas_call | solution.py:312
  25.1 0.1 collective-permute-start.5
  25.2 2.2 %collective-permute-start.10 = (s16[1040,128]{1,0:T(8,128)(2,1)S(1)}, s16[1040,128]{1,0:T(8,128)(2,1)S(1)}, u32[]{:S(2)}, u32[]{:S(2)}) collective-permute-start(s16[1040,128]{1,0:T(8,128)(2,1)S(1)} %get-tuple-element.44), channel_id=1, source_target_pairs={{0,1},{1,0},{2,3},{3,2},{4,5},{5,4},{6,7},{7,6},{8,9},{9,8},{10,11... | collective-permute-start | bytes 798728 | tf_op jit(solution)/shard_map/ppermute | solution.py:402
  27.4 0.0 collective-permute-start.4
  27.4 7.7 %collective-permute-done.3.came_f = s16[2064,128]{1,0:T(8,128)(2,1)S(1)} collective-permute-done((s16[2064,128]{1,0:T(8,128)(2,1)S(1)}, s16[2064,128]{1,0:T(8,128)(2,1)S(1)}, u32[]{:S(2)}, u32[]{:S(2)}) %collective-permute-start.3) | collective-permute-done | bytes 528416 | tf_op jit(solution)/shard_map/ppermute | solution.py:389
  35.1 3.9 %shard_map.62 = (f32[512,512]{1,0:T(8,128)S(1)}, f32[512,512]{1,0:T(8,128)S(1)}, s32[16,128]{1,0:T(8,128)S(1)}, s32[16,128]{1,0:T(8,128)S(1)}) custom-call(s32[288]{0:T(512)S(1)} %get-tuple-element.30.plan_ref, bf16[512,2048]{1,0:T(8,128)(2,1)S(1)} %get-tuple-element.27.operand, bf16[16,1,128,128]{3,2,1,0:T(8,128)(2,1)S(1)} %get-tuple-element.31.refs_0_, ...), custom_call_target="tpu_custom_call" | custom-call | flops 2147483648 | bytes 6308992 | tf_op jit(solution)/shard_map/pallas_call | solution.py:312
  39.0 1.8 %collective-permute-done.10.came = s16[1040,128]{1,0:T(8,128)(2,1)S(1)} collective-permute-done((s16[1040,128]{1,0:T(8,128)(2,1)S(1)}, s16[1040,128]{1,0:T(8,128)(2,1)S(1)}, u32[]{:S(2)}, u32[]{:S(2)}) %collective-permute-start.10) | collective-permute-done | bytes 266272 | tf_op jit(solution)/shard_map/ppermute | solution.py:402
  40.8 0.2 shard_map.67
  41.0 2.6 %collective-permute-start.11 = (s16[1040,128]{1,0:T(8,128)(2,1)S(1)}, s16[1040,128]{1,0:T(8,128)(2,1)S(1)}, u32[]{:S(2)}, u32[]{:S(2)}) collective-permute-start(s16[1040,128]{1,0:T(8,128)(2,1)S(1)} %shard_map.67), channel_id=1, source_target_pairs={{0,1},{1,3},{3,2},{2,0},{4,5},{5,7},{7,6},{6,4},{8,9},{9,11},{11,1... | collective-permute-start | bytes 798728 | tf_op jit(solution)/shard_map/ppermute | solution.py:424
  43.6 2.9 %collective-permute-done.4.came = s16[1040,128]{1,0:T(8,128)(2,1)S(1)} collective-permute-done((s16[1040,128]{1,0:T(8,128)(2,1)S(1)}, s16[1040,128]{1,0:T(8,128)(2,1)S(1)}, u32[]{:S(2)}, u32[]{:S(2)}) %collective-permute-start.4) | collective-permute-done | bytes 266272 | tf_op jit(solution)/shard_map/ppermute | solution.py:402
  46.5 0.0 collective-permute-done.5.came_b
  46.5 0.2 shard_map.65
  46.7 2.6 %collective-permute-start.6 = (s16[1040,128]{1,0:T(8,128)(2,1)S(1)}, s16[1040,128]{1,0:T(8,128)(2,1)S(1)}, u32[]{:S(2)}, u32[]{:S(2)}) collective-permute-start(s16[1040,128]{1,0:T(8,128)(2,1)S(1)} %shard_map.65), channel_id=1, source_target_pairs={{0,1},{1,3},{3,2},{2,0},{4,5},{5,7},{7,6},{6,4},{8,9},{9,11},{11,1... | collective-permute-start | bytes 798728 | tf_op jit(solution)/shard_map/ppermute | solution.py:424
  49.3 0.2 shard_map.64
  49.4 3.7 %collective-permute-done.11.came = s16[1040,128]{1,0:T(8,128)(2,1)S(1)} collective-permute-done((s16[1040,128]{1,0:T(8,128)(2,1)S(1)}, s16[1040,128]{1,0:T(8,128)(2,1)S(1)}, u32[]{:S(2)}, u32[]{:S(2)}) %collective-permute-start.11) | collective-permute-done | bytes 266272 | tf_op jit(solution)/shard_map/ppermute | solution.py:424
  53.1 0.1 shard_map.68
  53.3 0.1 collective-permute-start.14
  53.3 1.6 %collective-permute-start.13 = (f32[8,256]{1,0:T(8,128)S(1)}, f32[8,256]{1,0:T(8,128)S(1)}, u32[]{:S(2)}, u32[]{:S(2)}) collective-permute-start(f32[8,256]{1,0:T(8,128)S(1)} %get-tuple-element.46.refs_0_), channel_id=1, source_target_pairs={{0,8},{4,12},{8,0},{12,4},{1,9},{5,13},{9,1},{13,5},{2,10},{6,14},... | collective-permute-start | bytes 24584 | tf_op jit(solution)/shard_map/ppermute | solution.py:443
  54.9 0.3 collective-permute-start.12
  55.2 3.6 %collective-permute-done.6.came = s16[1040,128]{1,0:T(8,128)(2,1)S(1)} collective-permute-done((s16[1040,128]{1,0:T(8,128)(2,1)S(1)}, s16[1040,128]{1,0:T(8,128)(2,1)S(1)}, u32[]{:S(2)}, u32[]{:S(2)}) %collective-permute-start.6) | collective-permute-done | bytes 266272 | tf_op jit(solution)/shard_map/ppermute | solution.py:424
  58.8 0.1 shard_map.66
  58.9 0.1 collective-permute-start.9
  59.0 1.6 %collective-permute-start.8 = (f32[8,256]{1,0:T(8,128)S(1)}, f32[8,256]{1,0:T(8,128)S(1)}, u32[]{:S(2)}, u32[]{:S(2)}) collective-permute-start(f32[8,256]{1,0:T(8,128)S(1)} %get-tuple-element.43.refs_0_), channel_id=1, source_target_pairs={{0,8},{4,12},{8,0},{12,4},{1,9},{5,13},{9,1},{13,5},{2,10},{6,14},... | collective-permute-start | bytes 24584 | tf_op jit(solution)/shard_map/ppermute | solution.py:443
  60.6 0.0 collective-permute-done.14.refs_3_
  60.6 0.3 collective-permute-start.7
  60.8 0.7 %shard_map.71 = s32[4]{0:T(128)} custom-call(s32[16,128]{1,0:T(8,128)S(1)} %get-tuple-element.47.own_load, s16[1040,128]{1,0:T(8,128)(2,1)S(1)} %collective-permute-done.11.came), custom_call_target="tpu_custom_call" | custom-call | bytes 274448 | tf_op jit(solution)/shard_map/pallas_call | solution.py:312
  61.6 0.0 collective-permute-done.13.refs_2_
  61.6 0.0 collective-permute-done.12.refs_1_
  61.6 0.8 %shard_map.69.refs_4_ = f32[512,512]{1,0:T(8,128)} custom-call(f32[512,256]{1,0:T(8,128)S(1)} %get-tuple-element.45.inflated, f32[8,256]{1,0:T(8,128)S(1)} %get-tuple-element.46.refs_0_, f32[8,256]{1,0:T(8,128)S(1)} %collective-permute-done.12.refs_1_, f32[8,256]{1,0:T(8,128)S(1)} %collective-permute-done.13.refs_2_, ...), custom_call_target="tpu_custom_call" | custom-call | bytes 1605632 | tf_op jit(solution)/shard_map/pallas_call | solution.py:312
  62.4 0.0 collective-permute-done.9.refs_3_
  62.4 0.2 collective-permute-done.8.refs_2_
  62.7 1.0 %collective-permute-done.7.refs_1_ = f32[8,256]{1,0:T(8,128)S(1)} collective-permute-done((f32[8,256]{1,0:T(8,128)S(1)}, f32[8,256]{1,0:T(8,128)S(1)}, u32[]{:S(2)}, u32[]{:S(2)}) %collective-permute-start.7) | collective-permute-done | bytes 8224 | tf_op jit(solution)/shard_map/ppermute | solution.py:443
  63.6 0.8 %shard_map.70 = f32[512,512]{1,0:T(8,128)} custom-call(f32[512,256]{1,0:T(8,128)S(1)} %get-tuple-element.42.inflated, f32[8,256]{1,0:T(8,128)S(1)} %get-tuple-element.43.refs_0_, f32[8,256]{1,0:T(8,128)S(1)} %collective-permute-done.7.refs_1_, f32[8,256]{1,0:T(8,128)S(1)} %collective-permute-done.8.refs_2_, ...), custom_call_target="tpu_custom_call", output_to_operand_aliasing={{}: (5, {})} | custom-call | bytes 2654208 | tf_op jit(solution)/shard_map/pallas_call | solution.py:312
Async XLA Ops:
  0.6 3.1 %collective-permute-start.1 = (bf16[16,1,128,128]{3,2,1,0:T(8,128)(2,1)}, bf16[16,1,128,128]{3,2,1,0:T(8,128)(2,1)S(1)}, u32[]{:S(2)}, u32[]{:S(2)}) collective-permute-start(bf16[16,1,128,128]{3,2,1,0:T(8,128)(2,1)} %own.1), channel_id=1, source_target_pairs={{0,4},{4,0},{8,12},{12,8},{1,5},{5,1},{9,13},{13,9},{2,6},{6,2},{1... | collective-permute-start | bytes 1572872 | tf_op jit(solution)/shard_map/ppermute | solution.py:350
  1.1 15.3 %collective-permute-start = (bf16[16,1,128,128]{3,2,1,0:T(8,128)(2,1)}, bf16[16,1,128,128]{3,2,1,0:T(8,128)(2,1)S(1)}, u32[]{:S(2)}, u32[]{:S(2)}) collective-permute-start(bf16[16,1,128,128]{3,2,1,0:T(8,128)(2,1)} %own.1), channel_id=1, source_target_pairs={{0,8},{4,12},{8,0},{12,4},{1,9},{5,13},{9,1},{13,5},{2,10},{6,14},... | collective-permute-start | bytes 1572872 | tf_op jit(solution)/shard_map/ppermute | solution.py:349
  3.7 1.6 %copy-start = (bf16[512,2048]{1,0:T(8,128)(2,1)S(1)}, bf16[512,2048]{1,0:T(8,128)(2,1)}, u32[]{:S(2)}) copy-start(bf16[512,2048]{1,0:T(8,128)(2,1)} %operand.1) | copy-start | bytes 6291460
  5.3 1.0 %copy-start.1 = (bf16[16,1,128,128]{3,2,1,0:T(8,128)(2,1)S(1)}, bf16[16,1,128,128]{3,2,1,0:T(8,128)(2,1)}, u32[]{:S(2)}) copy-start(bf16[16,1,128,128]{3,2,1,0:T(8,128)(2,1)} %own.1) | copy-start | bytes 1572868
  6.4 0.7 %copy-start.2 = (s32[16,4]{0,1:T(4,128)S(1)}, s32[16,4]{0,1:T(4,128)}, u32[]{:S(2)}) copy-start(s32[16,4]{0,1:T(4,128)} %param.6) | copy-start | bytes 772
  7.1 0.7 %copy-start.3 = (s32[16]{0:T(128)S(1)}, s32[16]{0:T(128)}, u32[]{:S(2)}) copy-start(s32[16]{0:T(128)} %counts.1) | copy-start | bytes 196
  16.5 1.9 %collective-permute-start.2 = (bf16[16,1,128,128]{3,2,1,0:T(8,128)(2,1)S(1)}, bf16[16,1,128,128]{3,2,1,0:T(8,128)(2,1)S(1)}, u32[]{:S(2)}, u32[]{:S(2)}) collective-permute-start(bf16[16,1,128,128]{3,2,1,0:T(8,128)(2,1)S(1)} %collective-permute-done.held.refs_2_), channel_id=1, source_target_pairs={{0,4},{4,0},{8,12},{12,8},{1,5},{5,1},{9,13},{13,9},{2,6},{6,2},{1... | collective-permute-start | bytes 1572872 | tf_op jit(solution)/shard_map/ppermute | solution.py:368
  19.8 15.3 %collective-permute-start.3 = (s16[2064,128]{1,0:T(8,128)(2,1)S(1)}, s16[2064,128]{1,0:T(8,128)(2,1)S(1)}, u32[]{:S(2)}, u32[]{:S(2)}) collective-permute-start(s16[2064,128]{1,0:T(8,128)(2,1)S(1)} %shard_map.61), channel_id=1, source_target_pairs={{0,2},{1,0},{2,3},{3,1},{4,6},{5,4},{6,7},{7,5},{8,10},{9,8},{10,1... | collective-permute-start | bytes 1585160 | tf_op jit(solution)/shard_map/ppermute | solution.py:389
  25.1 21.4 %collective-permute-start.5 = (s16[2064,128]{1,0:T(8,128)(2,1)S(1)}, s16[2064,128]{1,0:T(8,128)(2,1)S(1)}, u32[]{:S(2)}, u32[]{:S(2)}) collective-permute-start(s16[2064,128]{1,0:T(8,128)(2,1)S(1)} %get-tuple-element.35), channel_id=1, source_target_pairs={{0,4},{1,2},{2,1},{3,7},{4,0},{5,6},{6,5},{7,3},{8,12},{9,10},{10,... | collective-permute-start | bytes 1585160 | tf_op jit(solution)/shard_map/ppermute | solution.py:403
  25.2 15.6 %collective-permute-start.10 = (s16[1040,128]{1,0:T(8,128)(2,1)S(1)}, s16[1040,128]{1,0:T(8,128)(2,1)S(1)}, u32[]{:S(2)}, u32[]{:S(2)}) collective-permute-start(s16[1040,128]{1,0:T(8,128)(2,1)S(1)} %get-tuple-element.44), channel_id=1, source_target_pairs={{0,1},{1,0},{2,3},{3,2},{4,5},{5,4},{6,7},{7,6},{8,9},{9,8},{10,11... | collective-permute-start | bytes 798728 | tf_op jit(solution)/shard_map/ppermute | solution.py:402
  27.4 19.1 %collective-permute-start.4 = (s16[1040,128]{1,0:T(8,128)(2,1)S(1)}, s16[1040,128]{1,0:T(8,128)(2,1)S(1)}, u32[]{:S(2)}, u32[]{:S(2)}) collective-permute-start(s16[1040,128]{1,0:T(8,128)(2,1)S(1)} %get-tuple-element.34), channel_id=1, source_target_pairs={{0,1},{1,0},{2,3},{3,2},{4,5},{5,4},{6,7},{7,6},{8,9},{9,8},{10,11... | collective-permute-start | bytes 798728 | tf_op jit(solution)/shard_map/ppermute | solution.py:402
  41.0 12.1 %collective-permute-start.11 = (s16[1040,128]{1,0:T(8,128)(2,1)S(1)}, s16[1040,128]{1,0:T(8,128)(2,1)S(1)}, u32[]{:S(2)}, u32[]{:S(2)}) collective-permute-start(s16[1040,128]{1,0:T(8,128)(2,1)S(1)} %shard_map.67), channel_id=1, source_target_pairs={{0,1},{1,3},{3,2},{2,0},{4,5},{5,7},{7,6},{6,4},{8,9},{9,11},{11,1... | collective-permute-start | bytes 798728 | tf_op jit(solution)/shard_map/ppermute | solution.py:424
  46.7 12.1 %collective-permute-start.6 = (s16[1040,128]{1,0:T(8,128)(2,1)S(1)}, s16[1040,128]{1,0:T(8,128)(2,1)S(1)}, u32[]{:S(2)}, u32[]{:S(2)}) collective-permute-start(s16[1040,128]{1,0:T(8,128)(2,1)S(1)} %shard_map.65), channel_id=1, source_target_pairs={{0,1},{1,3},{3,2},{2,0},{4,5},{5,7},{7,6},{6,4},{8,9},{9,11},{11,1... | collective-permute-start | bytes 798728 | tf_op jit(solution)/shard_map/ppermute | solution.py:424
  53.3 7.3 %collective-permute-start.14 = (f32[8,256]{1,0:T(8,128)S(1)}, f32[8,256]{1,0:T(8,128)S(1)}, u32[]{:S(2)}, u32[]{:S(2)}) collective-permute-start(f32[8,256]{1,0:T(8,128)S(1)} %get-tuple-element.46.refs_0_), channel_id=1, source_target_pairs={{0,4},{4,0},{8,12},{12,8},{1,5},{5,1},{9,13},{13,9},{2,6},{6,2},{1... | collective-permute-start | bytes 24584 | tf_op jit(solution)/shard_map/ppermute | solution.py:443
  53.3 8.2 %collective-permute-start.13 = (f32[8,256]{1,0:T(8,128)S(1)}, f32[8,256]{1,0:T(8,128)S(1)}, u32[]{:S(2)}, u32[]{:S(2)}) collective-permute-start(f32[8,256]{1,0:T(8,128)S(1)} %get-tuple-element.46.refs_0_), channel_id=1, source_target_pairs={{0,8},{4,12},{8,0},{12,4},{1,9},{5,13},{9,1},{13,5},{2,10},{6,14},... | collective-permute-start | bytes 24584 | tf_op jit(solution)/shard_map/ppermute | solution.py:443
  54.9 6.6 %collective-permute-start.12 = (f32[8,256]{1,0:T(8,128)S(1)}, f32[8,256]{1,0:T(8,128)S(1)}, u32[]{:S(2)}, u32[]{:S(2)}) collective-permute-start(f32[8,256]{1,0:T(8,128)S(1)} %get-tuple-element.46.refs_0_), channel_id=1, source_target_pairs={{0,12},{4,8},{8,4},{12,0},{1,13},{5,9},{9,5},{13,1},{2,14},{6,10},... | collective-permute-start | bytes 24584 | tf_op jit(solution)/shard_map/ppermute | solution.py:443
  58.9 3.5 %collective-permute-start.9 = (f32[8,256]{1,0:T(8,128)S(1)}, f32[8,256]{1,0:T(8,128)S(1)}, u32[]{:S(2)}, u32[]{:S(2)}) collective-permute-start(f32[8,256]{1,0:T(8,128)S(1)} %get-tuple-element.43.refs_0_), channel_id=1, source_target_pairs={{0,4},{4,0},{8,12},{12,8},{1,5},{5,1},{9,13},{13,9},{2,6},{6,2},{1... | collective-permute-start | bytes 24584 | tf_op jit(solution)/shard_map/ppermute | solution.py:443
  59.0 3.7 %collective-permute-start.8 = (f32[8,256]{1,0:T(8,128)S(1)}, f32[8,256]{1,0:T(8,128)S(1)}, u32[]{:S(2)}, u32[]{:S(2)}) collective-permute-start(f32[8,256]{1,0:T(8,128)S(1)} %get-tuple-element.43.refs_0_), channel_id=1, source_target_pairs={{0,8},{4,12},{8,0},{12,4},{1,9},{5,13},{9,1},{13,5},{2,10},{6,14},... | collective-permute-start | bytes 24584 | tf_op jit(solution)/shard_map/ppermute | solution.py:443
  60.6 3.1 %collective-permute-start.7 = (f32[8,256]{1,0:T(8,128)S(1)}, f32[8,256]{1,0:T(8,128)S(1)}, u32[]{:S(2)}, u32[]{:S(2)}) collective-permute-start(f32[8,256]{1,0:T(8,128)S(1)} %get-tuple-element.43.refs_0_), channel_id=1, source_target_pairs={{0,12},{4,8},{8,4},{12,0},{1,13},{5,9},{9,5},{13,1},{2,14},{6,10},... | collective-permute-start | bytes 24584 | tf_op jit(solution)/shard_map/ppermute | solution.py:443

commit v8 on v6

--- a/solution.py
+++ b/solution.py
@@ -463,11 +463,10 @@
             [VMEM] * 2,
         )
         others = [totals]
-        for by in range(ny):
-            for flip in (0, 1):
-                if by or flip:
-                    pairs = [(a, ((a // 2 + by) % ny) * 2 + (a % 2 ^ flip)) for a in range(2 * ny)]
-                    others.append(lax.ppermute(totals, "row", pairs))
+        steps = [(by, 1) for by in range(1, ny)] + [(by, 0) for by in range(1, ny)] + [(0, 1)]
+        for by, flip in steps:
+            pairs = [(a, ((a // 2 + by) % ny) * 2 + (a % 2 ^ flip)) for a in range(2 * ny)]
+            others.append(lax.ppermute(totals, "row", pairs))
         result = call(
             functools.partial(scale, all_rows, part),
             [inflated, *others, *result],

time: 64.8 us -> 64.7 us (level)
  waiting for transfers between devices: 23.3 us -> 24.4 us
  starting transfers between devices: 17.7 us -> 16.9 us
    ppermute x1, waiting for transfers between devices: 3.96 us -> 4.84 us  [body_line(): turned = [lax.ppermute(slot_blocks, 'row', turn(by)) for by in range(1, ny)]]
  transfers between devices with their start and end apart: 15 -> 15, of which waited for: 8 -> 9; matrix products, arithmetic and copies ran while one was open for 0% -> 0% of each run, Pallas kernels for 26% -> 25%
where the time goes in v8:
time: 64.7 us; the launch traced here: 64.4 us
  waiting for transfers between devices  24.4 us (38%)
  Pallas kernels  18.4 us (28%)
  starting transfers between devices  16.9 us (26%)
  local copies, waits for them, and re-layouts  3.97 us (6%)
  between operations  0.78 us (1%)
    pallas_call x14, Pallas kernels, call(): pl.pallas_call(kernel, in_specs=[SMEM] * few + [pl.BlockSpec(memory_space...  18.4 us
    ppermute x2, waiting for transfers between devices, body_line(): came_t.append(lax.ppermute(send_t, 'col', [(0, 1), (1, 3), (3, 2), (2, 0)]))  7.95 us
    ppermute x1, waiting for transfers between devices, body_line(): came_f = lax.ppermute(send_f, 'col', [(0, 2), (1, 0), (2, 3), (3, 1)])  4.89 us
    ppermute x1, waiting for transfers between devices, body_line(): turned = [lax.ppermute(slot_blocks, 'row', turn(by)) for by in range(1, ny)]  4.84 us
    ppermute x2, starting transfers between devices, body_line(): came_t.append(lax.ppermute(send_t, 'col', [(0, 1), (1, 3), (3, 2), (2, 0)]))  4.79 us
    ppermute x2, waiting for transfers between devices, body_line(): lax.ppermute(one, 'col', [(0, 1), (1, 0), (2, 3), (3, 2)])  4.63 us
    unnamed x8, local copies, waits for them, and re-layouts  3.97 us
    ppermute x6, starting transfers between devices, body_line(): others.append(lax.ppermute(totals, 'row', pairs))  3.86 us
  transfers between devices with their start and end apart: 15, of which 9 were waited for; matrix products, arithmetic and copies ran while one was open for 0% of the time, Pallas kernels for 25%

profile of v8, /device:TPU:0, one launch (start us, length us, event | category | flops | bytes accessed | tf_op | source)
XLA Modules:
  0.0 64.4 jit_solution(3341546653321000417)
XLA Ops:
  0.6 0.5 collective-permute-start.1
  1.1 2.6 %collective-permute-start = (bf16[16,1,128,128]{3,2,1,0:T(8,128)(2,1)}, bf16[16,1,128,128]{3,2,1,0:T(8,128)(2,1)S(1)}, u32[]{:S(2)}, u32[]{:S(2)}) collective-permute-start(bf16[16,1,128,128]{3,2,1,0:T(8,128)(2,1)} %own.1), channel_id=1, source_target_pairs={{0,8},{4,12},{8,0},{12,4},{1,9},{5,13},{9,1},{13,5},{2,10},{6,14},... | collective-permute-start | bytes 1572872 | tf_op jit(solution)/shard_map/ppermute | solution.py:372
  3.7 0.0 collective-permute-done.1.twin.refs_1_
  3.7 0.0 copy-start
  3.7 1.6 %copy-done = bf16[512,2048]{1,0:T(8,128)(2,1)S(1)} copy-done((bf16[512,2048]{1,0:T(8,128)(2,1)S(1)}, bf16[512,2048]{1,0:T(8,128)(2,1)}, u32[]{:S(2)}) %copy-start) | copy-done | bytes 2097176
  5.3 0.0 copy-start.1
  5.3 1.0 %copy-done.1 = bf16[16,1,128,128]{3,2,1,0:T(8,128)(2,1)S(1)} copy-done((bf16[16,1,128,128]{3,2,1,0:T(8,128)(2,1)S(1)}, bf16[16,1,128,128]{3,2,1,0:T(8,128)(2,1)}, u32[]{:S(2)}) %copy-start.1) | copy-done | bytes 524312
  6.4 0.0 copy-start.2
  6.4 0.7 %copy-done.2 = s32[16,4]{0,1:T(4,128)S(1)} copy-done((s32[16,4]{0,1:T(4,128)S(1)}, s32[16,4]{0,1:T(4,128)}, u32[]{:S(2)}) %copy-start.2) | copy-done | bytes 280
  7.1 0.0 copy-start.3
  7.1 0.7 %copy-done.3 = s32[16]{0:T(128)S(1)} copy-done((s32[16]{0:T(128)S(1)}, s32[16]{0:T(128)}, u32[]{:S(2)}) %copy-start.3) | copy-done | bytes 88
  7.7 3.9 %shard_map.59 = (s32[288]{0:T(512)S(1)}, bf16[512,2048]{1,0:T(8,128)(2,1)S(1)}, bf16[16,1,128,128]{3,2,1,0:T(8,128)(2,1)S(1)}, f32[512,512]{1,0:T(8,128)S(1)}) custom-call(s32[4,16]{1,0:T(4,128)S(1)} %bitcast.1, s32[16]{0:T(128)S(1)} %copy-done.3, bf16[512,2048]{1,0:T(8,128)(2,1)S(1)} %copy-done, bf16[16,1,128,128]{3,2,1,0:T(8,128)(2,1)S(1)} %copy-done.1, ...), custom_call_target="tpu_custom_call" | custom-call | flops 268435456 | bytes 6817216 | tf_op jit(solution)/shard_map/pallas_call | solution.py:332
  11.6 4.8 %collective-permute-done.held.refs_2_ = bf16[16,1,128,128]{3,2,1,0:T(8,128)(2,1)S(1)} collective-permute-done((bf16[16,1,128,128]{3,2,1,0:T(8,128)(2,1)}, bf16[16,1,128,128]{3,2,1,0:T(8,128)(2,1)S(1)}, u32[]{:S(2)}, u32[]{:S(2)}) %collective-permute-start) | collective-permute-done | bytes 524320 | tf_op jit(solution)/shard_map/ppermute | solution.py:372
  16.5 0.0 collective-permute-start.2
  16.5 1.0 %shard_map.60.total = f32[512,512]{1,0:T(8,128)S(1)} custom-call(s32[288]{0:T(512)S(1)} %get-tuple-element.29.plan_ref, bf16[512,2048]{1,0:T(8,128)(2,1)S(1)} %get-tuple-element.26.operand, bf16[16,1,128,128]{3,2,1,0:T(8,128)(2,1)S(1)} %collective-permute-done.held.refs_2_, f32[512,512]{1,0:T(8,128)S(1)} %get-tuple-element.28._), custom_call_target="tpu_custom_call", output_to_operand_aliasing={{}: (3, {})} | custom-call | flops 134217728 | bytes 4719744 | tf_op jit(solution)/shard_map/pallas_call | solution.py:332
  17.5 0.9 %collective-permute-done.2.held.refs_3_ = bf16[16,1,128,128]{3,2,1,0:T(8,128)(2,1)S(1)} collective-permute-done((bf16[16,1,128,128]{3,2,1,0:T(8,128)(2,1)S(1)}, bf16[16,1,128,128]{3,2,1,0:T(8,128)(2,1)S(1)}, u32[]{:S(2)}, u32[]{:S(2)}) %collective-permute-start.2) | collective-permute-done | bytes 524320 | tf_op jit(solution)/shard_map/ppermute | solution.py:391
  18.4 1.4 %shard_map.61 = s16[2064,128]{1,0:T(8,128)(2,1)S(1)} custom-call(s32[288]{0:T(512)S(1)} %get-tuple-element.29.plan_ref, bf16[512,2048]{1,0:T(8,128)(2,1)S(1)} %get-tuple-element.26.operand, bf16[16,1,128,128]{3,2,1,0:T(8,128)(2,1)S(1)} %collective-permute-done.2.held.refs_3_, f32[512,512]{1,0:T(8,128)S(1)} %shard_map.60.total), custom_call_target="tpu_custom_call" | custom-call | flops 134217728 | bytes 4199552 | tf_op jit(solution)/shard_map/pallas_call | solution.py:332
  19.8 2.1 %collective-permute-start.3 = (s16[2064,128]{1,0:T(8,128)(2,1)S(1)}, s16[2064,128]{1,0:T(8,128)(2,1)S(1)}, u32[]{:S(2)}, u32[]{:S(2)}) collective-permute-start(s16[2064,128]{1,0:T(8,128)(2,1)S(1)} %shard_map.61), channel_id=1, source_target_pairs={{0,2},{1,0},{2,3},{3,1},{4,6},{5,4},{6,7},{7,5},{8,10},{9,8},{10,1... | collective-permute-start | bytes 1585160 | tf_op jit(solution)/shard_map/ppermute | solution.py:412
  21.9 2.4 %shard_map.64 = s16[2064,128]{1,0:T(8,128)(2,1)S(1)} custom-call(s32[288]{0:T(512)S(1)} %get-tuple-element.29.plan_ref, bf16[512,2048]{1,0:T(8,128)(2,1)S(1)} %get-tuple-element.26.operand, bf16[16,1,128,128]{3,2,1,0:T(8,128)(2,1)S(1)} %get-tuple-element.30.refs_0_, bf16[16,1,128,128]{3,2,1,0:T(8,128)(2,1)S(1)} %collective-permute-done.1.twin.refs_1_, ...), custom_call_target="tpu_custom_call" | custom-call | flops 1073741824 | bytes 4723840 | tf_op jit(solution)/shard_map/pallas_call | solution.py:332
  24.3 0.1 collective-permute-start.6
  24.4 2.4 %shard_map.63 = (s16[1040,128]{1,0:T(8,128)(2,1)S(1)}, s16[1040,128]{1,0:T(8,128)(2,1)S(1)}) custom-call(s32[288]{0:T(512)S(1)} %get-tuple-element.29.plan_ref, bf16[512,2048]{1,0:T(8,128)(2,1)S(1)} %get-tuple-element.26.operand, bf16[16,1,128,128]{3,2,1,0:T(8,128)(2,1)S(1)} %get-tuple-element.30.refs_0_, ...), custom_call_target="tpu_custom_call" | custom-call | flops 1073741824 | bytes 4727936 | tf_op jit(solution)/shard_map/pallas_call | solution.py:332
  26.8 2.9 %collective-permute-start.4 = (s16[1040,128]{1,0:T(8,128)(2,1)S(1)}, s16[1040,128]{1,0:T(8,128)(2,1)S(1)}, u32[]{:S(2)}, u32[]{:S(2)}) collective-permute-start(s16[1040,128]{1,0:T(8,128)(2,1)S(1)} %get-tuple-element.33), channel_id=1, source_target_pairs={{0,1},{1,0},{2,3},{3,2},{4,5},{5,4},{6,7},{7,6},{8,9},{9,8},{10,11... | collective-permute-start | bytes 798728 | tf_op jit(solution)/shard_map/ppermute | solution.py:425
  29.7 0.1 collective-permute-start.5
  29.8 4.9 %collective-permute-done.3.refs_3_ = s16[2064,128]{1,0:T(8,128)(2,1)S(1)} collective-permute-done((s16[2064,128]{1,0:T(8,128)(2,1)S(1)}, s16[2064,128]{1,0:T(8,128)(2,1)S(1)}, u32[]{:S(2)}, u32[]{:S(2)}) %collective-permute-start.3) | collective-permute-done | bytes 528416 | tf_op jit(solution)/shard_map/ppermute | solution.py:412
  34.7 4.0 %shard_map.62 = (f32[512,512]{1,0:T(8,128)S(1)}, f32[512,512]{1,0:T(8,128)S(1)}, s32[16,128]{1,0:T(8,128)S(1)}, s32[16,128]{1,0:T(8,128)S(1)}) custom-call(s32[288]{0:T(512)S(1)} %get-tuple-element.29.plan_ref, bf16[512,2048]{1,0:T(8,128)(2,1)S(1)} %get-tuple-element.26.operand, bf16[16,1,128,128]{3,2,1,0:T(8,128)(2,1)S(1)} %get-tuple-element.30.refs_0_, ...), custom_call_target="tpu_custom_call" | custom-call | flops 2147483648 | bytes 6308992 | tf_op jit(solution)/shard_map/pallas_call | solution.py:332
  38.7 1.7 %collective-permute-done.4.refs_0_.came = s16[1040,128]{1,0:T(8,128)(2,1)S(1)} collective-permute-done((s16[1040,128]{1,0:T(8,128)(2,1)S(1)}, s16[1040,128]{1,0:T(8,128)(2,1)S(1)}, u32[]{:S(2)}, u32[]{:S(2)}) %collective-permute-start.4) | collective-permute-done | bytes 266272 | tf_op jit(solution)/shard_map/ppermute | solution.py:425
  40.4 0.2 shard_map.68
  40.6 2.2 %collective-permute-start.11 = (s16[1040,128]{1,0:T(8,128)(2,1)S(1)}, s16[1040,128]{1,0:T(8,128)(2,1)S(1)}, u32[]{:S(2)}, u32[]{:S(2)}) collective-permute-start(s16[1040,128]{1,0:T(8,128)(2,1)S(1)} %shard_map.68), channel_id=1, source_target_pairs={{0,1},{1,3},{3,2},{2,0},{4,5},{5,7},{7,6},{6,4},{8,9},{9,11},{11,1... | collective-permute-start | bytes 798728 | tf_op jit(solution)/shard_map/ppermute | solution.py:450
  42.8 2.9 %collective-permute-done.5.refs_1_.came = s16[1040,128]{1,0:T(8,128)(2,1)S(1)} collective-permute-done((s16[1040,128]{1,0:T(8,128)(2,1)S(1)}, s16[1040,128]{1,0:T(8,128)(2,1)S(1)}, u32[]{:S(2)}, u32[]{:S(2)}) %collective-permute-start.5) | collective-permute-done | bytes 266272 | tf_op jit(solution)/shard_map/ppermute | solution.py:425
  45.7 0.0 collective-permute-done.6.refs_2_
  45.7 0.2 shard_map.66
  45.9 2.6 %collective-permute-start.7 = (s16[1040,128]{1,0:T(8,128)(2,1)S(1)}, s16[1040,128]{1,0:T(8,128)(2,1)S(1)}, u32[]{:S(2)}, u32[]{:S(2)}) collective-permute-start(s16[1040,128]{1,0:T(8,128)(2,1)S(1)} %shard_map.66), channel_id=1, source_target_pairs={{0,1},{1,3},{3,2},{2,0},{4,5},{5,7},{7,6},{6,4},{8,9},{9,11},{11,1... | collective-permute-start | bytes 798728 | tf_op jit(solution)/shard_map/ppermute | solution.py:450
  48.5 0.2 shard_map.65
  48.7 4.4 %collective-permute-done.11.came = s16[1040,128]{1,0:T(8,128)(2,1)S(1)} collective-permute-done((s16[1040,128]{1,0:T(8,128)(2,1)S(1)}, s16[1040,128]{1,0:T(8,128)(2,1)S(1)}, u32[]{:S(2)}, u32[]{:S(2)}) %collective-permute-start.11) | collective-permute-done | bytes 266272 | tf_op jit(solution)/shard_map/ppermute | solution.py:450
  53.1 0.1 shard_map.69
  53.2 0.1 collective-permute-start.14
  53.3 1.6 %collective-permute-start.13 = (f32[8,256]{1,0:T(8,128)S(1)}, f32[8,256]{1,0:T(8,128)S(1)}, u32[]{:S(2)}, u32[]{:S(2)}) collective-permute-start(f32[8,256]{1,0:T(8,128)S(1)} %get-tuple-element.44.refs_0_), channel_id=1, source_target_pairs={{0,8},{4,12},{8,0},{12,4},{1,9},{5,13},{9,1},{13,5},{2,10},{6,14},... | collective-permute-start | bytes 24584 | tf_op jit(solution)/shard_map/ppermute | solution.py:469
  54.9 0.3 collective-permute-start.12
  55.2 3.6 %collective-permute-done.7.came = s16[1040,128]{1,0:T(8,128)(2,1)S(1)} collective-permute-done((s16[1040,128]{1,0:T(8,128)(2,1)S(1)}, s16[1040,128]{1,0:T(8,128)(2,1)S(1)}, u32[]{:S(2)}, u32[]{:S(2)}) %collective-permute-start.7) | collective-permute-done | bytes 266272 | tf_op jit(solution)/shard_map/ppermute | solution.py:450
  58.7 0.1 shard_map.67
  58.8 0.1 collective-permute-start.10
  58.9 1.6 %collective-permute-start.9 = (f32[8,256]{1,0:T(8,128)S(1)}, f32[8,256]{1,0:T(8,128)S(1)}, u32[]{:S(2)}, u32[]{:S(2)}) collective-permute-start(f32[8,256]{1,0:T(8,128)S(1)} %get-tuple-element.42.refs_0_), channel_id=1, source_target_pairs={{0,8},{4,12},{8,0},{12,4},{1,9},{5,13},{9,1},{13,5},{2,10},{6,14},... | collective-permute-start | bytes 24584 | tf_op jit(solution)/shard_map/ppermute | solution.py:469
  60.5 0.0 collective-permute-done.14.refs_3_
  60.5 0.3 collective-permute-start.8
  60.8 0.7 %shard_map.72 = s32[4]{0:T(128)} custom-call(s32[16,128]{1,0:T(8,128)S(1)} %get-tuple-element.45.own_load, s16[1040,128]{1,0:T(8,128)(2,1)S(1)} %collective-permute-done.11.came), custom_call_target="tpu_custom_call" | custom-call | bytes 274448 | tf_op jit(solution)/shard_map/pallas_call | solution.py:332
  61.5 0.0 collective-permute-done.13.refs_2_
  61.5 0.0 collective-permute-done.12.refs_1_
  61.5 0.8 %shard_map.70.refs_4_ = f32[512,512]{1,0:T(8,128)} custom-call(f32[512,256]{1,0:T(8,128)S(1)} %get-tuple-element.43.inflated, f32[8,256]{1,0:T(8,128)S(1)} %get-tuple-element.44.refs_0_, f32[8,256]{1,0:T(8,128)S(1)} %collective-permute-done.12.refs_1_, f32[8,256]{1,0:T(8,128)S(1)} %collective-permute-done.13.refs_2_, ...), custom_call_target="tpu_custom_call" | custom-call | bytes 1605632 | tf_op jit(solution)/shard_map/pallas_call | solution.py:332
  62.4 0.0 collective-permute-done.10.refs_3_
  62.4 0.2 collective-permute-done.9.refs_2_
  62.6 1.0 %collective-permute-done.8.refs_1_ = f32[8,256]{1,0:T(8,128)S(1)} collective-permute-done((f32[8,256]{1,0:T(8,128)S(1)}, f32[8,256]{1,0:T(8,128)S(1)}, u32[]{:S(2)}, u32[]{:S(2)}) %collective-permute-start.8) | collective-permute-done | bytes 8224 | tf_op jit(solution)/shard_map/ppermute | solution.py:469
  63.6 0.8 %shard_map.71 = f32[512,512]{1,0:T(8,128)} custom-call(f32[512,256]{1,0:T(8,128)S(1)} %get-tuple-element.41.inflated, f32[8,256]{1,0:T(8,128)S(1)} %get-tuple-element.42.refs_0_, f32[8,256]{1,0:T(8,128)S(1)} %collective-permute-done.8.refs_1_, f32[8,256]{1,0:T(8,128)S(1)} %collective-permute-done.9.refs_2_, ...), custom_call_target="tpu_custom_call", output_to_operand_aliasing={{}: (5, {})} | custom-call | bytes 2654208 | tf_op jit(solution)/shard_map/pallas_call | solution.py:332
Async XLA Ops:
  0.6 3.1 %collective-permute-start.1 = (bf16[16,1,128,128]{3,2,1,0:T(8,128)(2,1)}, bf16[16,1,128,128]{3,2,1,0:T(8,128)(2,1)S(1)}, u32[]{:S(2)}, u32[]{:S(2)}) collective-permute-start(bf16[16,1,128,128]{3,2,1,0:T(8,128)(2,1)} %own.1), channel_id=1, source_target_pairs={{0,4},{4,0},{8,12},{12,8},{1,5},{5,1},{9,13},{13,9},{2,6},{6,2},{1... | collective-permute-start | bytes 1572872 | tf_op jit(solution)/shard_map/ppermute | solution.py:373
  1.1 15.3 %collective-permute-start = (bf16[16,1,128,128]{3,2,1,0:T(8,128)(2,1)}, bf16[16,1,128,128]{3,2,1,0:T(8,128)(2,1)S(1)}, u32[]{:S(2)}, u32[]{:S(2)}) collective-permute-start(bf16[16,1,128,128]{3,2,1,0:T(8,128)(2,1)} %own.1), channel_id=1, source_target_pairs={{0,8},{4,12},{8,0},{12,4},{1,9},{5,13},{9,1},{13,5},{2,10},{6,14},... | collective-permute-start | bytes 1572872 | tf_op jit(solution)/shard_map/ppermute | solution.py:372
  3.7 1.6 %copy-start = (bf16[512,2048]{1,0:T(8,128)(2,1)S(1)}, bf16[512,2048]{1,0:T(8,128)(2,1)}, u32[]{:S(2)}) copy-start(bf16[512,2048]{1,0:T(8,128)(2,1)} %operand.1) | copy-start | bytes 6291460
  5.3 1.0 %copy-start.1 = (bf16[16,1,128,128]{3,2,1,0:T(8,128)(2,1)S(1)}, bf16[16,1,128,128]{3,2,1,0:T(8,128)(2,1)}, u32[]{:S(2)}) copy-start(bf16[16,1,128,128]{3,2,1,0:T(8,128)(2,1)} %own.1) | copy-start | bytes 1572868
  6.4 0.7 %copy-start.2 = (s32[16,4]{0,1:T(4,128)S(1)}, s32[16,4]{0,1:T(4,128)}, u32[]{:S(2)}) copy-start(s32[16,4]{0,1:T(4,128)} %param.6) | copy-start | bytes 772
  7.1 0.7 %copy-start.3 = (s32[16]{0:T(128)S(1)}, s32[16]{0:T(128)}, u32[]{:S(2)}) copy-start(s32[16]{0:T(128)} %counts.1) | copy-start | bytes 196
  16.5 1.9 %collective-permute-start.2 = (bf16[16,1,128,128]{3,2,1,0:T(8,128)(2,1)S(1)}, bf16[16,1,128,128]{3,2,1,0:T(8,128)(2,1)S(1)}, u32[]{:S(2)}, u32[]{:S(2)}) collective-permute-start(bf16[16,1,128,128]{3,2,1,0:T(8,128)(2,1)S(1)} %collective-permute-done.held.refs_2_), channel_id=1, source_target_pairs={{0,4},{4,0},{8,12},{12,8},{1,5},{5,1},{9,13},{13,9},{2,6},{6,2},{1... | collective-permute-start | bytes 1572872 | tf_op jit(solution)/shard_map/ppermute | solution.py:391
  19.8 14.9 %collective-permute-start.3 = (s16[2064,128]{1,0:T(8,128)(2,1)S(1)}, s16[2064,128]{1,0:T(8,128)(2,1)S(1)}, u32[]{:S(2)}, u32[]{:S(2)}) collective-permute-start(s16[2064,128]{1,0:T(8,128)(2,1)S(1)} %shard_map.61), channel_id=1, source_target_pairs={{0,2},{1,0},{2,3},{3,1},{4,6},{5,4},{6,7},{7,5},{8,10},{9,8},{10,1... | collective-permute-start | bytes 1585160 | tf_op jit(solution)/shard_map/ppermute | solution.py:412
  24.3 21.4 %collective-permute-start.6 = (s16[2064,128]{1,0:T(8,128)(2,1)S(1)}, s16[2064,128]{1,0:T(8,128)(2,1)S(1)}, u32[]{:S(2)}, u32[]{:S(2)}) collective-permute-start(s16[2064,128]{1,0:T(8,128)(2,1)S(1)} %shard_map.64), channel_id=1, source_target_pairs={{0,4},{1,2},{2,1},{3,7},{4,0},{5,6},{6,5},{7,3},{8,12},{9,10},{10,... | collective-permute-start | bytes 1585160 | tf_op jit(solution)/shard_map/ppermute | solution.py:429
  26.8 13.6 %collective-permute-start.4 = (s16[1040,128]{1,0:T(8,128)(2,1)S(1)}, s16[1040,128]{1,0:T(8,128)(2,1)S(1)}, u32[]{:S(2)}, u32[]{:S(2)}) collective-permute-start(s16[1040,128]{1,0:T(8,128)(2,1)S(1)} %get-tuple-element.33), channel_id=1, source_target_pairs={{0,1},{1,0},{2,3},{3,2},{4,5},{5,4},{6,7},{7,6},{8,9},{9,8},{10,11... | collective-permute-start | bytes 798728 | tf_op jit(solution)/shard_map/ppermute | solution.py:425
  29.7 16.0 %collective-permute-start.5 = (s16[1040,128]{1,0:T(8,128)(2,1)S(1)}, s16[1040,128]{1,0:T(8,128)(2,1)S(1)}, u32[]{:S(2)}, u32[]{:S(2)}) collective-permute-start(s16[1040,128]{1,0:T(8,128)(2,1)S(1)} %get-tuple-element.34), channel_id=1, source_target_pairs={{0,1},{1,0},{2,3},{3,2},{4,5},{5,4},{6,7},{7,6},{8,9},{9,8},{10,11... | collective-permute-start | bytes 798728 | tf_op jit(solution)/shard_map/ppermute | solution.py:425
  40.6 12.5 %collective-permute-start.11 = (s16[1040,128]{1,0:T(8,128)(2,1)S(1)}, s16[1040,128]{1,0:T(8,128)(2,1)S(1)}, u32[]{:S(2)}, u32[]{:S(2)}) collective-permute-start(s16[1040,128]{1,0:T(8,128)(2,1)S(1)} %shard_map.68), channel_id=1, source_target_pairs={{0,1},{1,3},{3,2},{2,0},{4,5},{5,7},{7,6},{6,4},{8,9},{9,11},{11,1... | collective-permute-start | bytes 798728 | tf_op jit(solution)/shard_map/ppermute | solution.py:450
  45.9 12.8 %collective-permute-start.7 = (s16[1040,128]{1,0:T(8,128)(2,1)S(1)}, s16[1040,128]{1,0:T(8,128)(2,1)S(1)}, u32[]{:S(2)}, u32[]{:S(2)}) collective-permute-start(s16[1040,128]{1,0:T(8,128)(2,1)S(1)} %shard_map.66), channel_id=1, source_target_pairs={{0,1},{1,3},{3,2},{2,0},{4,5},{5,7},{7,6},{6,4},{8,9},{9,11},{11,1... | collective-permute-start | bytes 798728 | tf_op jit(solution)/shard_map/ppermute | solution.py:450
  53.2 7.3 %collective-permute-start.14 = (f32[8,256]{1,0:T(8,128)S(1)}, f32[8,256]{1,0:T(8,128)S(1)}, u32[]{:S(2)}, u32[]{:S(2)}) collective-permute-start(f32[8,256]{1,0:T(8,128)S(1)} %get-tuple-element.44.refs_0_), channel_id=1, source_target_pairs={{0,4},{4,0},{8,12},{12,8},{1,5},{5,1},{9,13},{13,9},{2,6},{6,2},{1... | collective-permute-start | bytes 24584 | tf_op jit(solution)/shard_map/ppermute | solution.py:469
  53.3 8.2 %collective-permute-start.13 = (f32[8,256]{1,0:T(8,128)S(1)}, f32[8,256]{1,0:T(8,128)S(1)}, u32[]{:S(2)}, u32[]{:S(2)}) collective-permute-start(f32[8,256]{1,0:T(8,128)S(1)} %get-tuple-element.44.refs_0_), channel_id=1, source_target_pairs={{0,8},{4,12},{8,0},{12,4},{1,9},{5,13},{9,1},{13,5},{2,10},{6,14},... | collective-permute-start | bytes 24584 | tf_op jit(solution)/shard_map/ppermute | solution.py:469
  54.9 6.7 %collective-permute-start.12 = (f32[8,256]{1,0:T(8,128)S(1)}, f32[8,256]{1,0:T(8,128)S(1)}, u32[]{:S(2)}, u32[]{:S(2)}) collective-permute-start(f32[8,256]{1,0:T(8,128)S(1)} %get-tuple-element.44.refs_0_), channel_id=1, source_target_pairs={{0,12},{4,8},{8,4},{12,0},{1,13},{5,9},{9,5},{13,1},{2,14},{6,10},... | collective-permute-start | bytes 24584 | tf_op jit(solution)/shard_map/ppermute | solution.py:469
  58.8 3.5 %collective-permute-start.10 = (f32[8,256]{1,0:T(8,128)S(1)}, f32[8,256]{1,0:T(8,128)S(1)}, u32[]{:S(2)}, u32[]{:S(2)}) collective-permute-start(f32[8,256]{1,0:T(8,128)S(1)} %get-tuple-element.42.refs_0_), channel_id=1, source_target_pairs={{0,4},{4,0},{8,12},{12,8},{1,5},{5,1},{9,13},{13,9},{2,6},{6,2},{1... | collective-permute-start | bytes 24584 | tf_op jit(solution)/shard_map/ppermute | solution.py:469
  58.9 3.7 %collective-permute-start.9 = (f32[8,256]{1,0:T(8,128)S(1)}, f32[8,256]{1,0:T(8,128)S(1)}, u32[]{:S(2)}, u32[]{:S(2)}) collective-permute-start(f32[8,256]{1,0:T(8,128)S(1)} %get-tuple-element.42.refs_0_), channel_id=1, source_target_pairs={{0,8},{4,12},{8,0},{12,4},{1,9},{5,13},{9,1},{13,5},{2,10},{6,14},... | collective-permute-start | bytes 24584 | tf_op jit(solution)/shard_map/ppermute | solution.py:469
  60.5 3.1 %collective-permute-start.8 = (f32[8,256]{1,0:T(8,128)S(1)}, f32[8,256]{1,0:T(8,128)S(1)}, u32[]{:S(2)}, u32[]{:S(2)}) collective-permute-start(f32[8,256]{1,0:T(8,128)S(1)} %get-tuple-element.42.refs_0_), channel_id=1, source_target_pairs={{0,12},{4,8},{8,4},{12,0},{1,13},{5,9},{9,5},{13,1},{2,14},{6,10},... | collective-permute-start | bytes 24584 | tf_op jit(solution)/shard_map/ppermute | solution.py:469
